TPU v7x, 128 devices: a whole 4x4x4 slice. The times are simulated.
128 devices in a mesh: row: 8 (over x, core), col: 16 (over y, z).
Axes of the slice: x: 4, y: 4, z: 4, core: 2. Of those that a mesh axis runs over, the one named last changes fastest.
Arguments:
- p_valence: bfloat16 [4096, 4096], P('row', 'col'), as said below
- p_conduction: bfloat16 [4096, 4096], P('row', 'col'), as said below
- trial_vectors: bfloat16 [2, 4096, 4096], P(None, 'row', 'col'), may hold values from -6 to 6
- mask_valence: int32 [32, 32], replicated, may hold values from 0 to 1, as said below
- mask_conduction: int32 [32, 32], replicated, may hold values from 0 to 1, as said below
- mask_trial: int32 [32, 32], replicated, may hold values 0 or 1
- orbitals: bfloat16 [32, 128, 8192], P('row'), may hold values from -0.29882812 to 0.29882812
- sphere_starts: int32 [32], replicated, may hold values from 0 to 112, as said below
Outputs:
- kernel: bfloat16 [2, 4096, 4096], P(None, 'row', 'col')
- density: float32 [2, 65536], P(None, ('row', 'col'))
Inputs may be any that keep to these rules, and one draw needn't show every extreme that they name: `mask_valence`: symmetric, ones on the block diagonal and next to it. `mask_conduction`: symmetric, ones on the block diagonal and next to it. `p_valence`: symmetric. `p_conduction`: symmetric. `sphere_starts`: the first block's start is 0 and the last block's 128 - 16.
All inputs are finite; a program needn't handle non-finite values.
Results may differ from a plain program's by a relative error of at most 0.0049.
Values may be sent and summed in bfloat16 or wider, within the bound.
No kernel may reach another device: no remote copies, remote signals or barrier semaphores. Data moves between devices by JAX's collectives and lax.ppermute only.
A program may use at most 192 MiB of HBM per device.

v0:
```python
import jax
import jax.numpy as jnp
from jax import lax
from jax.sharding import PartitionSpec as P

BS = 128
SPAN = 16
SP = 512


def broadcast(x, axis, root):
    mine = lax.axis_index(axis) == root
    return lax.psum(jnp.where(mine, x, jnp.zeros_like(x)), axis)


def masked(values, block_mask, row_index, col_index):
    leading_dims = values.shape[:-2]
    row_blocks = values.shape[-2] // BS
    col_blocks = values.shape[-1] // BS
    tile_mask = lax.dynamic_slice(
        block_mask, (row_index * row_blocks, col_index * col_blocks), (row_blocks, col_blocks)
    ).astype(values.dtype)
    shaped = values.reshape(leading_dims + (row_blocks, BS, col_blocks, BS))
    return (shaped * tile_mask[:, None, :, None]).reshape(values.shape)


def local(
    p_valence,
    p_conduction,
    trial_vectors,
    mask_valence,
    mask_conduction,
    mask_trial,
    orbitals,
    sphere_starts,
):
    row_index = lax.axis_index("row")
    col_index = lax.axis_index("col")
    valence = masked(p_valence, mask_valence, row_index, col_index)
    conduction = masked(p_conduction, mask_conduction, row_index, col_index)
    trials = masked(trial_vectors, mask_trial, row_index, col_index)
    vector_count = trials.shape[0]
    local_rows = trials.shape[1]
    local_cols = trials.shape[2]
    panels = lax.all_gather(trials, "col", axis=2, tiled=True)
    response = jnp.einsum(
        "vik,kj->vij",
        panels,
        lax.all_gather(conduction, "row", axis=0, tiled=True),
        preferred_element_type=jnp.float32,
    )
    response_half = response.astype(jnp.bfloat16)
    gathered = lax.all_gather(response_half, "row", axis=1, tiled=True)
    kernel_sum = jnp.einsum(
        "ik,vkj->vij",
        lax.all_gather(valence, "col", axis=1, tiled=True),
        gathered,
        preferred_element_type=jnp.float32,
    )
    kernel = masked(kernel_sum, mask_trial, row_index, col_index).astype(jnp.bfloat16)
    row_blocks = local_rows // BS
    col_blocks = local_cols // BS
    ratio = lax.axis_size("col") // lax.axis_size("row")
    own_part = lax.dynamic_slice_in_dim(orbitals, col_index % ratio * col_blocks, col_blocks, 0)
    partner = broadcast(own_part, "row", col_index // ratio)
    partner_padded = jnp.pad(
        partner.reshape(col_blocks, BS, SPAN, SP), ((0, 0), (0, 0), (SPAN, SPAN), (0, 0))
    )
    starts_rows = lax.dynamic_slice_in_dim(sphere_starts, row_index * row_blocks, row_blocks, 0)
    starts_cols = lax.dynamic_slice_in_dim(sphere_starts, col_index * col_blocks, col_blocks, 0)
    offsets = jnp.clip(starts_rows[:, None] - starts_cols[None, :] + SPAN, 0, 2 * SPAN)

    def take_frame(orbital_block, offset):
        return lax.dynamic_slice_in_dim(orbital_block, offset, SPAN, 1)

    def frames_for_row(offset_row):
        return jax.vmap(take_frame)(partner_padded, offset_row)

    frames = jax.vmap(frames_for_row)(offsets).reshape(row_blocks, col_blocks, BS, SPAN * SP)
    kernel_blocks = kernel.reshape(vector_count, row_blocks, BS, col_blocks, BS).transpose(
        0, 1, 3, 2, 4
    )
    applied = jnp.einsum(
        "vabmn,abnp->vamp", kernel_blocks, frames, preferred_element_type=jnp.float32
    )
    contrib = jnp.sum(orbitals[None] * applied, axis=2)
    slab_count = lax.axis_size("row") * lax.axis_size("col")
    density_grid = jnp.zeros((vector_count, slab_count, SP), jnp.float32)
    zero_index = jnp.zeros((), jnp.int32)
    for local_block in range(row_blocks):
        begin_slab = starts_rows[local_block]
        current = lax.dynamic_slice(
            density_grid, (zero_index, begin_slab, zero_index), (vector_count, SPAN, SP)
        )
        update = current + contrib[:, local_block].reshape(vector_count, SPAN, SP)
        density_grid = lax.dynamic_update_slice(
            density_grid, update, (zero_index, begin_slab, zero_index)
        )
    own_slab = lax.psum_scatter(density_grid, ("row", "col"), scatter_dimension=1, tiled=True)
    density = own_slab.reshape(vector_count, SP)
    return (kernel, density)


def solution(mesh):
    placed = (
        P("row", "col"),
        P("row", "col"),
        P(None, "row", "col"),
        P(),
        P(),
        P(),
        P("row", None, None),
        P(),
    )
    return jax.shard_map(
        local,
        mesh=mesh,
        in_specs=placed,
        out_specs=(P(None, "row", "col"), P(None, ("row", "col"))),
        check_vma=False,
    )
```

profile of v0, /device:TPU:1, one launch (start us, length us, event | category | flops | bytes accessed | tf_op | source)
XLA Modules:
  0.0 464.5 jit_solution(12920767297528534804)
XLA Ops:
  8.2 1.7 bitcast_multiply_fusion.2
  11.0 1.9 broadcast_multiply_fusion
  13.0 2.5 dynamic-slice_select_fusion
  15.5 3.9 copy.34
  20.5 18.4 %all-gather.7.cloned.1.call-done = bf16[4096,256]{1,0:T(8,128)(2,1)} async-done(((bf16[512,256]{1,0:T(8,128)(2,1)}), bf16[4096,256]{1,0:T(8,128)(2,1)}) %all-gather.7.cloned.1.call-update) | async-done | bytes 2097168 | tf_op jit(solution)/shard_map/all_gather | solution.py:49
  38.9 80.3 %all-gather.5.cloned.1.call-done = bf16[2,512,4096]{2,1,0:T(8,128)(2,1)} async-done(((bf16[2,512,256]{2,1,0:T(8,128)(2,1)}), bf16[2,512,4096]{2,1,0:T(8,128)(2,1)}) %all-gather.5.cloned.1.call-update) | async-done | bytes 8388624 | tf_op jit(solution)/shard_map/all_gather | solution.py:45
  119.2 7.1 %fusion.15 = bf16[2,512,256]{2,1,0:T(8,128)(2,1)} fusion(bf16[2,512,4096]{2,1,0:T(8,128)(2,1)} %all-gather.5.cloned.1.call-done, bf16[4096,256]{1,0:T(8,128)(2,1)} %all-gather.7.cloned.1.call-done), kind=kOutput, calls=%fused_computation.13 | convolution fusion | flops 2147745792 | bytes 11010048 | tf_op jit(solution)/shard_map/vik,kj->vij/dot_general | solution.py:46
  126.7 11.5 %convert_element_type.30 = f32[4,128,8192]{2,1,0:T(8,128)} convert(bf16[4,128,8192]{2,1,0:T(8,128)(2,1)} %param.14) | non-fusion elementwise | flops 4194304 | bytes 25165824 | tf_op jit(solution)/shard_map/convert_element_type | solution.py:86
  146.9 45.6 %all-reduce.5.cloned.1.call-done = bf16[2,128,16,512]{3,2,1,0:T(8,128)(2,1)} async-done(((bf16[2,128,16,512]{3,2,1,0:T(8,128)(2,1)}), bf16[2,128,16,512]{3,2,1,0:T(8,128)(2,1)}) %all-reduce.5.cloned.1.call-update) | async-done | bytes 4194320 | tf_op jit(solution)/shard_map/psum | solution.py:13
  192.5 7.7 %pad.4 = bf16[2,128,48,512]{3,2,1,0:T(8,128)(2,1)} pad(bf16[2,128,16,512]{3,2,1,0:T(8,128)(2,1)} %all-reduce.5.cloned.1.call-done, bf16[]{:T(256)} %constant.48.clone.1), padding=0_0x0_0x16_16x0_0 | pad | bytes 16777218 | tf_op jit(solution)/shard_map/jit(_pad)/pad | solution.py:66
  200.3 48.1 %while.1 = (s32[]{:T(128)}, bf16[2,128,48,512]{3,2,1,0:T(8,128)(2,1)}, s32[8,4]{1,0:T(8,128)S(1)}, bf16[8,128,16,512]{3,2,1,0:T(8,128)(2,1)}, s32[]{:T(128)}) while((s32[]{:T(128)}, bf16[2,128,48,512]{3,2,1,0:T(8,128)(2,1)}, s32[8,4]{1,0:T(8,128)S(1)}, bf16[8,128,16,512]{3,2,1,0:T(8,128)(2,1)}, s32[]{:T(128)}) %tuple.52), condition=%wide.while_cond, body=%wide.while_body.sunk | while | flops 2 | bytes 4195953 | solution.py:74
  200.9 5.3 %dynamic-slice_dynamic-update-slice_fusion.2 = bf16[8,128,16,512]{3,2,1,0:T(8,128)(2,1)} fusion(bf16[8,128,16,512]{3,2,1,0:T(8,128)(2,1)} %get-tuple-element.87, s32[]{:T(128)} %get-tuple-element.84, bf16[2,128,48,512]{3,2,1,0:T(8,128)(2,1)} %get-tuple-element.90, s32[]{:T(128)} %bitcast.99, s32[]{:T(128)} %bitcast.100), kind=kLoop, calls=%fused_computation.clone.1 | loop fusion | bytes 4195840 | tf_op jit(solution)/shard_map/vmap(vmap())/gather
  206.8 5.6 %dynamic-slice_dynamic-update-slice_fusion.2 = bf16[8,128,16,512]{3,2,1,0:T(8,128)(2,1)} fusion(bf16[8,128,16,512]{3,2,1,0:T(8,128)(2,1)} %get-tuple-element.87, s32[]{:T(128)} %get-tuple-element.84, bf16[2,128,48,512]{3,2,1,0:T(8,128)(2,1)} %get-tuple-element.90, s32[]{:T(128)} %bitcast.99, s32[]{:T(128)} %bitcast.100), kind=kLoop, calls=%fused_computation.clone.1 | loop fusion | bytes 4195840 | tf_op jit(solution)/shard_map/vmap(vmap())/gather
  213.0 5.3 %dynamic-slice_dynamic-update-slice_fusion.2 = bf16[8,128,16,512]{3,2,1,0:T(8,128)(2,1)} fusion(bf16[8,128,16,512]{3,2,1,0:T(8,128)(2,1)} %get-tuple-element.87, s32[]{:T(128)} %get-tuple-element.84, bf16[2,128,48,512]{3,2,1,0:T(8,128)(2,1)} %get-tuple-element.90, s32[]{:T(128)} %bitcast.99, s32[]{:T(128)} %bitcast.100), kind=kLoop, calls=%fused_computation.clone.1 | loop fusion | bytes 4195840 | tf_op jit(solution)/shard_map/vmap(vmap())/gather
  218.9 5.6 %dynamic-slice_dynamic-update-slice_fusion.2 = bf16[8,128,16,512]{3,2,1,0:T(8,128)(2,1)} fusion(bf16[8,128,16,512]{3,2,1,0:T(8,128)(2,1)} %get-tuple-element.87, s32[]{:T(128)} %get-tuple-element.84, bf16[2,128,48,512]{3,2,1,0:T(8,128)(2,1)} %get-tuple-element.90, s32[]{:T(128)} %bitcast.99, s32[]{:T(128)} %bitcast.100), kind=kLoop, calls=%fused_computation.clone.1 | loop fusion | bytes 4195840 | tf_op jit(solution)/shard_map/vmap(vmap())/gather
  225.1 5.4 %dynamic-slice_dynamic-update-slice_fusion.2 = bf16[8,128,16,512]{3,2,1,0:T(8,128)(2,1)} fusion(bf16[8,128,16,512]{3,2,1,0:T(8,128)(2,1)} %get-tuple-element.87, s32[]{:T(128)} %get-tuple-element.84, bf16[2,128,48,512]{3,2,1,0:T(8,128)(2,1)} %get-tuple-element.90, s32[]{:T(128)} %bitcast.99, s32[]{:T(128)} %bitcast.100), kind=kLoop, calls=%fused_computation.clone.1 | loop fusion | bytes 4195840 | tf_op jit(solution)/shard_map/vmap(vmap())/gather
  231.1 5.3 %dynamic-slice_dynamic-update-slice_fusion.2 = bf16[8,128,16,512]{3,2,1,0:T(8,128)(2,1)} fusion(bf16[8,128,16,512]{3,2,1,0:T(8,128)(2,1)} %get-tuple-element.87, s32[]{:T(128)} %get-tuple-element.84, bf16[2,128,48,512]{3,2,1,0:T(8,128)(2,1)} %get-tuple-element.90, s32[]{:T(128)} %bitcast.99, s32[]{:T(128)} %bitcast.100), kind=kLoop, calls=%fused_computation.clone.1 | loop fusion | bytes 4195840 | tf_op jit(solution)/shard_map/vmap(vmap())/gather
  237.0 5.4 %dynamic-slice_dynamic-update-slice_fusion.2 = bf16[8,128,16,512]{3,2,1,0:T(8,128)(2,1)} fusion(bf16[8,128,16,512]{3,2,1,0:T(8,128)(2,1)} %get-tuple-element.87, s32[]{:T(128)} %get-tuple-element.84, bf16[2,128,48,512]{3,2,1,0:T(8,128)(2,1)} %get-tuple-element.90, s32[]{:T(128)} %bitcast.99, s32[]{:T(128)} %bitcast.100), kind=kLoop, calls=%fused_computation.clone.1 | loop fusion | bytes 4195840 | tf_op jit(solution)/shard_map/vmap(vmap())/gather
  243.0 5.3 %dynamic-slice_dynamic-update-slice_fusion.2 = bf16[8,128,16,512]{3,2,1,0:T(8,128)(2,1)} fusion(bf16[8,128,16,512]{3,2,1,0:T(8,128)(2,1)} %get-tuple-element.87, s32[]{:T(128)} %get-tuple-element.84, bf16[2,128,48,512]{3,2,1,0:T(8,128)(2,1)} %get-tuple-element.90, s32[]{:T(128)} %bitcast.99, s32[]{:T(128)} %bitcast.100), kind=kLoop, calls=%fused_computation.clone.1 | loop fusion | bytes 4195840 | tf_op jit(solution)/shard_map/vmap(vmap())/gather
  248.3 25.8 %reshape.126 = bf16[4,2,128,8192,1]{3,2,1,0,4:T(8,128)(2,1)} reshape(bf16[8,128,16,512]{3,2,1,0:T(8,128)(2,1)} %get-tuple-element.9) | data formatting | bytes 33554432 | tf_op jit(solution)/shard_map/reshape | solution.py:79
  274.1 13.8 %all-gather.9.cloned.1.call-done = bf16[2,4096,256]{2,1,0:T(8,128)(2,1)} async-done(((bf16[2,512,256]{2,1,0:T(8,128)(2,1)}), bf16[2,4096,256]{2,1,0:T(8,128)(2,1)}) %all-gather.9.cloned.1.call-update) | async-done | bytes 4194320 | tf_op jit(solution)/shard_map/all_gather | solution.py:53
  287.9 5.8 %fusion.12 = bf16[2,512,256]{1,2,0:T(8,128)(2,1)S(1)} fusion(bf16[2,4096,256]{2,1,0:T(8,128)(2,1)} %all-gather.9.cloned.1.call-done, bf16[512,4096]{1,0:T(8,128)(2,1)} %all-gather.11.cloned.1.call-done, f32[512,256]{0,1:T(8,128)S(1)} %bitcast.108), kind=kOutput, calls=%fused_computation.12 | convolution fusion | flops 2148007936 | bytes 9437184 | tf_op jit(solution)/shard_map/ik,vkj->vij/dot_general | solution.py:54
  294.3 14.2 %fusion = f32[2,4,8192]{2,0,1:T(2,128)S(1)} fusion(bf16[4,2,128,8192,1]{3,2,1,0,4:T(8,128)(2,1)} %reshape.126, f32[4,128,8192]{2,1,0:T(8,128)} %convert_element_type.30, bf16[2,4,128,2,128]{4,2,3,0,1:T(8,128)(2,1)S(1)} %copy.21), kind=kOutput, calls=%fused_computation.3 | convolution fusion | flops 4311678976 | bytes 34340864 | tf_op jit(solution)/shard_map/vabmn,abnp->vamp/dot_general | solution.py:83
  312.4 144.0 %all-reduce.7.cloned.1.call-done = f32[2,128,512]{2,0,1:T(2,128)} async-done(((f32[2,128,512]{2,0,1:T(2,128)}), f32[2,128,512]{2,0,1:T(2,128)}) %all-reduce.7.cloned.1.call-update) | async-done | bytes 524304
  (66 shorter events, 15.1 us)
Async XLA Ops:
  7.2 31.7 %all-gather.7.cloned.1.call-start = ((), (), s32[]{:S(2)}) async-start(), calls=%async_computation.1 | async-start | bytes 2359296 | tf_op jit(solution)/shard_map/all_gather | solution.py:49
  9.9 109.2 %all-gather.5.cloned.1.call-start = ((), (), s32[]{:S(2)}) async-start(), calls=%async_computation | async-start | bytes 8912896 | tf_op jit(solution)/shard_map/all_gather | solution.py:45
  12.9 179.6 %all-reduce.5.cloned.1.call-start = ((), (), s32[]{:S(2)}) async-start(), calls=%async_computation.4 | async-start | bytes 8388608 | tf_op jit(solution)/shard_map/psum | solution.py:13
  15.5 4.2 copy-start
  19.4 254.7 %all-gather.11.cloned.1.call-start = ((), (), s32[]{:S(2)}) async-start(), calls=%async_computation.3 | async-start | bytes 4456448 | tf_op jit(solution)/shard_map/all_gather | solution.py:56
  19.7 106.8 %copy-start.1 = (s32[32]{0:T(128)S(1)}, s32[32]{0:T(128)}, u32[]{:S(2)}) copy-start(s32[32]{0:T(128)} %param.15) | copy-start | bytes 388
  20.5 267.5 %all-gather.9.cloned.1.call-start = ((), (), s32[]{:S(2)}) async-start(), calls=%async_computation.2 | async-start | bytes 4718592 | tf_op jit(solution)/shard_map/all_gather | solution.py:53
  126.3 330.1 %all-reduce.7.cloned.1.call-start = ((), (), s32[]{:S(2)}) async-start(), calls=%async_computation.5 | async-start | bytes 1048576
Sparse Core Ops, SparseCore 0:
  10.1 28.7 all-gather.6
  41.6 77.5 all-gather.4
  121.5 70.9 all-reduce.4
  194.5 58.7 all-gather.10
  255.4 32.5 all-gather.8
  311.5 144.8 all-reduce.6
where the time goes:
time: 466 us; the launch traced here: 464 us
  waiting for transfers between devices  302 us (65%)
  local copies, waits for them, and re-layouts  92.7 us (20%)
  matrix products  27.1 us (6%)
  between operations  21.9 us (5%)
  other arithmetic  20.1 us (4%)
    unnamed x7, waiting for transfers between devices  144 us
    all_gather x1, waiting for transfers between devices, local(): panels = lax.all_gather(trials, 'col', axis=2, tiled=True)  80.3 us
    gather x24, local copies, waits for them, and re-layouts  48 us
    psum x1, waiting for transfers between devices, broadcast(): return lax.psum(jnp.where(mine, x, jnp.zeros_like(x)), axis)  45.6 us
    reshape x1, local copies, waits for them, and re-layouts, local(): jax.vmap(frames_for_row)(offsets)  25.8 us
    all_gather x1, waiting for transfers between devices, local(): lax.all_gather(conduction, 'row', axis=0, tiled=True)  18.4 us
    dot_general x1, matrix products, local(): jnp.einsum('vabmn,abnp->vamp', kernel_blocks, frames, preferred_element_t...  14.2 us
    all_gather x1, waiting for transfers between devices, local(): gathered = lax.all_gather(response_half, 'row', axis=1, tiled=True)  13.8 us
  transfers between devices with their start and end apart: 6, of which 5 were waited for; matrix products, arithmetic and copies ran while one was open for 24% of the time, Pallas kernels for 0%

commit v1 on v0

v1 whole, which is shorter than its diff:
```python
import jax
import jax.numpy as jnp
from jax import lax
from jax.experimental import pallas as pl
from jax.experimental.pallas import tpu as pltpu
from jax.sharding import PartitionSpec as P

BS = 128
NB = 32
SPAN = 16
SP = 512
NSLAB = 128
RING = 4
N_COL = 16
BF16 = jnp.bfloat16
F32 = jnp.float32
AXES = ("row", "col")


def place(x, core, y, z):
    return ((x % RING) * 2 + core) * N_COL + (y % RING) * RING + z % RING


def pairs(move):
    out = []
    for x in range(RING):
        for core in range(2):
            for y in range(RING):
                for z in range(RING):
                    target = move(x, core, y, z, 1 - 2 * core)
                    if target is not None:
                        out.append((place(x, core, y, z), place(*target)))
    return out


ALONG_X = pairs(lambda x, core, y, z, d: (x + d, core, y, z))
ALONG_Y = pairs(lambda x, core, y, z, d: (x, core, y + d, z))
ALONG_Z = pairs(lambda x, core, y, z, d: (x, core, y, z + d))
OTHER_CORE = pairs(lambda x, core, y, z, d: (x, 1 - core, y, z))
FROM_HOLDER = pairs(lambda x, core, y, z, d: (x, 1 - core, y, z) if x == y and core == z // 2 else None)


def hop(step):
    return pairs(lambda x, core, y, z, d: (x + d, core, y, z) if (d * (x - y)) % RING == step else None)


def send(value, route):
    return lax.ppermute(value, AXES, route)


def ring(value, route):
    held = [value]
    for _ in range(RING - 1):
        held.append(send(held[-1], route))
    return held


def plane_gather(piece, first, second):
    return ring(jnp.stack(ring(piece, first)), second)


def masked(values, block_mask, row_index, col_index):
    row_blocks, col_blocks = values.shape[0] // BS, values.shape[1] // BS
    tile_mask = lax.dynamic_slice(
        block_mask, (row_index * row_blocks, col_index * col_blocks), (row_blocks, col_blocks)
    ).astype(values.dtype)
    shaped = values.reshape(row_blocks, BS, col_blocks, BS)
    return (shaped * tile_mask[:, None, :, None]).reshape(values.shape)


def source(idx, half, h, g):
    step = 1 - 2 * idx[1]
    dy, dz = (h, g) if half == 0 else (g, h)
    return (idx[2] - step * dy) & 3, (idx[3] - step * dz) & 3


def response_kernel(idx, mask, *refs):
    t_refs, c_own, c_other, out, panel = refs[:8], refs[8], refs[9], refs[10], refs[11]
    x, core, row = idx[0], idx[1], idx[4]
    step = 1 - 2 * core
    for s in range(RING):
        panel[((x - step * s) & 3) * 2 + core] = c_own[s]
        panel[((x + step * s) & 3) * 2 + 1 - core] = c_other[s]
    first_lanes = lax.broadcasted_iota(jnp.int32, (BS, 2 * BS), 1) < BS
    for v in range(2):
        total = jnp.zeros((4 * BS, 2 * BS), F32)
        for h in range(RING):
            lefts, rights = [], []
            for g in range(RING):
                ys, zs = source(idx, v, h, g)
                col = ys * RING + zs
                rows = []
                for i in range(4):
                    at = (row * 4 + i) * NB + col * 2
                    scale = jnp.where(first_lanes, mask[at].astype(F32), mask[at + 1].astype(F32)).astype(BF16)
                    rows.append(t_refs[v * RING + h][g, i * BS:(i + 1) * BS, :] * scale)
                lefts.append(jnp.concatenate(rows, axis=0))
                half_rows = pl.multiple_of((zs & 1) * 2 * BS, 2 * BS)
                rights.append(panel[col // 2, pl.ds(half_rows, 2 * BS), :])
            total += jnp.dot(
                jnp.concatenate(lefts, axis=1), jnp.concatenate(rights, axis=0), preferred_element_type=F32
            )
        out[v] = total.astype(BF16)


def density_kernel(idx, mask, starts, *refs):
    v_refs, r_own, r_other = refs[:8], refs[8:12], refs[12:16]
    orb_hbm, near_hbm, far_hbm, k_out, d_out, r_panel, orb, partner, dens, sems = refs[16:]
    x, core, row, col = idx[0], idx[1], idx[4], idx[5]
    step = 1 - 2 * core
    copies = [
        pltpu.make_async_copy(orb_hbm, orb, sems.at[0]),
        pltpu.make_async_copy(near_hbm, partner.at[core], sems.at[1]),
        pltpu.make_async_copy(far_hbm, partner.at[1 - core], sems.at[2]),
    ]
    for copy in copies:
        copy.start()
    for s in range(RING):
        r_panel[((x - step * s) & 3) * 2 + core] = r_own[s][...]
        r_panel[((x + step * s) & 3) * 2 + 1 - core] = r_other[s][...]
    first_lanes = lax.broadcasted_iota(jnp.int32, (BS, 2 * BS), 1) < BS
    for half in range(2):
        totals = [jnp.zeros((2 * BS, 2 * BS), F32) for _ in range(2)]
        for h in range(RING):
            left = jnp.concatenate([v_refs[half * RING + h][g] for g in range(RING)], axis=1)
            for v in range(2):
                rights = []
                for g in range(RING):
                    ys, zs = source(idx, half, h, g)
                    half_rows = pl.multiple_of((zs & 1) * 2 * BS, 2 * BS)
                    rights.append(r_panel[(ys * RING + zs) // 2, v, pl.ds(half_rows, 2 * BS), :])
                totals[v] += jnp.dot(left, jnp.concatenate(rights, axis=0), preferred_element_type=F32)
        for v in range(2):
            for i in range(2):
                at = (row * 4 + half * 2 + i) * NB + col * 2
                scale = jnp.where(first_lanes, mask[at].astype(F32), mask[at + 1].astype(F32))
                begin = (half * 2 + i) * BS
                k_out[v, begin:begin + BS, :] = (totals[v][i * BS:(i + 1) * BS] * scale).astype(BF16)
    dens[...] = jnp.zeros_like(dens)
    for copy in copies:
        copy.wait()
    starts_j = [starts[col * 2 + j] for j in range(2)]
    for i in range(4):
        left = jnp.concatenate([k_out[v, i * BS:(i + 1) * BS, :] for v in range(2)], axis=0)
        start_i = starts[row * 4 + i]

        def slab(s, carry, left=left, start_i=start_i, i=i):
            offsets = [start_i + s - starts_j[j] for j in range(2)]
            inside = [(o >= 0) & (o < SPAN) for o in offsets]

            @pl.when(inside[0] | inside[1])
            def _():
                frames = []
                for j in range(2):
                    at = pl.multiple_of(jnp.clip(offsets[j], 0, SPAN - 1) * SP, SP)
                    frame = partner[j, :, pl.ds(at, SP)]
                    frames.append(frame * jnp.where(inside[j], 1.0, 0.0).astype(BF16))
                applied = jnp.dot(left, jnp.concatenate(frames, axis=0), preferred_element_type=F32)
                own = orb[i, :, pl.ds(pl.multiple_of(s * SP, SP), SP)].astype(F32)
                for v in range(2):
                    terms = jnp.sum(own * applied[v * BS:(v + 1) * BS], axis=0, keepdims=True)
                    dens[pl.ds(start_i + s, 1), v * SP:(v + 1) * SP] += terms

            return carry

        lax.fori_loop(0, SPAN, slab, 0)
    d_out[...] = dens[...]


SMEM = pl.BlockSpec(memory_space=pltpu.SMEM)
VMEM = pl.BlockSpec(memory_space=pltpu.VMEM)
ANY = pl.BlockSpec(memory_space=pl.ANY)


def local(p_valence, p_conduction, trial_vectors, mask_valence, mask_conduction, mask_trial, orbitals, sphere_starts):
    row, col = lax.axis_index("row"), lax.axis_index("col")
    x, core, y, z = row // 2, row % 2, col // RING, col % RING
    idx = jnp.stack([x, core, y, z, row, col]).astype(jnp.int32)
    mask_flat = mask_trial.reshape(-1)

    trials = plane_gather(trial_vectors[0], ALONG_Z, ALONG_Y) + plane_gather(trial_vectors[1], ALONG_Y, ALONG_Z)
    conduction = masked(p_conduction, mask_conduction, row, col)
    c_own = jnp.stack(ring(conduction, ALONG_X))
    c_other = send(c_own, OTHER_CORE)

    valence = masked(p_valence, mask_valence, row, col)
    valences = plane_gather(valence[:2 * BS], ALONG_Z, ALONG_Y) + plane_gather(valence[2 * BS:], ALONG_Y, ALONG_Z)

    first = 2 * (col % 2)
    mine = lax.dynamic_slice_in_dim(orbitals, first + core, 1, 0)[0]
    theirs = lax.dynamic_slice_in_dim(orbitals, first + 1 - core, 1, 0)[0]
    given = send(theirs, FROM_HOLDER)
    seed = jnp.where(core == z // 2, mine, given)
    half_points = SPAN * SP // 2
    hops = (1 - 2 * core) * (x - y) % RING
    parts = []
    for k in range(2):
        held = seed[:, k * half_points:(k + 1) * half_points]
        kept = held
        for step in range(RING - 1):
            held = send(held, hop(step))
            kept = jnp.where(hops == step + 1, held, kept)
        parts.append(kept)
    near = jnp.concatenate(parts, axis=1)
    far = send(near, OTHER_CORE)

    response = pl.pallas_call(
        response_kernel,
        name="response",
        out_shape=jax.ShapeDtypeStruct((2, 4 * BS, 2 * BS), BF16),
        in_specs=[SMEM, SMEM] + [VMEM] * 10,
        out_specs=VMEM,
        scratch_shapes=[pltpu.VMEM((8, 4 * BS, 2 * BS), BF16)],
        compiler_params=pltpu.CompilerParams(vmem_limit_bytes=40 * 2**20),
        cost_estimate=pl.CostEstimate(flops=2**32, bytes_accessed=11 * 2**20, transcendentals=0),
    )(idx, mask_flat, *trials, c_own, c_other)

    r_own = ring(response, ALONG_X)
    r_other = [send(piece, OTHER_CORE) for piece in r_own]

    kernel, density = pl.pallas_call(
        density_kernel,
        name="density",
        out_shape=(
            jax.ShapeDtypeStruct((2, 4 * BS, 2 * BS), BF16),
            jax.ShapeDtypeStruct((NSLAB, 2 * SP), F32),
        ),
        in_specs=[SMEM, SMEM, SMEM] + [VMEM] * 16 + [ANY] * 3,
        out_specs=(VMEM, VMEM),
        scratch_shapes=[
            pltpu.VMEM((8, 2, 4 * BS, 2 * BS), BF16),
            pltpu.VMEM((4, BS, SPAN * SP), BF16),
            pltpu.VMEM((2, BS, SPAN * SP), BF16),
            pltpu.VMEM((NSLAB, 2 * SP), F32),
            pltpu.SemaphoreType.DMA((3,)),
        ],
        compiler_params=pltpu.CompilerParams(vmem_limit_bytes=48 * 2**20),
        cost_estimate=pl.CostEstimate(flops=2**33, bytes_accessed=22 * 2**20, transcendentals=0),
    )(idx, mask_flat, sphere_starts, *valences, *r_own, *r_other, orbitals, near, far)

    terms = lax.all_to_all(density, AXES, 0, 0, tiled=True)
    return kernel, jnp.sum(terms, axis=0).reshape(2, SP)


def solution(mesh):
    placed = (
        P("row", "col"),
        P("row", "col"),
        P(None, "row", "col"),
        P(),
        P(),
        P(),
        P("row", None, None),
        P(),
    )
    return jax.shard_map(
        local,
        mesh=mesh,
        in_specs=placed,
        out_specs=(P(None, "row", "col"), P(None, AXES)),
        check_vma=False,
    )
```

time: 466 us -> 247 us (0.53)
  waiting for transfers between devices: 302 us -> 65.9 us
  starting transfers between devices: 0.43 us -> 111 us
  local copies, waits for them, and re-layouts: 92.7 us -> 12 us
  matrix products: 27.1 us -> 0 us
  blocking collectives: 0 us -> 23.6 us
  between operations: 21.9 us -> 1.03 us
  Pallas kernels: 0 us -> 20 us
  other arithmetic: 20.1 us -> 12.8 us
    unnamed x7 -> x0, waiting for transfers between devices: 144 us -> none
    all_gather x4 -> x0, waiting for transfers between devices: 112 us -> none  [the longest x1 80.3 us: local(): panels = lax.all_gather(trials, 'col', axis=2, tiled=True)]
    ppermute x0 -> x43, starting transfers between devices: none -> 111 us  [send(): return lax.ppermute(value, AXES, route)]
    ppermute x0 -> x43, waiting for transfers between devices: none -> 65.9 us  [send(): return lax.ppermute(value, AXES, route)]
    gather x24 -> x0, local copies, waits for them, and re-layouts: 48 us -> none
    psum x1 -> x0, waiting for transfers between devices: 45.6 us -> none  [broadcast(): return lax.psum(jnp.where(mine, x, jnp.zeros_like(x)), axis)]
    dot_general x3 -> x0, matrix products: 27.1 us -> none  [the longest x1 14.2 us: local(): jnp.einsum('vabmn,abnp->vamp', kernel_blocks, frames, preferred_element_t...]
    reshape x4 -> x3, local copies, waits for them, and re-layouts: 27.6 us -> 2.41 us  [the longest x1 1.01 us: masked(): shaped = values.reshape(row_blocks, BS, col_blocks, BS)]
  transfers between devices with their start and end apart: 6 -> 43, of which waited for: 5 -> 23; matrix products, arithmetic and copies ran while one was open for 24% -> 5% of each run, Pallas kernels for 0% -> 2%
where the time goes in v1:
time: 247 us
  starting transfers between devices  111 us (45%)
  waiting for transfers between devices  65.9 us (27%)
  blocking collectives  23.6 us (10%)
  Pallas kernels  20 us (8%)
  other arithmetic  12.8 us (5%)
  local copies, waits for them, and re-layouts  12 us (5%)
    ppermute x43, starting transfers between devices, send(): return lax.ppermute(value, AXES, route)  111 us
    ppermute x43, waiting for transfers between devices, send(): return lax.ppermute(value, AXES, route)  65.9 us
    all_to_all x1, blocking collectives, local(): terms = lax.all_to_all(density, AXES, 0, 0, tiled=True)  23.6 us
    pallas_call x1, Pallas kernels, local(): pl.pallas_call(density_kernel, name='density', out_shape=(jax.ShapeDtypeS...  14.4 us
    unnamed x52, local copies, waits for them, and re-layouts  6.51 us
    pallas_call x1, Pallas kernels, local(): pl.pallas_call(response_kernel, name='response', out_shape=jax.ShapeDtype...  5.58 us
  transfers between devices with their start and end apart: 43, of which 23 were waited for; matrix products, arithmetic and copies ran while one was open for 5% of the time, Pallas kernels for 2%

profile of v1, /device:TPU:1, one launch (start us, length us, event | category | flops | bytes accessed | tf_op | source)
XLA Modules:
  0.0 246.5 jit_solution(2880932962358716041)
XLA Ops:
  3.7 5.1 %collective-permute-done.35 = bf16[128,8192]{1,0:T(8,128)(2,1)} collective-permute-done((bf16[128,8192]{1,0:T(8,128)(2,1)S(1)}, bf16[128,8192]{1,0:T(8,128)(2,1)}, u32[]{:S(2)}, u32[]{:S(2)}) %collective-permute-start.35) | collective-permute-done | bytes 2097184 | tf_op jit(solution)/shard_map/ppermute | solution.py:48
  14.3 11.7 %collective-permute-done.36 = bf16[128,4096]{1,0:T(8,128)(2,1)S(1)} collective-permute-done((bf16[128,4096]{1,0:T(8,128)(2,1)S(1)}, bf16[128,4096]{1,0:T(8,128)(2,1)S(1)}, u32[]{:S(2)}, u32[]{:S(2)}) %collective-permute-start.36) | collective-permute-done | bytes 1048608 | tf_op jit(solution)/shard_map/ppermute | solution.py:48
  27.6 4.0 %collective-permute-start.12 = (bf16[512,256]{1,0:T(8,128)(2,1)S(1)}, bf16[512,256]{1,0:T(8,128)(2,1)S(1)}, u32[]{:S(2)}, u32[]{:S(2)}) collective-permute-start(bf16[512,256]{1,0:T(8,128)(2,1)S(1)} %get-tuple-element.9), channel_id=1, source_target_pairs={{0,1},{1,2},{2,3},{3,0},{4,5},{5,6},{6,7},{7,4},{8,9},{9,10},{10,1... | collective-permute-start | bytes 786440 | tf_op jit(solution)/shard_map/ppermute | solution.py:48
  38.1 9.7 %collective-permute-done.18 = bf16[512,256]{1,0:T(8,128)(2,1)S(1)} collective-permute-done((bf16[512,256]{1,0:T(8,128)(2,1)S(1)}, bf16[512,256]{1,0:T(8,128)(2,1)S(1)}, u32[]{:S(2)}, u32[]{:S(2)}) %collective-permute-start.18) | collective-permute-done | bytes 262176 | tf_op jit(solution)/shard_map/ppermute | solution.py:48
  47.8 4.3 %collective-permute-start.19 = (bf16[512,256]{1,0:T(8,128)(2,1)S(1)}, bf16[512,256]{1,0:T(8,128)(2,1)S(1)}, u32[]{:S(2)}, u32[]{:S(2)}) collective-permute-start(bf16[512,256]{1,0:T(8,128)(2,1)S(1)} %collective-permute-done.18), channel_id=1, source_target_pairs={{0,4},{1,5},{2,6},{3,7},{4,8},{5,9},{6,10},{7,11},{8,12},{9,13},{1... | collective-permute-start | bytes 786440 | tf_op jit(solution)/shard_map/ppermute | solution.py:48
  52.1 3.3 %collective-permute-start.14 = (bf16[512,256]{1,0:T(8,128)(2,1)S(1)}, bf16[512,256]{1,0:T(8,128)(2,1)S(1)}, u32[]{:S(2)}, u32[]{:S(2)}) collective-permute-start(bf16[512,256]{1,0:T(8,128)(2,1)S(1)} %collective-permute-done.13), channel_id=1, source_target_pairs={{0,1},{1,2},{2,3},{3,0},{4,5},{5,6},{6,7},{7,4},{8,9},{9,10},{10,1... | collective-permute-start | bytes 786440 | tf_op jit(solution)/shard_map/ppermute | solution.py:48
  60.7 3.2 %collective-permute-start.15 = (bf16[4,512,256]{2,1,0:T(8,128)(2,1)S(1)}, bf16[4,512,256]{2,1,0:T(8,128)(2,1)}, u32[]{:S(2)}, u32[]{:S(2)}) collective-permute-start(bf16[4,512,256]{2,1,0:T(8,128)(2,1)S(1)} %pad_maximum_fusion.1.refs_0_), channel_id=1, source_target_pairs={{0,4},{1,5},{2,6},{3,7},{4,8},{5,9},{6,10},{7,11},{8,12},{9,13},{1... | collective-permute-start | bytes 3145736 | tf_op jit(solution)/shard_map/ppermute | solution.py:48
  65.2 3.2 %collective-permute-start.21 = (bf16[4,512,256]{2,1,0:T(8,128)(2,1)S(1)}, bf16[4,512,256]{2,1,0:T(8,128)(2,1)}, u32[]{:S(2)}, u32[]{:S(2)}) collective-permute-start(bf16[4,512,256]{2,1,0:T(8,128)(2,1)S(1)} %pad_maximum_fusion.2.refs_4_), channel_id=1, source_target_pairs={{0,1},{1,2},{2,3},{3,0},{4,5},{5,6},{6,7},{7,4},{8,9},{9,10},{10,1... | collective-permute-start | bytes 3145736 | tf_op jit(solution)/shard_map/ppermute | solution.py:48
  75.7 3.5 %collective-permute-start.16 = (bf16[4,512,256]{2,1,0:T(8,128)(2,1)}, bf16[4,512,256]{2,1,0:T(8,128)(2,1)}, u32[]{:S(2)}, u32[]{:S(2)}) collective-permute-start(bf16[4,512,256]{2,1,0:T(8,128)(2,1)} %collective-permute-done.15.refs_1_), channel_id=1, source_target_pairs={{0,4},{1,5},{2,6},{3,7},{4,8},{5,9},{6,10},{7,11},{8,12},{9,13},{1... | collective-permute-start | bytes 3145736 | tf_op jit(solution)/shard_map/ppermute | solution.py:48
  80.1 3.3 %collective-permute-start.22 = (bf16[4,512,256]{2,1,0:T(8,128)(2,1)}, bf16[4,512,256]{2,1,0:T(8,128)(2,1)}, u32[]{:S(2)}, u32[]{:S(2)}) collective-permute-start(bf16[4,512,256]{2,1,0:T(8,128)(2,1)} %collective-permute-done.21.refs_5_), channel_id=1, source_target_pairs={{0,1},{1,2},{2,3},{3,0},{4,5},{5,6},{6,7},{7,4},{8,9},{9,10},{10,1... | collective-permute-start | bytes 3145736 | tf_op jit(solution)/shard_map/ppermute | solution.py:48
  84.7 6.1 %collective-permute-done.24 = bf16[512,256]{1,0:T(8,128)(2,1)S(1)} collective-permute-done((bf16[512,256]{1,0:T(8,128)(2,1)S(1)}, bf16[512,256]{1,0:T(8,128)(2,1)S(1)}, u32[]{:S(2)}, u32[]{:S(2)}) %collective-permute-start.24) | collective-permute-done | bytes 262176 | tf_op jit(solution)/shard_map/ppermute | solution.py:48
  103.9 9.2 %collective-permute-start.27 = (bf16[4,512,256]{2,1,0:T(8,128)(2,1)S(1)}, bf16[4,512,256]{2,1,0:T(8,128)(2,1)}, u32[]{:S(2)}, u32[]{:S(2)}) collective-permute-start(bf16[4,512,256]{2,1,0:T(8,128)(2,1)S(1)} %pad_maximum_fusion.3.refs_8_), channel_id=1, source_target_pairs={{0,16},{1,17},{2,18},{3,19},{4,20},{5,21},{6,22},{7,23},{8,24},{9,... | collective-permute-start | bytes 3145736 | tf_op jit(solution)/shard_map/ppermute | solution.py:48
  113.1 4.1 %collective-permute-start.17 = (bf16[4,512,256]{2,1,0:T(8,128)(2,1)}, bf16[4,512,256]{2,1,0:T(8,128)(2,1)}, u32[]{:S(2)}, u32[]{:S(2)}) collective-permute-start(bf16[4,512,256]{2,1,0:T(8,128)(2,1)} %collective-permute-done.16.refs_2_), channel_id=1, source_target_pairs={{0,4},{1,5},{2,6},{3,7},{4,8},{5,9},{6,10},{7,11},{8,12},{9,13},{1... | collective-permute-start | bytes 3145736 | tf_op jit(solution)/shard_map/ppermute | solution.py:48
  120.4 4.2 %collective-permute-start.6 = (bf16[256,256]{1,0:T(8,128)(2,1)S(1)}, bf16[256,256]{1,0:T(8,128)(2,1)S(1)}, u32[]{:S(2)}, u32[]{:S(2)}) collective-permute-start(bf16[256,256]{1,0:T(8,128)(2,1)S(1)} %bitcast.59), channel_id=1, source_target_pairs={{0,4},{1,5},{2,6},{3,7},{4,8},{5,9},{6,10},{7,11},{8,12},{9,13},{1... | collective-permute-start | bytes 393224 | tf_op jit(solution)/shard_map/ppermute | solution.py:48
  124.6 5.9 %collective-permute-done.6 = bf16[256,256]{1,0:T(8,128)(2,1)S(1)} collective-permute-done((bf16[256,256]{1,0:T(8,128)(2,1)S(1)}, bf16[256,256]{1,0:T(8,128)(2,1)S(1)}, u32[]{:S(2)}, u32[]{:S(2)}) %collective-permute-start.6) | collective-permute-done | bytes 131104 | tf_op jit(solution)/shard_map/ppermute | solution.py:48
  135.5 4.2 %collective-permute-start.7 = (bf16[256,256]{1,0:T(8,128)(2,1)S(1)}, bf16[256,256]{1,0:T(8,128)(2,1)S(1)}, u32[]{:S(2)}, u32[]{:S(2)}) collective-permute-start(bf16[256,256]{1,0:T(8,128)(2,1)S(1)} %collective-permute-done.6), channel_id=1, source_target_pairs={{0,4},{1,5},{2,6},{3,7},{4,8},{5,9},{6,10},{7,11},{8,12},{9,13},{1... | collective-permute-start | bytes 393224 | tf_op jit(solution)/shard_map/ppermute | solution.py:48
  142.2 3.4 %collective-permute-start.1 = (bf16[256,256]{1,0:T(8,128)(2,1)S(1)}, bf16[256,256]{1,0:T(8,128)(2,1)}, u32[]{:S(2)}, u32[]{:S(2)}) collective-permute-start(bf16[256,256]{1,0:T(8,128)(2,1)S(1)} %collective-permute-done), channel_id=1, source_target_pairs={{0,1},{1,2},{2,3},{3,0},{4,5},{5,6},{6,7},{7,4},{8,9},{9,10},{10,1... | collective-permute-start | bytes 393224 | tf_op jit(solution)/shard_map/ppermute | solution.py:48
  152.3 3.2 %collective-permute-start.2 = (bf16[256,256]{1,0:T(8,128)(2,1)}, bf16[256,256]{1,0:T(8,128)(2,1)}, u32[]{:S(2)}, u32[]{:S(2)}) collective-permute-start(bf16[256,256]{1,0:T(8,128)(2,1)} %collective-permute-done.1), channel_id=1, source_target_pairs={{0,1},{1,2},{2,3},{3,0},{4,5},{5,6},{6,7},{7,4},{8,9},{9,10},{10,1... | collective-permute-start | bytes 393224 | tf_op jit(solution)/shard_map/ppermute | solution.py:48
  165.1 5.6 %response.1.refs_8_ = bf16[2,512,256]{2,1,0:T(8,128)(2,1)S(1)} custom-call(s32[6]{0:T(128)S(1)} %stack.93.idx, s32[1024]{0:T(1024)S(1)} %reshape.31.mask, bf16[4,512,256]{2,1,0:T(8,128)(2,1)S(1)} %pad_maximum_fusion.1.refs_0_, bf16[4,512,256]{2,1,0:T(8,128)(2,1)} %collective-permute-done.15.refs_1_, bf16[4,512,256]{2,1,0:T(8,128)(2,1)} %collective-permute-done.16.refs_2_, ...), custom_call_target="tpu_custom_call" | custom-call | flops 4294967296 | bytes 11534336 | tf_op jit(solution)/shard_map/response/pallas_call | solution.py:207
  178.1 4.0 %collective-permute-start.4 = (bf16[4,256,256]{2,1,0:T(8,128)(2,1)S(1)}, bf16[4,256,256]{2,1,0:T(8,128)(2,1)S(1)}, u32[]{:S(2)}, u32[]{:S(2)}) collective-permute-start(bf16[4,256,256]{2,1,0:T(8,128)(2,1)S(1)} %collective-permute-done.3.refs_1_), channel_id=1, source_target_pairs={{0,4},{1,5},{2,6},{3,7},{4,8},{5,9},{6,10},{7,11},{8,12},{9,13},{1... | collective-permute-start | bytes 1572872 | tf_op jit(solution)/shard_map/ppermute | solution.py:48
  184.2 3.4 %collective-permute-start.11 = (bf16[4,256,256]{2,1,0:T(8,128)(2,1)S(1)}, bf16[4,256,256]{2,1,0:T(8,128)(2,1)S(1)}, u32[]{:S(2)}, u32[]{:S(2)}) collective-permute-start(bf16[4,256,256]{2,1,0:T(8,128)(2,1)S(1)} %collective-permute-done.10.refs_6_), channel_id=1, source_target_pairs={{0,1},{1,2},{2,3},{3,0},{4,5},{5,6},{6,7},{7,4},{8,9},{9,10},{10,1... | collective-permute-start | bytes 1572872 | tf_op jit(solution)/shard_map/ppermute | solution.py:48
  188.2 3.4 %collective-permute-start.5 = (bf16[4,256,256]{2,1,0:T(8,128)(2,1)S(1)}, bf16[4,256,256]{2,1,0:T(8,128)(2,1)S(1)}, u32[]{:S(2)}, u32[]{:S(2)}) collective-permute-start(bf16[4,256,256]{2,1,0:T(8,128)(2,1)S(1)} %collective-permute-done.4.refs_2_), channel_id=1, source_target_pairs={{0,4},{1,5},{2,6},{3,7},{4,8},{5,9},{6,10},{7,11},{8,12},{9,13},{1... | collective-permute-start | bytes 1572872 | tf_op jit(solution)/shard_map/ppermute | solution.py:48
  207.1 14.4 %density.1 = (bf16[2,512,256]{2,1,0:T(8,128)(2,1)}, f32[128,1024]{1,0:T(8,128)S(1)}) custom-call(s32[6]{0:T(128)S(1)} %stack.93.idx, s32[1024]{0:T(1024)S(1)} %reshape.31.mask, s32[32]{0:T(128)S(1)} %copy-done, bf16[4,256,256]{2,1,0:T(8,128)(2,1)S(1)} %pad_maximum_fusion.4.refs_0_, bf16[4,256,256]{2,1,0:T(8,128)(2,1)S(1)} %collective-permute-done.3.refs_1_, ...), custom_call_target="tpu_custom_call" | custom-call | flops 8589934592 | bytes 23068672 | tf_op jit(solution)/shard_map/density/pallas_call | solution.py:221
  222.0 23.6 %all_to_all.9 = f32[128,1,1024]{2,1,0:T(1,128)S(1)} all-to-all(f32[128,1,1024]{2,1,0:T(1,128)S(1)} %copy.10), channel_id=1, replica_groups=mesh['row'=8,'col'=16] {'row','col'}, dimensions={0} | all-to-all | bytes 1048576 | tf_op jit(solution)/shard_map/all_to_all | solution.py:241
  (142 shorter events, 99.6 us)
Async XLA Ops:
  12.8 13.2 %collective-permute-start.36 = (bf16[128,4096]{1,0:T(8,128)(2,1)S(1)}, bf16[128,4096]{1,0:T(8,128)(2,1)S(1)}, u32[]{:S(2)}, u32[]{:S(2)}) collective-permute-start(bf16[128,4096]{1,0:T(8,128)(2,1)S(1)} %slice.34), channel_id=1, source_target_pairs={{0,32},{1,33},{2,34},{3,35},{16,112},{17,113},{18,114},{19,115},{3... | collective-permute-start | bytes 3145736 | tf_op jit(solution)/shard_map/ppermute | solution.py:48
  31.7 36.7 %collective-permute-start.38 = (bf16[128,4096]{1,0:T(8,128)(2,1)}, bf16[128,4096]{1,0:T(8,128)(2,1)}, u32[]{:S(2)}, u32[]{:S(2)}) collective-permute-start(bf16[128,4096]{1,0:T(8,128)(2,1)} %collective-permute-done.37), channel_id=1, source_target_pairs={{8,40},{9,41},{10,42},{11,43},{24,120},{25,121},{26,122},{27,123},... | collective-permute-start | bytes 3145736 | tf_op jit(solution)/shard_map/ppermute | solution.py:48
  33.4 14.5 %collective-permute-start.18 = (bf16[512,256]{1,0:T(8,128)(2,1)S(1)}, bf16[512,256]{1,0:T(8,128)(2,1)S(1)}, u32[]{:S(2)}, u32[]{:S(2)}) collective-permute-start(bf16[512,256]{1,0:T(8,128)(2,1)S(1)} %get-tuple-element.10), channel_id=1, source_target_pairs={{0,4},{1,5},{2,6},{3,7},{4,8},{5,9},{6,10},{7,11},{8,12},{9,13},{1... | collective-permute-start | bytes 786440 | tf_op jit(solution)/shard_map/ppermute | solution.py:48
  35.0 17.1 %collective-permute-start.13 = (bf16[512,256]{1,0:T(8,128)(2,1)S(1)}, bf16[512,256]{1,0:T(8,128)(2,1)S(1)}, u32[]{:S(2)}, u32[]{:S(2)}) collective-permute-start(bf16[512,256]{1,0:T(8,128)(2,1)S(1)} %collective-permute-done.12), channel_id=1, source_target_pairs={{0,1},{1,2},{2,3},{3,0},{4,5},{5,6},{6,7},{7,4},{8,9},{9,10},{10,1... | collective-permute-start | bytes 786440 | tf_op jit(solution)/shard_map/ppermute | solution.py:48
  60.7 14.9 %collective-permute-start.15 = (bf16[4,512,256]{2,1,0:T(8,128)(2,1)S(1)}, bf16[4,512,256]{2,1,0:T(8,128)(2,1)}, u32[]{:S(2)}, u32[]{:S(2)}) collective-permute-start(bf16[4,512,256]{2,1,0:T(8,128)(2,1)S(1)} %pad_maximum_fusion.1.refs_0_), channel_id=1, source_target_pairs={{0,4},{1,5},{2,6},{3,7},{4,8},{5,9},{6,10},{7,11},{8,12},{9,13},{1... | collective-permute-start | bytes 3145736 | tf_op jit(solution)/shard_map/ppermute | solution.py:48
  65.2 14.9 %collective-permute-start.21 = (bf16[4,512,256]{2,1,0:T(8,128)(2,1)S(1)}, bf16[4,512,256]{2,1,0:T(8,128)(2,1)}, u32[]{:S(2)}, u32[]{:S(2)}) collective-permute-start(bf16[4,512,256]{2,1,0:T(8,128)(2,1)S(1)} %pad_maximum_fusion.2.refs_4_), channel_id=1, source_target_pairs={{0,1},{1,2},{2,3},{3,0},{4,5},{5,6},{6,7},{7,4},{8,9},{9,10},{10,1... | collective-permute-start | bytes 3145736 | tf_op jit(solution)/shard_map/ppermute | solution.py:48
  70.0 21.5 %collective-permute-start.39 = (bf16[128,4096]{1,0:T(8,128)(2,1)}, bf16[128,4096]{1,0:T(8,128)(2,1)}, u32[]{:S(2)}, u32[]{:S(2)}) collective-permute-start(bf16[128,4096]{1,0:T(8,128)(2,1)} %get-tuple-element.7), channel_id=1, source_target_pairs={{0,32},{1,33},{2,34},{3,35},{16,112},{17,113},{18,114},{19,115},{3... | collective-permute-start | bytes 3145736 | tf_op jit(solution)/shard_map/ppermute | solution.py:48
  75.7 37.4 %collective-permute-start.16 = (bf16[4,512,256]{2,1,0:T(8,128)(2,1)}, bf16[4,512,256]{2,1,0:T(8,128)(2,1)}, u32[]{:S(2)}, u32[]{:S(2)}) collective-permute-start(bf16[4,512,256]{2,1,0:T(8,128)(2,1)} %collective-permute-done.15.refs_1_), channel_id=1, source_target_pairs={{0,4},{1,5},{2,6},{3,7},{4,8},{5,9},{6,10},{7,11},{8,12},{9,13},{1... | collective-permute-start | bytes 3145736 | tf_op jit(solution)/shard_map/ppermute | solution.py:48
  80.1 37.1 %collective-permute-start.22 = (bf16[4,512,256]{2,1,0:T(8,128)(2,1)}, bf16[4,512,256]{2,1,0:T(8,128)(2,1)}, u32[]{:S(2)}, u32[]{:S(2)}) collective-permute-start(bf16[4,512,256]{2,1,0:T(8,128)(2,1)} %collective-permute-done.21.refs_5_), channel_id=1, source_target_pairs={{0,1},{1,2},{2,3},{3,0},{4,5},{5,6},{6,7},{7,4},{8,9},{9,10},{10,1... | collective-permute-start | bytes 3145736 | tf_op jit(solution)/shard_map/ppermute | solution.py:48
  91.5 48.1 %collective-permute-start.40 = (bf16[128,4096]{1,0:T(8,128)(2,1)}, bf16[128,4096]{1,0:T(8,128)(2,1)}, u32[]{:S(2)}, u32[]{:S(2)}) collective-permute-start(bf16[128,4096]{1,0:T(8,128)(2,1)} %collective-permute-done.39), channel_id=1, source_target_pairs={{12,44},{13,45},{14,46},{15,47},{20,116},{21,117},{22,118},{23,119... | collective-permute-start | bytes 3145736 | tf_op jit(solution)/shard_map/ppermute | solution.py:48
  103.9 58.0 %collective-permute-start.27 = (bf16[4,512,256]{2,1,0:T(8,128)(2,1)S(1)}, bf16[4,512,256]{2,1,0:T(8,128)(2,1)}, u32[]{:S(2)}, u32[]{:S(2)}) collective-permute-start(bf16[4,512,256]{2,1,0:T(8,128)(2,1)S(1)} %pad_maximum_fusion.3.refs_8_), channel_id=1, source_target_pairs={{0,16},{1,17},{2,18},{3,19},{4,20},{5,21},{6,22},{7,23},{8,24},{9,... | collective-permute-start | bytes 3145736 | tf_op jit(solution)/shard_map/ppermute | solution.py:48
  113.1 52.0 %collective-permute-start.17 = (bf16[4,512,256]{2,1,0:T(8,128)(2,1)}, bf16[4,512,256]{2,1,0:T(8,128)(2,1)}, u32[]{:S(2)}, u32[]{:S(2)}) collective-permute-start(bf16[4,512,256]{2,1,0:T(8,128)(2,1)} %collective-permute-done.16.refs_2_), channel_id=1, source_target_pairs={{0,4},{1,5},{2,6},{3,7},{4,8},{5,9},{6,10},{7,11},{8,12},{9,13},{1... | collective-permute-start | bytes 3145736 | tf_op jit(solution)/shard_map/ppermute | solution.py:48
  117.2 47.9 %collective-permute-start.23 = (bf16[4,512,256]{2,1,0:T(8,128)(2,1)}, bf16[4,512,256]{2,1,0:T(8,128)(2,1)}, u32[]{:S(2)}, u32[]{:S(2)}) collective-permute-start(bf16[4,512,256]{2,1,0:T(8,128)(2,1)} %collective-permute-done.22.refs_6_), channel_id=1, source_target_pairs={{0,1},{1,2},{2,3},{3,0},{4,5},{5,6},{6,7},{7,4},{8,9},{9,10},{10,1... | collective-permute-start | bytes 3145736 | tf_op jit(solution)/shard_map/ppermute | solution.py:48
  120.4 10.2 %collective-permute-start.6 = (bf16[256,256]{1,0:T(8,128)(2,1)S(1)}, bf16[256,256]{1,0:T(8,128)(2,1)S(1)}, u32[]{:S(2)}, u32[]{:S(2)}) collective-permute-start(bf16[256,256]{1,0:T(8,128)(2,1)S(1)} %bitcast.59), channel_id=1, source_target_pairs={{0,4},{1,5},{2,6},{3,7},{4,8},{5,9},{6,10},{7,11},{8,12},{9,13},{1... | collective-permute-start | bytes 393224 | tf_op jit(solution)/shard_map/ppermute | solution.py:48
  139.6 31.2 %collective-permute-start.41 = (bf16[128,4096]{1,0:T(8,128)(2,1)}, bf16[128,4096]{1,0:T(8,128)(2,1)}, u32[]{:S(2)}, u32[]{:S(2)}) collective-permute-start(bf16[128,4096]{1,0:T(8,128)(2,1)} %collective-permute-done.40), channel_id=1, source_target_pairs={{8,40},{9,41},{10,42},{11,43},{24,120},{25,121},{26,122},{27,123},... | collective-permute-start | bytes 3145736 | tf_op jit(solution)/shard_map/ppermute | solution.py:48
  157.8 17.3 %collective-permute-start.9 = (bf16[4,256,256]{2,1,0:T(8,128)(2,1)S(1)}, bf16[4,256,256]{2,1,0:T(8,128)(2,1)S(1)}, u32[]{:S(2)}, u32[]{:S(2)}) collective-permute-start(bf16[4,256,256]{2,1,0:T(8,128)(2,1)S(1)} %pad_maximum_fusion.5.refs_4_), channel_id=1, source_target_pairs={{0,1},{1,2},{2,3},{3,0},{4,5},{5,6},{6,7},{7,4},{8,9},{9,10},{10,1... | collective-permute-start | bytes 1572872 | tf_op jit(solution)/shard_map/ppermute | solution.py:48
  162.0 16.1 %collective-permute-start.3 = (bf16[4,256,256]{2,1,0:T(8,128)(2,1)S(1)}, bf16[4,256,256]{2,1,0:T(8,128)(2,1)S(1)}, u32[]{:S(2)}, u32[]{:S(2)}) collective-permute-start(bf16[4,256,256]{2,1,0:T(8,128)(2,1)S(1)} %pad_maximum_fusion.4.refs_0_), channel_id=1, source_target_pairs={{0,4},{1,5},{2,6},{3,7},{4,8},{5,9},{6,10},{7,11},{8,12},{9,13},{1... | collective-permute-start | bytes 1572872 | tf_op jit(solution)/shard_map/ppermute | solution.py:48
  170.7 11.4 %collective-permute-start.28 = (bf16[2,512,256]{2,1,0:T(8,128)(2,1)S(1)}, bf16[2,512,256]{2,1,0:T(8,128)(2,1)S(1)}, u32[]{:S(2)}, u32[]{:S(2)}) collective-permute-start(bf16[2,512,256]{2,1,0:T(8,128)(2,1)S(1)} %response.1.refs_8_), channel_id=1, source_target_pairs={{0,32},{1,33},{2,34},{3,35},{4,36},{5,37},{6,38},{7,39},{8,40},{9,... | collective-permute-start | bytes 1572872 | tf_op jit(solution)/shard_map/ppermute | solution.py:48
  172.1 32.8 %collective-permute-start.42 = (bf16[128,8192]{1,0:T(8,128)(2,1)S(1)}, bf16[128,8192]{1,0:T(8,128)(2,1)S(1)}, u32[]{:S(2)}, u32[]{:S(2)}) collective-permute-start(bf16[128,8192]{1,0:T(8,128)(2,1)S(1)} %pad_maximum_fusion.refs_17_), channel_id=1, source_target_pairs={{0,16},{1,17},{2,18},{3,19},{4,20},{5,21},{6,22},{7,23},{8,24},{9,... | collective-permute-start | bytes 6291464 | tf_op jit(solution)/shard_map/ppermute | solution.py:48
  178.1 10.1 %collective-permute-start.4 = (bf16[4,256,256]{2,1,0:T(8,128)(2,1)S(1)}, bf16[4,256,256]{2,1,0:T(8,128)(2,1)S(1)}, u32[]{:S(2)}, u32[]{:S(2)}) collective-permute-start(bf16[4,256,256]{2,1,0:T(8,128)(2,1)S(1)} %collective-permute-done.3.refs_1_), channel_id=1, source_target_pairs={{0,4},{1,5},{2,6},{3,7},{4,8},{5,9},{6,10},{7,11},{8,12},{9,13},{1... | collective-permute-start | bytes 1572872 | tf_op jit(solution)/shard_map/ppermute | solution.py:48
  182.1 9.5 %collective-permute-start.29 = (bf16[2,512,256]{2,1,0:T(8,128)(2,1)S(1)}, bf16[2,512,256]{2,1,0:T(8,128)(2,1)S(1)}, u32[]{:S(2)}, u32[]{:S(2)}) collective-permute-start(bf16[2,512,256]{2,1,0:T(8,128)(2,1)S(1)} %collective-permute-done.28.refs_9_), channel_id=1, source_target_pairs={{0,32},{1,33},{2,34},{3,35},{4,36},{5,37},{6,38},{7,39},{8,40},{9,... | collective-permute-start | bytes 1572872 | tf_op jit(solution)/shard_map/ppermute | solution.py:48
  184.2 9.5 %collective-permute-start.11 = (bf16[4,256,256]{2,1,0:T(8,128)(2,1)S(1)}, bf16[4,256,256]{2,1,0:T(8,128)(2,1)S(1)}, u32[]{:S(2)}, u32[]{:S(2)}) collective-permute-start(bf16[4,256,256]{2,1,0:T(8,128)(2,1)S(1)} %collective-permute-done.10.refs_6_), channel_id=1, source_target_pairs={{0,1},{1,2},{2,3},{3,0},{4,5},{5,6},{6,7},{7,4},{8,9},{9,10},{10,1... | collective-permute-start | bytes 1572872 | tf_op jit(solution)/shard_map/ppermute | solution.py:48
  191.7 11.7 %collective-permute-start.31 = (bf16[2,512,256]{2,1,0:T(8,128)(2,1)S(1)}, bf16[2,512,256]{2,1,0:T(8,128)(2,1)S(1)}, u32[]{:S(2)}, u32[]{:S(2)}) collective-permute-start(bf16[2,512,256]{2,1,0:T(8,128)(2,1)S(1)} %response.1.refs_8_), channel_id=1, source_target_pairs={{0,16},{1,17},{2,18},{3,19},{4,20},{5,21},{6,22},{7,23},{8,24},{9,... | collective-permute-start | bytes 1572872 | tf_op jit(solution)/shard_map/ppermute | solution.py:48
  193.8 9.6 %collective-permute-start.32 = (bf16[2,512,256]{2,1,0:T(8,128)(2,1)S(1)}, bf16[2,512,256]{2,1,0:T(8,128)(2,1)S(1)}, u32[]{:S(2)}, u32[]{:S(2)}) collective-permute-start(bf16[2,512,256]{2,1,0:T(8,128)(2,1)S(1)} %collective-permute-done.28.refs_9_), channel_id=1, source_target_pairs={{0,16},{1,17},{2,18},{3,19},{4,20},{5,21},{6,22},{7,23},{8,24},{9,... | collective-permute-start | bytes 1572872 | tf_op jit(solution)/shard_map/ppermute | solution.py:48
  (44 other events, 365.0 us)

commit v2 on v1

v2 whole, which is shorter than its diff:
```python
import functools

import jax
import jax.numpy as jnp
from jax import lax
from jax.experimental import pallas as pl
from jax.experimental.pallas import tpu as pltpu
from jax.sharding import PartitionSpec as P

BS = 128
NB = 32
SPAN = 16
SP = 512
NSLAB = 128
RING = 4
N_COL = 16
BF16 = jnp.bfloat16
F32 = jnp.float32
AXES = ("row", "col")


def place(x, core, y, z):
    return ((x % RING) * 2 + core) * N_COL + (y % RING) * RING + z % RING


def pairs(move):
    out = []
    for x in range(RING):
        for core in range(2):
            for y in range(RING):
                for z in range(RING):
                    target = move(x, core, y, z)
                    if target is not None:
                        out.append((place(x, core, y, z), place(*target)))
    return out


def along(axis, step):
    def move(x, core, y, z, flip):
        at = [x, y, z]
        at["xyz".index(axis)] ^= flip
        return at[0], core, at[1], at[2]

    return pairs(lambda x, core, y, z: move(x, core, y, z, 1 if core == step else 3))


OTHER_CORE = pairs(lambda x, core, y, z: (x, 1 - core, y, z))

def send(value, route):
    return lax.ppermute(value, AXES, route)


def together(*values):
    return lax.optimization_barrier(values)


def masked(values, block_mask, row_index, col_index):
    row_blocks, col_blocks = values.shape[0] // BS, values.shape[1] // BS
    tile_mask = lax.dynamic_slice(
        block_mask, (row_index * row_blocks, col_index * col_blocks), (row_blocks, col_blocks)
    ).astype(values.dtype)
    shaped = values.reshape(row_blocks, BS, col_blocks, BS)
    return (shaped * tile_mask[:, None, :, None]).reshape(values.shape)


def offset(core, g):
    return (0, 1 + 2 * core, 3 - 2 * core, 2)[g]


def source(idx, first, h, g):
    dy, dz = (h, g) if first == 0 else (g, h)
    return idx[2] ^ offset(idx[1], dy), idx[3] ^ offset(idx[1], dz)


def piece_scale(mask, row_block, col_block, rows, dtype):
    first_lanes = lax.broadcasted_iota(jnp.int32, (BS, 2 * BS), 1) < BS
    scales = []
    for i in range(rows):
        at = (row_block + i) * NB + col_block
        scales.append(jnp.where(first_lanes, mask[at].astype(F32), mask[at + 1].astype(F32)).astype(dtype))
    return jnp.concatenate(scales, axis=0)


def group_left(idx, mask, ref, first, h, row_block):
    lefts = []
    for g in range(RING):
        ys, zs = source(idx, first, h, g)
        scale = piece_scale(mask, row_block, (ys * RING + zs) * 2, 2, BF16)
        lefts.append(ref[h % 2 * RING + g] * scale)
    return jnp.concatenate(lefts, axis=1)


def group_right(idx, panel, first, h, *lead):
    rights = []
    for g in range(RING):
        ys, zs = source(idx, first, h, g)
        half_rows = pl.multiple_of((zs & 1) * 2 * BS, 2 * BS)
        rights.append(panel[((ys * RING + zs) // 2, *lead, pl.ds(half_rows, 2 * BS))])
    return jnp.concatenate(rights, axis=0)


def response_kernel(part, idx, mask, *refs):
    t_refs, c_own, c_other = refs[:4], refs[4], refs[5]
    before, out, panel = (None, *refs[6:]) if part == 0 else refs[6:]
    x, core, row = idx[0], idx[1], idx[4]
    for g in range(RING):
        panel[(x ^ offset(core, g)) * 2 + core] = c_own[g]
        panel[(x ^ offset(1 - core, g)) * 2 + 1 - core] = c_other[g]
    for v in range(2):
        rights = [group_right(idx, panel, v, 2 * part + h) for h in range(2)]
        for half in range(2):
            rows = pl.ds(half * 2 * BS, 2 * BS)
            total = jnp.zeros((2 * BS, 2 * BS), F32) if part == 0 else before[v, rows]
            for h in range(2):
                left = group_left(idx, mask, t_refs[2 * half + v], v, 2 * part + h, row * 4 + half * 2)
                total += jnp.dot(left, rights[h], preferred_element_type=F32)
            out[v, rows] = total.astype(out.dtype)


def density_kernel(idx, mask, mask_v, starts, *refs):
    v_refs, r_refs = refs[:4], refs[4:10]
    orb_hbm, near_hbm, far_hbm, k_out, d_out, r_panel, orb, partner, dens, sems = refs[10:]
    x, core, row, col = idx[0], idx[1], idx[4], idx[5]
    copies = [
        pltpu.make_async_copy(orb_hbm, orb, sems.at[0]),
        pltpu.make_async_copy(near_hbm, partner.at[core], sems.at[1]),
        pltpu.make_async_copy(far_hbm, partner.at[1 - core], sems.at[2]),
    ]
    for copy in copies:
        copy.start()
    for side in range(2):
        own = core ^ side
        first, second, rest = r_refs[3 * side:3 * side + 3]
        r_panel[x * 2 + own] = first[...]
        r_panel[(x ^ offset(own, 1)) * 2 + own] = second[...]
        r_panel[(x ^ offset(own, 2)) * 2 + own] = rest[0]
        r_panel[(x ^ offset(own, 3)) * 2 + own] = rest[1]
    for half in range(2):
        totals = [jnp.zeros((2 * BS, 2 * BS), F32) for _ in range(2)]
        for h in range(RING):
            left = group_left(idx, mask_v, v_refs[half * 2 + h // 2], half, h, row * 4 + half * 2)
            for v in range(2):
                totals[v] += jnp.dot(left, group_right(idx, r_panel, half, h, v), preferred_element_type=F32)
        scale = piece_scale(mask, row * 4 + half * 2, col * 2, 2, F32)
        for v in range(2):
            k_out[v, half * 2 * BS:(half + 1) * 2 * BS, :] = (totals[v] * scale).astype(BF16)
    dens[...] = jnp.zeros_like(dens)
    for copy in copies:
        copy.wait()
    starts_j = [starts[col * 2 + j] for j in range(2)]
    for i in range(4):
        left = jnp.concatenate([k_out[v, i * BS:(i + 1) * BS, :] for v in range(2)], axis=0)
        start_i = starts[row * 4 + i]

        def slab(s, carry, left=left, start_i=start_i, i=i):
            offsets = [start_i + s - starts_j[j] for j in range(2)]
            inside = [(o >= 0) & (o < SPAN) for o in offsets]

            @pl.when(inside[0] | inside[1])
            def _():
                frames = []
                for j in range(2):
                    at = pl.multiple_of(jnp.clip(offsets[j], 0, SPAN - 1) * SP, SP)
                    frame = partner[j, :, pl.ds(at, SP)]
                    frames.append(frame * jnp.where(inside[j], 1.0, 0.0).astype(BF16))
                applied = jnp.dot(left, jnp.concatenate(frames, axis=0), preferred_element_type=F32)
                own = orb[i, :, pl.ds(pl.multiple_of(s * SP, SP), SP)].astype(F32)
                for v in range(2):
                    terms = jnp.sum(own * applied[v * BS:(v + 1) * BS], axis=0, keepdims=True)
                    dens[pl.ds(start_i + s, 1), v * SP:(v + 1) * SP] += terms

            return carry

        lax.fori_loop(0, SPAN, slab, 0)
    d_out[...] = dens[...]


SMEM = pl.BlockSpec(memory_space=pltpu.SMEM)
VMEM = pl.BlockSpec(memory_space=pltpu.VMEM)
ANY = pl.BlockSpec(memory_space=pl.ANY)


def local(p_valence, p_conduction, trial_vectors, mask_valence, mask_conduction, mask_trial, orbitals, sphere_starts):
    row, col = lax.axis_index("row"), lax.axis_index("col")
    x, core, y, z = row // 2, row % 2, col // RING, col % RING
    idx = jnp.stack([x, core, y, z, row, col]).astype(jnp.int32)
    mask_flat = mask_trial.reshape(-1)

    first = 2 * (col % 2)
    mine = lax.dynamic_slice_in_dim(orbitals, first + core, 1, 0)[0]
    theirs = lax.dynamic_slice_in_dim(orbitals, first + 1 - core, 1, 0)[0]

    by_z = jnp.concatenate([trial_vectors[0], p_valence[:2 * BS]])[None]
    by_y = jnp.concatenate([trial_vectors[1], p_valence[2 * BS:]])[None]
    by_x = masked(p_conduction, mask_conduction, row, col)[None]
    for step in range(2):
        outs = [send(by_z, along("z", step)), send(by_y, along("y", step)), send(by_x, along("x", step))]
        if step == 0:
            outs.append(send(theirs, OTHER_CORE))
        outs = together(*outs)
        if step == 0:
            given = outs[3]
        else:
            outs = together(*outs, given)
            given = outs[3]
        by_z, by_y, by_x = (jnp.concatenate(both) for both in zip((by_z, by_y, by_x), outs))
    seed = jnp.where(core == z // 2, mine, given)

    def across_plane(lo, hi):
        held = [by_z[:, lo:hi], by_y[:, lo:hi]]
        got = [send(held[0], along("y", 0)), send(held[1], along("z", 0))]
        near = [jnp.concatenate(both) for both in zip(held, got)]
        return near, [send(near[0], along("y", 1)), send(near[1], along("z", 1))]

    c_other = send(by_x, OTHER_CORE)
    upper, lower = across_plane(0, 2 * BS), across_plane(2 * BS, 4 * BS)
    reached = send(seed, along("x", 0))
    passed = jnp.where(x == y, seed, reached)

    response = None
    for part in range(2):
        last = part == 1
        response = pl.pallas_call(
            functools.partial(response_kernel, part),
            name="response",
            out_shape=jax.ShapeDtypeStruct((2, 4 * BS, 2 * BS), BF16 if last else F32),
            in_specs=[SMEM, SMEM] + [VMEM] * (7 if last else 6),
            out_specs=VMEM,
            scratch_shapes=[pltpu.VMEM((8, 4 * BS, 2 * BS), BF16)],
            compiler_params=pltpu.CompilerParams(vmem_limit_bytes=32 * 2**20),
            cost_estimate=pl.CostEstimate(flops=2**31, bytes_accessed=7 * 2**20, transcendentals=0),
        )(idx, mask_flat, *upper[part], *lower[part], by_x, c_other, *([response] if last else []))

    held, got, *upper_far = together(by_z[:, 4 * BS:], by_y[:, 4 * BS:], *upper[1])
    spread_out = send(passed, along("x", 1))
    outs = together(
        send(held, along("y", 0)),
        send(got, along("z", 0)),
        send(response, along("x", 0)),
        send(response, OTHER_CORE),
    )
    valence_0, valence_1 = jnp.concatenate([held, outs[0]]), jnp.concatenate([got, outs[1]])
    second, r_swapped = outs[2], outs[3]
    rest = send(jnp.stack([response, second]), along("x", 1))
    second_swapped = send(second, OTHER_CORE)
    valence_0_far, valence_1_far = send(valence_0, along("y", 1)), send(valence_1, along("z", 1))
    flip = 1 + 2 * core
    near = jnp.where((x == y) | (x ^ flip == y), passed, spread_out)
    far = send(near, OTHER_CORE)
    rest_swapped = send(rest, OTHER_CORE)
    valences = [valence_0, valence_0_far, valence_1, valence_1_far]
    responses = [response, second, rest, r_swapped, second_swapped, rest_swapped]

    kernel, density = pl.pallas_call(
        density_kernel,
        name="density",
        out_shape=(
            jax.ShapeDtypeStruct((2, 4 * BS, 2 * BS), BF16),
            jax.ShapeDtypeStruct((NSLAB, 2 * SP), F32),
        ),
        in_specs=[SMEM] * 4 + [VMEM] * 10 + [ANY] * 3,
        out_specs=(VMEM, VMEM),
        scratch_shapes=[
            pltpu.VMEM((8, 2, 4 * BS, 2 * BS), BF16),
            pltpu.VMEM((4, BS, SPAN * SP), BF16),
            pltpu.VMEM((2, BS, SPAN * SP), BF16),
            pltpu.VMEM((NSLAB, 2 * SP), F32),
            pltpu.SemaphoreType.DMA((3,)),
        ],
        compiler_params=pltpu.CompilerParams(vmem_limit_bytes=48 * 2**20),
        cost_estimate=pl.CostEstimate(flops=2**33, bytes_accessed=22 * 2**20, transcendentals=0),
    )(idx, mask_flat, mask_valence.reshape(-1), sphere_starts, *valences, *responses, orbitals, near, far)

    terms = lax.all_to_all(density, AXES, 0, 0, tiled=True)
    return kernel, jnp.sum(terms, axis=0).reshape(2, SP)


def solution(mesh):
    placed = (
        P("row", "col"),
        P("row", "col"),
        P(None, "row", "col"),
        P(),
        P(),
        P(),
        P("row", None, None),
        P(),
    )
    return jax.shard_map(
        local,
        mesh=mesh,
        in_specs=placed,
        out_specs=(P(None, "row", "col"), P(None, AXES)),
        check_vma=False,
    )
```

time: 247 us -> 178 us (0.72)
  starting transfers between devices: 111 us -> 30.7 us
  other arithmetic: 12.8 us -> 26.2 us
  waiting for transfers between devices: 65.9 us -> 60.2 us
    ppermute x43 -> x28, starting transfers between devices: 111 us -> 30.7 us  [send(): return lax.ppermute(value, AXES, route)]
    concatenate x1 -> x9, other arithmetic: 0.19 us -> 14.5 us  [the longest x5 7.88 us: local(): jnp.concatenate(both)]
    another operation x5 -> x1, other arithmetic: 5.99 us -> 0.1 us  [local(): rest = send(jnp.stack([response, second]), along('x', 1))]
    ppermute x43 -> x28, waiting for transfers between devices: 65.9 us -> 60.2 us  [send(): return lax.ppermute(value, AXES, route)]
    select_n x2, other arithmetic: 1.82 us -> 6.28 us  [the longest x1 3.14 us: local(): near = jnp.where((x == y) | (x ^ flip == y), passed, spread_out)]
    unnamed x52 -> x32, local copies, waits for them, and re-layouts: 6.51 us -> 5.29 us
    pallas_call x1 -> x2, Pallas kernels: 5.58 us -> 6.6 us  [local(): pl.pallas_call(functools.partial(response_kernel, part), name='response',...]
  transfers between devices with their start and end apart: 43 -> 28, of which waited for: 23 -> 12; matrix products, arithmetic and copies ran while one was open for 5% -> 15% of each run, Pallas kernels for 2% -> 4%
where the time goes in v2:
time: 178 us
  waiting for transfers between devices  60.2 us (34%)
  starting transfers between devices  30.7 us (17%)
  other arithmetic  26.2 us (15%)
  blocking collectives  24.4 us (14%)
  Pallas kernels  22.4 us (13%)
  local copies, waits for them, and re-layouts  13.2 us (7%)
    ppermute x28, waiting for transfers between devices, send(): return lax.ppermute(value, AXES, route)  60.2 us
    ppermute x28, starting transfers between devices, send(): return lax.ppermute(value, AXES, route)  30.7 us
    all_to_all x1, blocking collectives, local(): terms = lax.all_to_all(density, AXES, 0, 0, tiled=True)  24.4 us
    pallas_call x1, Pallas kernels, local(): pl.pallas_call(density_kernel, name='density', out_shape=(jax.ShapeDtypeS...  15.8 us
    concatenate x5, other arithmetic, local(): jnp.concatenate(both)  7.88 us
    concatenate x4, other arithmetic, across_plane(): near = [jnp.concatenate(both) for both in zip(held, got)]  6.64 us
    pallas_call x2, Pallas kernels, local(): pl.pallas_call(functools.partial(response_kernel, part), name='response',...  6.6 us
    unnamed x32, local copies, waits for them, and re-layouts  5.29 us
  transfers between devices with their start and end apart: 28, of which 12 were waited for; matrix products, arithmetic and copies ran while one was open for 15% of the time, Pallas kernels for 4%

profile of v2, /device:TPU:1, one launch (start us, length us, event | category | flops | bytes accessed | tf_op | source)
XLA Modules:
  0.0 177.9 jit_solution(10276267718671734795)
XLA Ops:
  0.7 3.2 %dynamic-slice_bitcast_fusion = bf16[128,8192]{1,0:T(8,128)(2,1)} fusion(bf16[4,128,8192]{2,1,0:T(8,128)(2,1)} %refs_10_.1, s32[]{:T(128)S(6)} %select_n.64), kind=kLoop, calls=%fused_computation.1 | loop fusion | bytes 4194308 | tf_op jit(solution)/shard_map/squeeze | solution.py:191
  5.4 3.9 %collective-permute-start = (bf16[1,768,256]{2,1,0:T(8,128)(2,1)S(1)}, bf16[1,768,256]{2,1,0:T(8,128)(2,1)}, u32[]{:S(2)}, u32[]{:S(2)}) collective-permute-start(bf16[1,768,256]{2,1,0:T(8,128)(2,1)S(1)} %maximum_bitcast_fusion), channel_id=1, source_target_pairs={{0,1},{1,0},{2,3},{3,2},{4,5},{5,4},{6,7},{7,6},{8,9},{9,8},{10,11... | collective-permute-start | bytes 1179656 | tf_op jit(solution)/shard_map/ppermute | solution.py:50
  9.4 2.8 %collective-permute-start.1 = (bf16[1,768,256]{2,1,0:T(8,128)(2,1)S(1)}, bf16[1,768,256]{2,1,0:T(8,128)(2,1)}, u32[]{:S(2)}, u32[]{:S(2)}) collective-permute-start(bf16[1,768,256]{2,1,0:T(8,128)(2,1)S(1)} %maximum_bitcast_fusion.1), channel_id=1, source_target_pairs={{0,4},{1,5},{2,6},{3,7},{4,0},{5,1},{6,2},{7,3},{8,12},{9,13},{10,... | collective-permute-start | bytes 1179656 | tf_op jit(solution)/shard_map/ppermute | solution.py:50
  14.1 2.6 %collective-permute-start.2 = (bf16[1,512,256]{2,1,0:T(8,128)(2,1)S(1)}, bf16[1,512,256]{2,1,0:T(8,128)(2,1)S(1)}, u32[]{:S(2)}, u32[]{:S(2)}) collective-permute-start(bf16[1,512,256]{2,1,0:T(8,128)(2,1)S(1)} %fusion), channel_id=1, source_target_pairs={{0,32},{1,33},{2,34},{3,35},{4,36},{5,37},{6,38},{7,39},{8,40},{9,... | collective-permute-start | bytes 786440 | tf_op jit(solution)/shard_map/ppermute | solution.py:50
  16.7 4.0 %collective-permute-done.2 = bf16[1,512,256]{2,1,0:T(8,128)(2,1)S(1)} collective-permute-done((bf16[1,512,256]{2,1,0:T(8,128)(2,1)S(1)}, bf16[1,512,256]{2,1,0:T(8,128)(2,1)S(1)}, u32[]{:S(2)}, u32[]{:S(2)}) %collective-permute-start.2) | collective-permute-done | bytes 262176 | tf_op jit(solution)/shard_map/ppermute | solution.py:50
  25.5 8.6 %collective-permute-done.6 = bf16[2,512,256]{2,1,0:T(8,128)(2,1)} collective-permute-done((bf16[2,512,256]{2,1,0:T(8,128)(2,1)}, bf16[2,512,256]{2,1,0:T(8,128)(2,1)}, u32[]{:S(2)}, u32[]{:S(2)}) %collective-permute-start.6) | collective-permute-done | bytes 524320 | tf_op jit(solution)/shard_map/ppermute | solution.py:50
  36.1 3.1 %bitcast_select_fusion = bf16[128,8192]{1,0:T(8,128)(2,1)} fusion(bf16[128,8192]{1,0:T(8,128)(2,1)S(1)} %collective-permute-done.3, bf16[4,128,8192]{2,1,0:T(8,128)(2,1)} %refs_10_.1, s32[]{:T(128)S(6)} %select_n.69, pred[]{:T(512)S(6)} %eq.16), kind=kLoop, calls=%fused_computation | loop fusion | flops 1048576 | bytes 6291461 | tf_op jit(solution)/shard_map/jit(_where)/select_n | solution.py:207
  46.5 2.7 %collective-permute-start.9 = (bf16[4,256,256]{2,1,0:T(8,128)(2,1)}, bf16[4,256,256]{2,1,0:T(8,128)(2,1)S(1)}, u32[]{:S(2)}, u32[]{:S(2)}) collective-permute-start(bf16[4,256,256]{2,1,0:T(8,128)(2,1)} %get-tuple-element.41), channel_id=1, source_target_pairs={{0,1},{1,0},{2,3},{3,2},{4,5},{5,4},{6,7},{7,6},{8,9},{9,8},{10,11... | collective-permute-start | bytes 1572872 | tf_op jit(solution)/shard_map/ppermute | solution.py:50
  50.4 3.7 %collective-permute-done.15 = bf16[4,256,256]{2,1,0:T(8,128)(2,1)} collective-permute-done((bf16[4,256,256]{2,1,0:T(8,128)(2,1)S(1)}, bf16[4,256,256]{2,1,0:T(8,128)(2,1)}, u32[]{:S(2)}, u32[]{:S(2)}) %collective-permute-start.15) | collective-permute-done | bytes 524320 | tf_op jit(solution)/shard_map/ppermute | solution.py:50
  57.3 8.7 %collective-permute-done.25 = bf16[128,8192]{1,0:T(8,128)(2,1)} collective-permute-done((bf16[128,8192]{1,0:T(8,128)(2,1)}, bf16[128,8192]{1,0:T(8,128)(2,1)}, u32[]{:S(2)}, u32[]{:S(2)}) %collective-permute-start.25) | collective-permute-done | bytes 2097184 | tf_op jit(solution)/shard_map/ppermute | solution.py:50
  67.4 3.1 %broadcast_select_fusion = bf16[128,8192]{1,0:T(8,128)(2,1)} fusion(bf16[128,8192]{1,0:T(8,128)(2,1)} %bitcast_select_fusion, bf16[128,8192]{1,0:T(8,128)(2,1)} %collective-permute-done.25, pred[]{:T(512)S(6)} %eq.14), kind=kLoop, calls=%fused_computation.2 | loop fusion | flops 1048576 | bytes 6291457 | tf_op jit(solution)/shard_map/jit(_where)/select_n | solution.py:218
  77.2 3.0 %response.2.refs_6_ = f32[2,512,256]{2,1,0:T(8,128)S(1)} custom-call(s32[6]{0:T(128)S(1)} %stack.36.idx, s32[1024]{0:T(1024)S(1)} %reshape.23.mask, bf16[8,256,256]{2,1,0:T(8,128)(2,1)} %pad_maximum_fusion.2.refs_0_, bf16[8,256,256]{2,1,0:T(8,128)(2,1)} %pad_maximum_fusion.3.refs_1_, bf16[8,256,256]{2,1,0:T(8,128)(2,1)S(1)} %pad_maximum_fusion.4.refs_2_, ...), custom_call_target="tpu_custom_call" | custom-call | flops 2147483648 | bytes 7340032 | tf_op jit(solution)/shard_map/response/pallas_call | solution.py:223
  80.2 6.7 %collective-permute-done.10.refs_1_ = bf16[8,256,256]{2,1,0:T(8,128)(2,1)} collective-permute-done((bf16[8,256,256]{2,1,0:T(8,128)(2,1)}, bf16[8,256,256]{2,1,0:T(8,128)(2,1)}, u32[]{:S(2)}, u32[]{:S(2)}) %collective-permute-start.10) | collective-permute-done | bytes 1048608 | tf_op jit(solution)/shard_map/ppermute | solution.py:50
  87.0 4.3 %collective-permute-done.8.refs_0_ = bf16[8,256,256]{2,1,0:T(8,128)(2,1)} collective-permute-done((bf16[8,256,256]{2,1,0:T(8,128)(2,1)}, bf16[8,256,256]{2,1,0:T(8,128)(2,1)}, u32[]{:S(2)}, u32[]{:S(2)}) %collective-permute-start.8) | collective-permute-done | bytes 1048608 | tf_op jit(solution)/shard_map/ppermute | solution.py:50
  91.3 3.6 %response.3.refs_4_ = bf16[2,512,256]{2,1,0:T(8,128)(2,1)S(1)} custom-call(s32[6]{0:T(128)S(1)} %stack.36.idx, s32[1024]{0:T(1024)S(1)} %reshape.23.mask, bf16[8,256,256]{2,1,0:T(8,128)(2,1)} %collective-permute-done.8.refs_0_, bf16[8,256,256]{2,1,0:T(8,128)(2,1)} %collective-permute-done.10.refs_1_, bf16[8,256,256]{2,1,0:T(8,128)(2,1)} %collective-permute-done.14.refs_2_, ...), custom_call_target="tpu_custom_call" | custom-call | flops 2147483648 | bytes 7340032 | tf_op jit(solution)/shard_map/response/pallas_call | solution.py:223
  94.8 2.6 %collective-permute-start.18 = (bf16[2,512,256]{2,1,0:T(8,128)(2,1)S(1)}, bf16[2,512,256]{2,1,0:T(8,128)(2,1)S(1)}, u32[]{:S(2)}, u32[]{:S(2)}) collective-permute-start(bf16[2,512,256]{2,1,0:T(8,128)(2,1)S(1)} %response.3.refs_4_), channel_id=1, source_target_pairs={{0,32},{1,33},{2,34},{3,35},{4,36},{5,37},{6,38},{7,39},{8,40},{9,... | collective-permute-start | bytes 1572872 | tf_op jit(solution)/shard_map/ppermute | solution.py:50
  97.4 4.3 %collective-permute-start.19 = (bf16[2,512,256]{2,1,0:T(8,128)(2,1)S(1)}, bf16[2,512,256]{2,1,0:T(8,128)(2,1)S(1)}, u32[]{:S(2)}, u32[]{:S(2)}) collective-permute-start(bf16[2,512,256]{2,1,0:T(8,128)(2,1)S(1)} %response.3.refs_4_), channel_id=1, source_target_pairs={{0,16},{1,17},{2,18},{3,19},{4,20},{5,21},{6,22},{7,23},{8,24},{9,... | collective-permute-start | bytes 1572872 | tf_op jit(solution)/shard_map/ppermute | solution.py:50
  104.5 6.7 %collective-permute-done.11 = bf16[4,256,256]{2,1,0:T(8,128)(2,1)S(1)} collective-permute-done((bf16[4,256,256]{2,1,0:T(8,128)(2,1)}, bf16[4,256,256]{2,1,0:T(8,128)(2,1)S(1)}, u32[]{:S(2)}, u32[]{:S(2)}) %collective-permute-start.11) | collective-permute-done | bytes 524320 | tf_op jit(solution)/shard_map/ppermute | solution.py:50
  114.8 3.1 %broadcast_select_fusion.1.refs_11_ = bf16[128,8192]{1,0:T(8,128)(2,1)} fusion(bf16[128,8192]{1,0:T(8,128)(2,1)} %broadcast_select_fusion, bf16[128,8192]{1,0:T(8,128)(2,1)} %collective-permute-done.26, pred[]{:T(512)S(6)} %or.3), kind=kLoop, calls=%fused_computation.3 | loop fusion | flops 1048576 | bytes 6291457 | tf_op jit(solution)/shard_map/jit(_where)/select_n | solution.py:248
  122.1 5.3 %collective-permute-done.22.refs_6_ = bf16[2,2,512,256]{3,2,1,0:T(8,128)(2,1)} collective-permute-done((bf16[2,2,512,256]{3,2,1,0:T(8,128)(2,1)S(1)}, bf16[2,2,512,256]{3,2,1,0:T(8,128)(2,1)}, u32[]{:S(2)}, u32[]{:S(2)}) %collective-permute-start.22) | collective-permute-done | bytes 1048608 | tf_op jit(solution)/shard_map/ppermute | solution.py:50
  127.9 3.0 %collective-permute-done.23.refs_8_ = bf16[2,512,256]{2,1,0:T(8,128)(2,1)} collective-permute-done((bf16[2,512,256]{2,1,0:T(8,128)(2,1)S(1)}, bf16[2,512,256]{2,1,0:T(8,128)(2,1)}, u32[]{:S(2)}, u32[]{:S(2)}) %collective-permute-start.23) | collective-permute-done | bytes 524320 | tf_op jit(solution)/shard_map/ppermute | solution.py:50
  130.9 5.3 %collective-permute-done.21.refs_3_ = bf16[8,256,256]{2,1,0:T(8,128)(2,1)} collective-permute-done((bf16[8,256,256]{2,1,0:T(8,128)(2,1)}, bf16[8,256,256]{2,1,0:T(8,128)(2,1)}, u32[]{:S(2)}, u32[]{:S(2)}) %collective-permute-start.21) | collective-permute-done | bytes 1048608 | tf_op jit(solution)/shard_map/ppermute | solution.py:50
  136.2 15.8 %density.1 = (bf16[2,512,256]{2,1,0:T(8,128)(2,1)}, f32[128,1024]{1,0:T(8,128)S(1)}) custom-call(s32[6]{0:T(128)S(1)} %stack.36.idx, s32[1024]{0:T(1024)S(1)} %reshape.23.mask, s32[1024]{0:T(1024)S(1)} %reshape.24.mask_v, s32[32]{0:T(128)S(1)} %copy-done.3, bf16[8,256,256]{2,1,0:T(8,128)(2,1)S(1)} %constant_dynamic-update-slice_fusion.refs_0_, ...), custom_call_target="tpu_custom_call" | custom-call | flops 8589934592 | bytes 23068672 | tf_op jit(solution)/shard_map/density/pallas_call | solution.py:254
  152.6 24.4 %all_to_all.9 = f32[128,1,1024]{2,1,0:T(1,128)S(1)} all-to-all(f32[128,1,1024]{2,1,0:T(1,128)S(1)} %copy.10), channel_id=1, replica_groups=mesh['row'=8,'col'=16] {'row','col'}, dimensions={0} | all-to-all | bytes 1048576 | tf_op jit(solution)/shard_map/all_to_all | solution.py:274
  (99 shorter events, 42.5 us)
Async XLA Ops:
  3.9 16.8 %collective-permute-start.3 = (bf16[128,8192]{1,0:T(8,128)(2,1)}, bf16[128,8192]{1,0:T(8,128)(2,1)S(1)}, u32[]{:S(2)}, u32[]{:S(2)}) collective-permute-start(bf16[128,8192]{1,0:T(8,128)(2,1)} %dynamic-slice_bitcast_fusion), channel_id=1, source_target_pairs={{0,16},{1,17},{2,18},{3,19},{4,20},{5,21},{6,22},{7,23},{8,24},{9,... | collective-permute-start | bytes 6291464 | tf_op jit(solution)/shard_map/ppermute | solution.py:50
  5.4 15.2 %collective-permute-start = (bf16[1,768,256]{2,1,0:T(8,128)(2,1)S(1)}, bf16[1,768,256]{2,1,0:T(8,128)(2,1)}, u32[]{:S(2)}, u32[]{:S(2)}) collective-permute-start(bf16[1,768,256]{2,1,0:T(8,128)(2,1)S(1)} %maximum_bitcast_fusion), channel_id=1, source_target_pairs={{0,1},{1,0},{2,3},{3,2},{4,5},{5,4},{6,7},{7,6},{8,9},{9,8},{10,11... | collective-permute-start | bytes 1179656 | tf_op jit(solution)/shard_map/ppermute | solution.py:50
  9.4 11.3 %collective-permute-start.1 = (bf16[1,768,256]{2,1,0:T(8,128)(2,1)S(1)}, bf16[1,768,256]{2,1,0:T(8,128)(2,1)}, u32[]{:S(2)}, u32[]{:S(2)}) collective-permute-start(bf16[1,768,256]{2,1,0:T(8,128)(2,1)S(1)} %maximum_bitcast_fusion.1), channel_id=1, source_target_pairs={{0,4},{1,5},{2,6},{3,7},{4,0},{5,1},{6,2},{7,3},{8,12},{9,13},{10,... | collective-permute-start | bytes 1179656 | tf_op jit(solution)/shard_map/ppermute | solution.py:50
  22.7 11.5 %collective-permute-start.5 = (bf16[2,768,256]{2,1,0:T(8,128)(2,1)}, bf16[2,768,256]{2,1,0:T(8,128)(2,1)}, u32[]{:S(2)}, u32[]{:S(2)}) collective-permute-start(bf16[2,768,256]{2,1,0:T(8,128)(2,1)} %pad_maximum_fusion.9), channel_id=1, source_target_pairs={{0,12},{1,13},{2,14},{3,15},{4,8},{5,9},{6,10},{7,11},{8,4},{9,5},... | collective-permute-start | bytes 2359304 | tf_op jit(solution)/shard_map/ppermute | solution.py:50
  24.7 11.5 %collective-permute-start.4 = (bf16[2,768,256]{2,1,0:T(8,128)(2,1)}, bf16[2,768,256]{2,1,0:T(8,128)(2,1)}, u32[]{:S(2)}, u32[]{:S(2)}) collective-permute-start(bf16[2,768,256]{2,1,0:T(8,128)(2,1)} %pad_maximum_fusion.8), channel_id=1, source_target_pairs={{0,3},{1,2},{2,1},{3,0},{4,7},{5,6},{6,5},{7,4},{8,11},{9,10},{10,... | collective-permute-start | bytes 2359304 | tf_op jit(solution)/shard_map/ppermute | solution.py:50
  39.3 26.7 %collective-permute-start.25 = (bf16[128,8192]{1,0:T(8,128)(2,1)}, bf16[128,8192]{1,0:T(8,128)(2,1)}, u32[]{:S(2)}, u32[]{:S(2)}) collective-permute-start(bf16[128,8192]{1,0:T(8,128)(2,1)} %bitcast_select_fusion), channel_id=1, source_target_pairs={{0,32},{1,33},{2,34},{3,35},{4,36},{5,37},{6,38},{7,39},{8,40},{9,... | collective-permute-start | bytes 6291464 | tf_op jit(solution)/shard_map/ppermute | solution.py:50
  44.7 9.3 %collective-permute-start.15 = (bf16[4,256,256]{2,1,0:T(8,128)(2,1)S(1)}, bf16[4,256,256]{2,1,0:T(8,128)(2,1)}, u32[]{:S(2)}, u32[]{:S(2)}) collective-permute-start(bf16[4,256,256]{2,1,0:T(8,128)(2,1)S(1)} %get-tuple-element.40), channel_id=1, source_target_pairs={{0,1},{1,0},{2,3},{3,2},{4,5},{5,4},{6,7},{7,6},{8,9},{9,8},{10,11... | collective-permute-start | bytes 1572872 | tf_op jit(solution)/shard_map/ppermute | solution.py:50
  45.8 10.0 %collective-permute-start.13 = (bf16[4,256,256]{2,1,0:T(8,128)(2,1)S(1)}, bf16[4,256,256]{2,1,0:T(8,128)(2,1)}, u32[]{:S(2)}, u32[]{:S(2)}) collective-permute-start(bf16[4,256,256]{2,1,0:T(8,128)(2,1)S(1)} %get-tuple-element.43), channel_id=1, source_target_pairs={{0,4},{1,5},{2,6},{3,7},{4,0},{5,1},{6,2},{7,3},{8,12},{9,13},{10,... | collective-permute-start | bytes 1572872 | tf_op jit(solution)/shard_map/ppermute | solution.py:50
  46.5 24.1 %collective-permute-start.9 = (bf16[4,256,256]{2,1,0:T(8,128)(2,1)}, bf16[4,256,256]{2,1,0:T(8,128)(2,1)S(1)}, u32[]{:S(2)}, u32[]{:S(2)}) collective-permute-start(bf16[4,256,256]{2,1,0:T(8,128)(2,1)} %get-tuple-element.41), channel_id=1, source_target_pairs={{0,1},{1,0},{2,3},{3,2},{4,5},{5,4},{6,7},{7,6},{8,9},{9,8},{10,11... | collective-permute-start | bytes 1572872 | tf_op jit(solution)/shard_map/ppermute | solution.py:50
  50.3 24.5 %collective-permute-start.17 = (bf16[4,512,256]{2,1,0:T(8,128)(2,1)S(1)}, bf16[4,512,256]{2,1,0:T(8,128)(2,1)S(1)}, u32[]{:S(2)}, u32[]{:S(2)}) collective-permute-start(bf16[4,512,256]{2,1,0:T(8,128)(2,1)S(1)} %pad_maximum_fusion.6.refs_4_), channel_id=1, source_target_pairs={{0,16},{1,17},{2,18},{3,19},{4,20},{5,21},{6,22},{7,23},{8,24},{9,... | collective-permute-start | bytes 3145736 | tf_op jit(solution)/shard_map/ppermute | solution.py:50
  54.1 18.6 %collective-permute-start.7 = (bf16[4,256,256]{2,1,0:T(8,128)(2,1)}, bf16[4,256,256]{2,1,0:T(8,128)(2,1)S(1)}, u32[]{:S(2)}, u32[]{:S(2)}) collective-permute-start(bf16[4,256,256]{2,1,0:T(8,128)(2,1)} %get-tuple-element.44), channel_id=1, source_target_pairs={{0,4},{1,5},{2,6},{3,7},{4,0},{5,1},{6,2},{7,3},{8,12},{9,13},{10,... | collective-permute-start | bytes 1572872 | tf_op jit(solution)/shard_map/ppermute | solution.py:50
  55.9 24.3 %collective-permute-start.16 = (bf16[8,256,256]{2,1,0:T(8,128)(2,1)S(1)}, bf16[8,256,256]{2,1,0:T(8,128)(2,1)}, u32[]{:S(2)}, u32[]{:S(2)}) collective-permute-start(bf16[8,256,256]{2,1,0:T(8,128)(2,1)S(1)} %pad_maximum_fusion.5.refs_3_), channel_id=1, source_target_pairs={{0,3},{1,2},{2,1},{3,0},{4,7},{5,6},{6,5},{7,4},{8,11},{9,10},{10,... | collective-permute-start | bytes 3145736 | tf_op jit(solution)/shard_map/ppermute | solution.py:50
  66.0 14.2 %collective-permute-start.14 = (bf16[8,256,256]{2,1,0:T(8,128)(2,1)S(1)}, bf16[8,256,256]{2,1,0:T(8,128)(2,1)}, u32[]{:S(2)}, u32[]{:S(2)}) collective-permute-start(bf16[8,256,256]{2,1,0:T(8,128)(2,1)S(1)} %pad_maximum_fusion.4.refs_2_), channel_id=1, source_target_pairs={{0,12},{1,13},{2,14},{3,15},{4,8},{5,9},{6,10},{7,11},{8,4},{9,5},... | collective-permute-start | bytes 3145736 | tf_op jit(solution)/shard_map/ppermute | solution.py:50
  70.6 44.2 %collective-permute-start.26 = (bf16[128,8192]{1,0:T(8,128)(2,1)}, bf16[128,8192]{1,0:T(8,128)(2,1)}, u32[]{:S(2)}, u32[]{:S(2)}) collective-permute-start(bf16[128,8192]{1,0:T(8,128)(2,1)} %broadcast_select_fusion), channel_id=1, source_target_pairs={{0,96},{1,97},{2,98},{3,99},{4,100},{5,101},{6,102},{7,103},{8,104... | collective-permute-start | bytes 6291464 | tf_op jit(solution)/shard_map/ppermute | solution.py:50
  72.7 14.3 %collective-permute-start.10 = (bf16[8,256,256]{2,1,0:T(8,128)(2,1)}, bf16[8,256,256]{2,1,0:T(8,128)(2,1)}, u32[]{:S(2)}, u32[]{:S(2)}) collective-permute-start(bf16[8,256,256]{2,1,0:T(8,128)(2,1)} %pad_maximum_fusion.3.refs_1_), channel_id=1, source_target_pairs={{0,3},{1,2},{2,1},{3,0},{4,7},{5,6},{6,5},{7,4},{8,11},{9,10},{10,... | collective-permute-start | bytes 3145736 | tf_op jit(solution)/shard_map/ppermute | solution.py:50
  75.8 15.5 %collective-permute-start.8 = (bf16[8,256,256]{2,1,0:T(8,128)(2,1)}, bf16[8,256,256]{2,1,0:T(8,128)(2,1)}, u32[]{:S(2)}, u32[]{:S(2)}) collective-permute-start(bf16[8,256,256]{2,1,0:T(8,128)(2,1)} %pad_maximum_fusion.2.refs_0_), channel_id=1, source_target_pairs={{0,12},{1,13},{2,14},{3,15},{4,8},{5,9},{6,10},{7,11},{8,4},{9,5},... | collective-permute-start | bytes 3145736 | tf_op jit(solution)/shard_map/ppermute | solution.py:50
  94.8 9.6 %collective-permute-start.18 = (bf16[2,512,256]{2,1,0:T(8,128)(2,1)S(1)}, bf16[2,512,256]{2,1,0:T(8,128)(2,1)S(1)}, u32[]{:S(2)}, u32[]{:S(2)}) collective-permute-start(bf16[2,512,256]{2,1,0:T(8,128)(2,1)S(1)} %response.3.refs_4_), channel_id=1, source_target_pairs={{0,32},{1,33},{2,34},{3,35},{4,36},{5,37},{6,38},{7,39},{8,40},{9,... | collective-permute-start | bytes 1572872 | tf_op jit(solution)/shard_map/ppermute | solution.py:50
  101.7 9.5 %collective-permute-start.11 = (bf16[4,256,256]{2,1,0:T(8,128)(2,1)}, bf16[4,256,256]{2,1,0:T(8,128)(2,1)S(1)}, u32[]{:S(2)}, u32[]{:S(2)}) collective-permute-start(bf16[4,256,256]{2,1,0:T(8,128)(2,1)} %get-tuple-element.30), channel_id=1, source_target_pairs={{0,4},{1,5},{2,6},{3,7},{4,0},{5,1},{6,2},{7,3},{8,12},{9,13},{10,... | collective-permute-start | bytes 1572872 | tf_op jit(solution)/shard_map/ppermute | solution.py:50
  103.6 9.5 %collective-permute-start.12 = (bf16[4,256,256]{2,1,0:T(8,128)(2,1)}, bf16[4,256,256]{2,1,0:T(8,128)(2,1)S(1)}, u32[]{:S(2)}, u32[]{:S(2)}) collective-permute-start(bf16[4,256,256]{2,1,0:T(8,128)(2,1)} %get-tuple-element.31), channel_id=1, source_target_pairs={{0,1},{1,0},{2,3},{3,2},{4,5},{5,4},{6,7},{7,6},{8,9},{9,8},{10,11... | collective-permute-start | bytes 1572872 | tf_op jit(solution)/shard_map/ppermute | solution.py:50
  113.1 14.2 %collective-permute-start.22 = (bf16[2,2,512,256]{3,2,1,0:T(8,128)(2,1)S(1)}, bf16[2,2,512,256]{3,2,1,0:T(8,128)(2,1)}, u32[]{:S(2)}, u32[]{:S(2)}) collective-permute-start(bf16[2,2,512,256]{3,2,1,0:T(8,128)(2,1)S(1)} %pad_maximum_fusion.7), channel_id=1, source_target_pairs={{0,96},{1,97},{2,98},{3,99},{4,100},{5,101},{6,102},{7,103},{8,104... | collective-permute-start | bytes 3145736 | tf_op jit(solution)/shard_map/ppermute | solution.py:50
  117.9 18.3 %collective-permute-start.27 = (bf16[128,8192]{1,0:T(8,128)(2,1)}, bf16[128,8192]{1,0:T(8,128)(2,1)}, u32[]{:S(2)}, u32[]{:S(2)}) collective-permute-start(bf16[128,8192]{1,0:T(8,128)(2,1)} %broadcast_select_fusion.1.refs_11_), channel_id=1, source_target_pairs={{0,16},{1,17},{2,18},{3,19},{4,20},{5,21},{6,22},{7,23},{8,24},{9,... | collective-permute-start | bytes 6291464 | tf_op jit(solution)/shard_map/ppermute | solution.py:50
  121.9 14.3 %collective-permute-start.21 = (bf16[8,256,256]{2,1,0:T(8,128)(2,1)}, bf16[8,256,256]{2,1,0:T(8,128)(2,1)}, u32[]{:S(2)}, u32[]{:S(2)}) collective-permute-start(bf16[8,256,256]{2,1,0:T(8,128)(2,1)} %constant_dynamic-update-slice_fusion.2.refs_2_), channel_id=1, source_target_pairs={{0,3},{1,2},{2,1},{3,0},{4,7},{5,6},{6,5},{7,4},{8,11},{9,10},{10,... | collective-permute-start | bytes 3145736 | tf_op jit(solution)/shard_map/ppermute | solution.py:50
  122.0 14.2 %collective-permute-start.20 = (bf16[8,256,256]{2,1,0:T(8,128)(2,1)S(1)}, bf16[8,256,256]{2,1,0:T(8,128)(2,1)}, u32[]{:S(2)}, u32[]{:S(2)}) collective-permute-start(bf16[8,256,256]{2,1,0:T(8,128)(2,1)S(1)} %constant_dynamic-update-slice_fusion.refs_0_), channel_id=1, source_target_pairs={{0,12},{1,13},{2,14},{3,15},{4,8},{5,9},{6,10},{7,11},{8,4},{9,5},... | collective-permute-start | bytes 3145736 | tf_op jit(solution)/shard_map/ppermute | solution.py:50
  127.3 8.8 %collective-permute-start.24 = (bf16[2,2,512,256]{3,2,1,0:T(8,128)(2,1)}, bf16[2,2,512,256]{3,2,1,0:T(8,128)(2,1)}, u32[]{:S(2)}, u32[]{:S(2)}) collective-permute-start(bf16[2,2,512,256]{3,2,1,0:T(8,128)(2,1)} %collective-permute-done.22.refs_6_), channel_id=1, source_target_pairs={{0,16},{1,17},{2,18},{3,19},{4,20},{5,21},{6,22},{7,23},{8,24},{9,... | collective-permute-start | bytes 3145736 | tf_op jit(solution)/shard_map/ppermute | solution.py:50
  (19 other events, 119.5 us)

commit v3 on v2

--- a/solution.py
+++ b/solution.py
@@ -14,6 +14,7 @@
 NSLAB = 128
 RING = 4
 N_COL = 16
+WIDE = 2
 BF16 = jnp.bfloat16
 F32 = jnp.float32
 AXES = ("row", "col")
@@ -119,13 +120,11 @@
 
 def density_kernel(idx, mask, mask_v, starts, *refs):
     v_refs, r_refs = refs[:4], refs[4:10]
-    orb_hbm, near_hbm, far_hbm, k_out, d_out, r_panel, orb, partner, dens, sems = refs[10:]
+    orb_hbm, near_hbm, far_hbm, k_out, dens, r_panel, orb, partner, sems = refs[10:]
     x, core, row, col = idx[0], idx[1], idx[4], idx[5]
-    copies = [
-        pltpu.make_async_copy(orb_hbm, orb, sems.at[0]),
-        pltpu.make_async_copy(near_hbm, partner.at[core], sems.at[1]),
-        pltpu.make_async_copy(far_hbm, partner.at[1 - core], sems.at[2]),
-    ]
+    copies = [(near_hbm, partner.at[core]), (far_hbm, partner.at[1 - core])]
+    copies += [(orb_hbm.at[i], orb.at[i]) for i in range(4)]
+    copies = [pltpu.make_async_copy(a, b, sems.at[k]) for k, (a, b) in enumerate(copies)]
     for copy in copies:
         copy.start()
     for side in range(2):
@@ -145,34 +144,38 @@
         for v in range(2):
             k_out[v, half * 2 * BS:(half + 1) * 2 * BS, :] = (totals[v] * scale).astype(BF16)
     dens[...] = jnp.zeros_like(dens)
-    for copy in copies:
-        copy.wait()
+    copies[0].wait()
+    copies[1].wait()
     starts_j = [starts[col * 2 + j] for j in range(2)]
     for i in range(4):
+        copies[2 + i].wait()
         left = jnp.concatenate([k_out[v, i * BS:(i + 1) * BS, :] for v in range(2)], axis=0)
         start_i = starts[row * 4 + i]
 
-        def slab(s, carry, left=left, start_i=start_i, i=i):
-            offsets = [start_i + s - starts_j[j] for j in range(2)]
-            inside = [(o >= 0) & (o < SPAN) for o in offsets]
-
-            @pl.when(inside[0] | inside[1])
+        def slabs(step, carry, left=left, start_i=start_i, i=i):
+            begin = step * WIDE
+            offsets = [start_i + begin - starts_j[j] for j in range(2)]
+            touched = [(o > -WIDE) & (o < SPAN) for o in offsets]
+
+            @pl.when(touched[0] | touched[1])
             def _():
-                frames = []
-                for j in range(2):
-                    at = pl.multiple_of(jnp.clip(offsets[j], 0, SPAN - 1) * SP, SP)
-                    frame = partner[j, :, pl.ds(at, SP)]
-                    frames.append(frame * jnp.where(inside[j], 1.0, 0.0).astype(BF16))
-                applied = jnp.dot(left, jnp.concatenate(frames, axis=0), preferred_element_type=F32)
-                own = orb[i, :, pl.ds(pl.multiple_of(s * SP, SP), SP)].astype(F32)
-                for v in range(2):
-                    terms = jnp.sum(own * applied[v * BS:(v + 1) * BS], axis=0, keepdims=True)
-                    dens[pl.ds(start_i + s, 1), v * SP:(v + 1) * SP] += terms
+                for k in range(WIDE):
+                    frames = []
+                    for j in range(2):
+                        o = offsets[j] + k
+                        at = pl.multiple_of(jnp.clip(o, 0, SPAN - 1) * SP, SP)
+                        inside = jnp.where((o >= 0) & (o < SPAN), 1.0, 0.0).astype(BF16)
+                        frames.append(partner[j, :, pl.ds(at, SP)] * inside)
+                    applied = jnp.dot(left, jnp.concatenate(frames, axis=0), preferred_element_type=F32)
+                    own = orb[i, :, pl.ds(pl.multiple_of((begin + k) * SP, SP), SP)].astype(F32)
+                    for v in range(2):
+                        terms = jnp.sum(own * applied[v * BS:(v + 1) * BS], axis=0, keepdims=True)
+                        for q in range(4):
+                            dens[start_i + begin + k, pl.ds(v * 4 + q, 1), :] += terms[:, q * BS:(q + 1) * BS]
 
             return carry
 
-        lax.fori_loop(0, SPAN, slab, 0)
-    d_out[...] = dens[...]
+        lax.fori_loop(0, SPAN // WIDE, slabs, 0)
 
 
 SMEM = pl.BlockSpec(memory_space=pltpu.SMEM)
@@ -187,39 +190,42 @@
     mask_flat = mask_trial.reshape(-1)
 
     first = 2 * (col % 2)
-    mine = lax.dynamic_slice_in_dim(orbitals, first + core, 1, 0)[0]
     theirs = lax.dynamic_slice_in_dim(orbitals, first + 1 - core, 1, 0)[0]
-
     by_z = jnp.concatenate([trial_vectors[0], p_valence[:2 * BS]])[None]
     by_y = jnp.concatenate([trial_vectors[1], p_valence[2 * BS:]])[None]
     by_x = masked(p_conduction, mask_conduction, row, col)[None]
-    for step in range(2):
-        outs = [send(by_z, along("z", step)), send(by_y, along("y", step)), send(by_x, along("x", step))]
-        if step == 0:
-            outs.append(send(theirs, OTHER_CORE))
-        outs = together(*outs)
-        if step == 0:
-            given = outs[3]
-        else:
-            outs = together(*outs, given)
-            given = outs[3]
-        by_z, by_y, by_x = (jnp.concatenate(both) for both in zip((by_z, by_y, by_x), outs))
+    z_got, y_got, x_got, given, first = together(
+        send(by_z, along("z", 0)), send(by_y, along("y", 0)), send(by_x, along("x", 0)), send(theirs, OTHER_CORE), first
+    )
+    by_z, by_y, by_x = (jnp.concatenate(both) for both in ((by_z, z_got), (by_y, y_got), (by_x, x_got)))
+    z_got, y_got, x_got, given, first = together(
+        send(by_z, along("z", 1)), send(by_y, along("y", 1)), send(by_x, along("x", 1)), given, first
+    )
+    by_z, by_y, by_x = (jnp.concatenate(both) for both in ((by_z, z_got), (by_y, y_got), (by_x, x_got)))
+    mine = lax.dynamic_slice_in_dim(orbitals, first + core, 1, 0)[0]
     seed = jnp.where(core == z // 2, mine, given)
 
-    def across_plane(lo, hi):
-        held = [by_z[:, lo:hi], by_y[:, lo:hi]]
-        got = [send(held[0], along("y", 0)), send(held[1], along("z", 0))]
+    upper, lower = [by_z[:, :2 * BS], by_y[:, :2 * BS]], [by_z[:, 2 * BS:4 * BS], by_y[:, 2 * BS:4 * BS]]
+
+    def first_step(held):
+        return [send(held[0], along("y", 0)), send(held[1], along("z", 0))]
+
+    def second_step(held, got):
         near = [jnp.concatenate(both) for both in zip(held, got)]
         return near, [send(near[0], along("y", 1)), send(near[1], along("z", 1))]
 
+    upper = second_step(upper, first_step(upper))
+    *lower_got, reached, by_x = together(*first_step(lower), send(seed, along("x", 0)), by_x)
+    lower = second_step(lower, lower_got)
     c_other = send(by_x, OTHER_CORE)
-    upper, lower = across_plane(0, 2 * BS), across_plane(2 * BS, 4 * BS)
-    reached = send(seed, along("x", 0))
     passed = jnp.where(x == y, seed, reached)
+    arrived = send(passed, along("x", 1))
 
     response = None
     for part in range(2):
         last = part == 1
+        if last:
+            by_z, by_y, upper[1][0], upper[1][1] = together(by_z, by_y, *upper[1])
         response = pl.pallas_call(
             functools.partial(response_kernel, part),
             name="response",
@@ -231,8 +237,7 @@
             cost_estimate=pl.CostEstimate(flops=2**31, bytes_accessed=7 * 2**20, transcendentals=0),
         )(idx, mask_flat, *upper[part], *lower[part], by_x, c_other, *([response] if last else []))
 
-    held, got, *upper_far = together(by_z[:, 4 * BS:], by_y[:, 4 * BS:], *upper[1])
-    spread_out = send(passed, along("x", 1))
+    held, got = by_z[:, 4 * BS:], by_y[:, 4 * BS:]
     outs = together(
         send(held, along("y", 0)),
         send(got, along("z", 0)),
@@ -245,7 +250,8 @@
     second_swapped = send(second, OTHER_CORE)
     valence_0_far, valence_1_far = send(valence_0, along("y", 1)), send(valence_1, along("z", 1))
     flip = 1 + 2 * core
-    near = jnp.where((x == y) | (x ^ flip == y), passed, spread_out)
+    arrived, second = together(arrived, second)
+    near = jnp.where((x == y) | (x ^ flip == y), passed, arrived)
     far = send(near, OTHER_CORE)
     rest_swapped = send(rest, OTHER_CORE)
     valences = [valence_0, valence_0_far, valence_1, valence_1_far]
@@ -256,7 +262,7 @@
         name="density",
         out_shape=(
             jax.ShapeDtypeStruct((2, 4 * BS, 2 * BS), BF16),
-            jax.ShapeDtypeStruct((NSLAB, 2 * SP), F32),
+            jax.ShapeDtypeStruct((NSLAB, 8, BS), F32),
         ),
         in_specs=[SMEM] * 4 + [VMEM] * 10 + [ANY] * 3,
         out_specs=(VMEM, VMEM),
@@ -264,8 +270,7 @@
             pltpu.VMEM((8, 2, 4 * BS, 2 * BS), BF16),
             pltpu.VMEM((4, BS, SPAN * SP), BF16),
             pltpu.VMEM((2, BS, SPAN * SP), BF16),
-            pltpu.VMEM((NSLAB, 2 * SP), F32),
-            pltpu.SemaphoreType.DMA((3,)),
+            pltpu.SemaphoreType.DMA((6,)),
         ],
         compiler_params=pltpu.CompilerParams(vmem_limit_bytes=48 * 2**20),
         cost_estimate=pl.CostEstimate(flops=2**33, bytes_accessed=22 * 2**20, transcendentals=0),

time: 178 us -> 179 us (level)
  waiting for transfers between devices: 60.2 us -> 48.5 us
  starting transfers between devices: 30.7 us -> 40.2 us
  other arithmetic: 26.2 us -> 30.9 us
  Pallas kernels: 22.4 us -> 18.2 us
    ppermute x28, waiting for transfers between devices: 60.2 us -> 48.5 us  [send(): return lax.ppermute(value, AXES, route)]
    ppermute x28, starting transfers between devices: 30.7 us -> 40.2 us  [send(): return lax.ppermute(value, AXES, route)]
    slice x2 -> x4, local copies, waits for them, and re-layouts: 2.17 us -> 6.66 us  [the longest x2 3.73 us: local(): held, got = (by_z[:, 4 * BS:], by_y[:, 4 * BS:])]
    pallas_call x1, Pallas kernels: 15.8 us -> 11.4 us  [local(): pl.pallas_call(density_kernel, name='density', out_shape=(jax.ShapeDtypeS...]
    concatenate x4 -> x6, other arithmetic: 6.64 us -> 9.53 us  [the longest x4 6.94 us: second_step(): near = [jnp.concatenate(both) for both in zip(held, got)]]
    unnamed x32 -> x26, local copies, waits for them, and re-layouts: 5.29 us -> 3.2 us
    concatenate x5 -> x6, other arithmetic: 7.88 us -> 9.94 us  [local(): jnp.concatenate(both)]
  transfers between devices with their start and end apart: 28 -> 28, of which waited for: 12 -> 13; matrix products, arithmetic and copies ran while one was open for 15% -> 17% of each run, Pallas kernels for 4% -> 4%
where the time goes in v3:
time: 179 us; the launch traced here: 178 us
  waiting for transfers between devices  48.5 us (27%)
  starting transfers between devices  40.2 us (22%)
  other arithmetic  30.9 us (17%)
  blocking collectives  25 us (14%)
  Pallas kernels  18.2 us (10%)
  local copies, waits for them, and re-layouts  14.2 us (8%)
    ppermute x28, waiting for transfers between devices, send(): return lax.ppermute(value, AXES, route)  48.5 us
    ppermute x28, starting transfers between devices, send(): return lax.ppermute(value, AXES, route)  40.2 us
    all_to_all x1, blocking collectives, local(): terms = lax.all_to_all(density, AXES, 0, 0, tiled=True)  25 us
    pallas_call x1, Pallas kernels, local(): pl.pallas_call(density_kernel, name='density', out_shape=(jax.ShapeDtypeS...  11.4 us
    concatenate x6, other arithmetic, local(): jnp.concatenate(both)  9.94 us
    concatenate x4, other arithmetic, second_step(): near = [jnp.concatenate(both) for both in zip(held, got)]  6.94 us
    pallas_call x2, Pallas kernels, local(): pl.pallas_call(functools.partial(response_kernel, part), name='response',...  6.83 us
    slice x2, local copies, waits for them, and re-layouts, local(): held, got = (by_z[:, 4 * BS:], by_y[:, 4 * BS:])  3.73 us
  transfers between devices with their start and end apart: 28, of which 13 were waited for; matrix products, arithmetic and copies ran while one was open for 17% of the time, Pallas kernels for 4%

profile of v3, /device:TPU:1, one launch (start us, length us, event | category | flops | bytes accessed | tf_op | source)
XLA Modules:
  0.0 177.9 jit_solution(12833965850811688560)
XLA Ops:
  0.7 3.2 %dynamic-slice_bitcast_fusion = bf16[128,8192]{1,0:T(8,128)(2,1)} fusion(bf16[4,128,8192]{2,1,0:T(8,128)(2,1)} %refs_10_.1, s32[]{:T(128)S(6)} %select_n.64), kind=kLoop, calls=%fused_computation.1 | loop fusion | bytes 4194308 | tf_op jit(solution)/shard_map/squeeze | solution.py:193
  5.4 3.9 %collective-permute-start = (bf16[1,768,256]{2,1,0:T(8,128)(2,1)S(1)}, bf16[1,768,256]{2,1,0:T(8,128)(2,1)}, u32[]{:S(2)}, u32[]{:S(2)}) collective-permute-start(bf16[1,768,256]{2,1,0:T(8,128)(2,1)S(1)} %maximum_bitcast_fusion), channel_id=1, source_target_pairs={{0,1},{1,0},{2,3},{3,2},{4,5},{5,4},{6,7},{7,6},{8,9},{9,8},{10,11... | collective-permute-start | bytes 1179656 | tf_op jit(solution)/shard_map/ppermute | solution.py:51
  9.4 2.8 %collective-permute-start.1 = (bf16[1,768,256]{2,1,0:T(8,128)(2,1)S(1)}, bf16[1,768,256]{2,1,0:T(8,128)(2,1)}, u32[]{:S(2)}, u32[]{:S(2)}) collective-permute-start(bf16[1,768,256]{2,1,0:T(8,128)(2,1)S(1)} %maximum_bitcast_fusion.1), channel_id=1, source_target_pairs={{0,4},{1,5},{2,6},{3,7},{4,0},{5,1},{6,2},{7,3},{8,12},{9,13},{10,... | collective-permute-start | bytes 1179656 | tf_op jit(solution)/shard_map/ppermute | solution.py:51
  14.2 2.6 %collective-permute-start.2 = (bf16[1,512,256]{2,1,0:T(8,128)(2,1)S(1)}, bf16[1,512,256]{2,1,0:T(8,128)(2,1)S(1)}, u32[]{:S(2)}, u32[]{:S(2)}) collective-permute-start(bf16[1,512,256]{2,1,0:T(8,128)(2,1)S(1)} %fusion), channel_id=1, source_target_pairs={{0,32},{1,33},{2,34},{3,35},{4,36},{5,37},{6,38},{7,39},{8,40},{9,... | collective-permute-start | bytes 786440 | tf_op jit(solution)/shard_map/ppermute | solution.py:51
  16.7 4.0 %collective-permute-done.2 = bf16[1,512,256]{2,1,0:T(8,128)(2,1)S(1)} collective-permute-done((bf16[1,512,256]{2,1,0:T(8,128)(2,1)S(1)}, bf16[1,512,256]{2,1,0:T(8,128)(2,1)S(1)}, u32[]{:S(2)}, u32[]{:S(2)}) %collective-permute-start.2) | collective-permute-done | bytes 262176 | tf_op jit(solution)/shard_map/ppermute | solution.py:51
  25.6 8.6 %collective-permute-done.6 = bf16[2,512,256]{2,1,0:T(8,128)(2,1)} collective-permute-done((bf16[2,512,256]{2,1,0:T(8,128)(2,1)}, bf16[2,512,256]{2,1,0:T(8,128)(2,1)}, u32[]{:S(2)}, u32[]{:S(2)}) %collective-permute-start.6) | collective-permute-done | bytes 524320 | tf_op jit(solution)/shard_map/ppermute | solution.py:51
  36.2 3.1 %bitcast_select_fusion = bf16[128,8192]{1,0:T(8,128)(2,1)} fusion(bf16[128,8192]{1,0:T(8,128)(2,1)S(1)} %collective-permute-done.3, bf16[4,128,8192]{2,1,0:T(8,128)(2,1)} %refs_10_.1, s32[]{:T(128)S(6)} %select_n.67, pred[]{:T(512)S(6)} %eq.14), kind=kLoop, calls=%fused_computation | loop fusion | flops 1048576 | bytes 6291461 | tf_op jit(solution)/shard_map/jit(_where)/select_n | solution.py:206
  39.3 2.5 %collective-permute-start.15 = (bf16[128,8192]{1,0:T(8,128)(2,1)}, bf16[128,8192]{1,0:T(8,128)(2,1)}, u32[]{:S(2)}, u32[]{:S(2)}) collective-permute-start(bf16[128,8192]{1,0:T(8,128)(2,1)} %bitcast_select_fusion), channel_id=1, source_target_pairs={{0,32},{1,33},{2,34},{3,35},{4,36},{5,37},{6,38},{7,39},{8,40},{9,... | collective-permute-start | bytes 6291464 | tf_op jit(solution)/shard_map/ppermute | solution.py:51
  45.8 2.5 %pad_maximum_fusion.1 = bf16[4,768,256]{2,1,0:T(8,128)(2,1)} fusion(bf16[2,768,256]{2,1,0:T(8,128)(2,1)} %collective-permute-done.5, bf16[1,768,256]{2,1,0:T(8,128)(2,1)} %collective-permute-done.1, bf16[1,768,256]{2,1,0:T(8,128)(2,1)S(1)} %maximum_bitcast_fusion.1), kind=kLoop, calls=%fused_computation.5 | loop fusion | flops 1572864 | bytes 3145728 | tf_op jit(solution)/shard_map/concatenate | solution.py:204
  50.5 2.7 %collective-permute-start.14 = (bf16[4,256,256]{2,1,0:T(8,128)(2,1)}, bf16[4,256,256]{2,1,0:T(8,128)(2,1)}, u32[]{:S(2)}, u32[]{:S(2)}) collective-permute-start(bf16[4,256,256]{2,1,0:T(8,128)(2,1)} %get-tuple-element.54), channel_id=1, source_target_pairs={{0,1},{1,0},{2,3},{3,2},{4,5},{5,4},{6,7},{7,6},{8,9},{9,8},{10,11... | collective-permute-start | bytes 1572872 | tf_op jit(solution)/shard_map/ppermute | solution.py:51
  61.2 4.4 %collective-permute-done.14 = bf16[4,256,256]{2,1,0:T(8,128)(2,1)} collective-permute-done((bf16[4,256,256]{2,1,0:T(8,128)(2,1)}, bf16[4,256,256]{2,1,0:T(8,128)(2,1)}, u32[]{:S(2)}, u32[]{:S(2)}) %collective-permute-start.14) | collective-permute-done | bytes 524320 | tf_op jit(solution)/shard_map/ppermute | solution.py:51
  67.4 3.1 %broadcast_select_fusion.1 = bf16[128,8192]{1,0:T(8,128)(2,1)} fusion(bf16[128,8192]{1,0:T(8,128)(2,1)} %bitcast_select_fusion, bf16[128,8192]{1,0:T(8,128)(2,1)} %collective-permute-done.15, pred[]{:T(512)S(6)} %eq.15), kind=kLoop, calls=%fused_computation.3 | loop fusion | flops 1048576 | bytes 6291457 | tf_op jit(solution)/shard_map/jit(_where)/select_n | solution.py:221
  72.8 2.3 %pad_maximum_fusion.6.refs_3_ = bf16[8,256,256]{2,1,0:T(8,128)(2,1)} fusion(bf16[4,256,256]{2,1,0:T(8,128)(2,1)} %collective-permute-done.14, bf16[4,256,256]{2,1,0:T(8,128)(2,1)} %get-tuple-element.54), kind=kLoop, calls=%fused_computation.10 | loop fusion | flops 524288 | bytes 2097152 | tf_op jit(solution)/shard_map/concatenate | solution.py:214
  76.5 2.3 %pad_maximum_fusion.5.refs_2_ = bf16[8,256,256]{2,1,0:T(8,128)(2,1)} fusion(bf16[4,256,256]{2,1,0:T(8,128)(2,1)} %collective-permute-done.13, bf16[4,256,256]{2,1,0:T(8,128)(2,1)} %get-tuple-element.56), kind=kLoop, calls=%fused_computation.9 | loop fusion | flops 524288 | bytes 2097152 | tf_op jit(solution)/shard_map/concatenate | solution.py:214
  87.1 3.2 %response.2.refs_6_ = f32[2,512,256]{2,1,0:T(8,128)S(1)} custom-call(s32[6]{0:T(128)S(1)} %stack.36.idx, s32[1024]{0:T(1024)S(1)} %reshape.21.mask, bf16[8,256,256]{2,1,0:T(8,128)(2,1)S(1)} %pad_maximum_fusion.2.refs_0_, bf16[8,256,256]{2,1,0:T(8,128)(2,1)S(1)} %pad_maximum_fusion.3.refs_1_, bf16[8,256,256]{2,1,0:T(8,128)(2,1)} %pad_maximum_fusion.5.refs_2_, ...), custom_call_target="tpu_custom_call" | custom-call | flops 2147483648 | bytes 7340032 | tf_op jit(solution)/shard_map/response/pallas_call | solution.py:229
  90.3 6.3 %collective-permute-done.16.refs_2_ = bf16[8,256,256]{2,1,0:T(8,128)(2,1)} collective-permute-done((bf16[8,256,256]{2,1,0:T(8,128)(2,1)}, bf16[8,256,256]{2,1,0:T(8,128)(2,1)}, u32[]{:S(2)}, u32[]{:S(2)}) %collective-permute-start.16) | collective-permute-done | bytes 1048608 | tf_op jit(solution)/shard_map/ppermute | solution.py:51
  96.6 3.6 %response.3.refs_4_ = bf16[2,512,256]{2,1,0:T(8,128)(2,1)S(1)} custom-call(s32[6]{0:T(128)S(1)} %stack.36.idx, s32[1024]{0:T(1024)S(1)} %reshape.21.mask, bf16[8,256,256]{2,1,0:T(8,128)(2,1)S(1)} %copy-done.1, bf16[8,256,256]{2,1,0:T(8,128)(2,1)} %collective-permute-done.10.refs_1_, bf16[8,256,256]{2,1,0:T(8,128)(2,1)} %collective-permute-done.16.refs_2_, ...), custom_call_target="tpu_custom_call" | custom-call | flops 2147483648 | bytes 7340032 | tf_op jit(solution)/shard_map/response/pallas_call | solution.py:229
  100.2 9.3 %collective-permute-start.20 = (bf16[2,512,256]{2,1,0:T(8,128)(2,1)S(1)}, bf16[2,512,256]{2,1,0:T(8,128)(2,1)S(1)}, u32[]{:S(2)}, u32[]{:S(2)}) collective-permute-start(bf16[2,512,256]{2,1,0:T(8,128)(2,1)S(1)} %response.3.refs_4_), channel_id=1, source_target_pairs={{0,16},{1,17},{2,18},{3,19},{4,20},{5,21},{6,22},{7,23},{8,24},{9,... | collective-permute-start | bytes 1572872 | tf_op jit(solution)/shard_map/ppermute | solution.py:51
  111.0 7.7 %collective-permute-done.19.refs_5_ = bf16[2,512,256]{2,1,0:T(8,128)(2,1)S(1)} collective-permute-done((bf16[2,512,256]{2,1,0:T(8,128)(2,1)S(1)}, bf16[2,512,256]{2,1,0:T(8,128)(2,1)S(1)}, u32[]{:S(2)}, u32[]{:S(2)}) %collective-permute-start.19) | collective-permute-done | bytes 524320 | tf_op jit(solution)/shard_map/ppermute | solution.py:51
  119.4 3.1 %broadcast_select_fusion.refs_11_ = bf16[128,8192]{1,0:T(8,128)(2,1)} fusion(bf16[128,8192]{1,0:T(8,128)(2,1)} %broadcast_select_fusion.1, bf16[128,8192]{1,0:T(8,128)(2,1)} %collective-permute-done.23, pred[]{:T(512)S(6)} %or.3), kind=kLoop, calls=%fused_computation.2 | loop fusion | flops 1048576 | bytes 6291457 | tf_op jit(solution)/shard_map/jit(_where)/select_n | solution.py:254
  125.9 7.1 %collective-permute-done.24.refs_6_ = bf16[2,2,512,256]{3,2,1,0:T(8,128)(2,1)} collective-permute-done((bf16[2,2,512,256]{3,2,1,0:T(8,128)(2,1)S(1)}, bf16[2,2,512,256]{3,2,1,0:T(8,128)(2,1)}, u32[]{:S(2)}, u32[]{:S(2)}) %collective-permute-start.24) | collective-permute-done | bytes 1048608 | tf_op jit(solution)/shard_map/ppermute | solution.py:51
  135.1 3.0 %collective-permute-done.25.refs_8_ = bf16[2,512,256]{2,1,0:T(8,128)(2,1)} collective-permute-done((bf16[2,512,256]{2,1,0:T(8,128)(2,1)S(1)}, bf16[2,512,256]{2,1,0:T(8,128)(2,1)}, u32[]{:S(2)}, u32[]{:S(2)}) %collective-permute-start.25) | collective-permute-done | bytes 524320 | tf_op jit(solution)/shard_map/ppermute | solution.py:51
  140.7 11.4 %density.1 = (bf16[2,512,256]{2,1,0:T(8,128)(2,1)}, f32[128,8,128]{2,1,0:T(8,128)S(1)}) custom-call(s32[6]{0:T(128)S(1)} %stack.36.idx, s32[1024]{0:T(1024)S(1)} %reshape.21.mask, s32[1024]{0:T(1024)S(1)} %reshape.22.mask_v, s32[32]{0:T(128)S(1)} %copy-done.4, bf16[8,256,256]{2,1,0:T(8,128)(2,1)S(1)} %pad_maximum_fusion.7.refs_0_, ...), custom_call_target="tpu_custom_call" | custom-call | flops 8589934592 | bytes 23068672 | tf_op jit(solution)/shard_map/density/pallas_call | solution.py:260
  152.1 25.0 %all_to_all.5 = f32[128,8,128]{2,1,0:T(8,128)S(1)} all-to-all(f32[128,8,128]{2,1,0:T(8,128)S(1)} %get-tuple-element.53), channel_id=1, replica_groups=mesh['row'=8,'col'=16] {'row','col'}, dimensions={0} | all-to-all | bytes 1048576 | tf_op jit(solution)/shard_map/all_to_all | solution.py:279
  (95 shorter events, 49.3 us)
Async XLA Ops:
  3.9 16.8 %collective-permute-start.3 = (bf16[128,8192]{1,0:T(8,128)(2,1)}, bf16[128,8192]{1,0:T(8,128)(2,1)S(1)}, u32[]{:S(2)}, u32[]{:S(2)}) collective-permute-start(bf16[128,8192]{1,0:T(8,128)(2,1)} %dynamic-slice_bitcast_fusion), channel_id=1, source_target_pairs={{0,16},{1,17},{2,18},{3,19},{4,20},{5,21},{6,22},{7,23},{8,24},{9,... | collective-permute-start | bytes 6291464 | tf_op jit(solution)/shard_map/ppermute | solution.py:51
  5.4 15.2 %collective-permute-start = (bf16[1,768,256]{2,1,0:T(8,128)(2,1)S(1)}, bf16[1,768,256]{2,1,0:T(8,128)(2,1)}, u32[]{:S(2)}, u32[]{:S(2)}) collective-permute-start(bf16[1,768,256]{2,1,0:T(8,128)(2,1)S(1)} %maximum_bitcast_fusion), channel_id=1, source_target_pairs={{0,1},{1,0},{2,3},{3,2},{4,5},{5,4},{6,7},{7,6},{8,9},{9,8},{10,11... | collective-permute-start | bytes 1179656 | tf_op jit(solution)/shard_map/ppermute | solution.py:51
  9.4 11.3 %collective-permute-start.1 = (bf16[1,768,256]{2,1,0:T(8,128)(2,1)S(1)}, bf16[1,768,256]{2,1,0:T(8,128)(2,1)}, u32[]{:S(2)}, u32[]{:S(2)}) collective-permute-start(bf16[1,768,256]{2,1,0:T(8,128)(2,1)S(1)} %maximum_bitcast_fusion.1), channel_id=1, source_target_pairs={{0,4},{1,5},{2,6},{3,7},{4,0},{5,1},{6,2},{7,3},{8,12},{9,13},{10,... | collective-permute-start | bytes 1179656 | tf_op jit(solution)/shard_map/ppermute | solution.py:51
  24.7 11.5 %collective-permute-start.5 = (bf16[2,768,256]{2,1,0:T(8,128)(2,1)}, bf16[2,768,256]{2,1,0:T(8,128)(2,1)}, u32[]{:S(2)}, u32[]{:S(2)}) collective-permute-start(bf16[2,768,256]{2,1,0:T(8,128)(2,1)} %pad_maximum_fusion.11), channel_id=1, source_target_pairs={{0,12},{1,13},{2,14},{3,15},{4,8},{5,9},{6,10},{7,11},{8,4},{9,5},... | collective-permute-start | bytes 2359304 | tf_op jit(solution)/shard_map/ppermute | solution.py:51
  24.7 11.5 %collective-permute-start.4 = (bf16[2,768,256]{2,1,0:T(8,128)(2,1)}, bf16[2,768,256]{2,1,0:T(8,128)(2,1)}, u32[]{:S(2)}, u32[]{:S(2)}) collective-permute-start(bf16[2,768,256]{2,1,0:T(8,128)(2,1)} %pad_maximum_fusion.10), channel_id=1, source_target_pairs={{0,3},{1,2},{2,1},{3,0},{4,7},{5,6},{6,5},{7,4},{8,11},{9,10},{10,... | collective-permute-start | bytes 2359304 | tf_op jit(solution)/shard_map/ppermute | solution.py:51
  39.3 26.7 %collective-permute-start.15 = (bf16[128,8192]{1,0:T(8,128)(2,1)}, bf16[128,8192]{1,0:T(8,128)(2,1)}, u32[]{:S(2)}, u32[]{:S(2)}) collective-permute-start(bf16[128,8192]{1,0:T(8,128)(2,1)} %bitcast_select_fusion), channel_id=1, source_target_pairs={{0,32},{1,33},{2,34},{3,35},{4,36},{5,37},{6,38},{7,39},{8,40},{9,... | collective-permute-start | bytes 6291464 | tf_op jit(solution)/shard_map/ppermute | solution.py:51
  45.2 11.1 %collective-permute-start.7 = (bf16[4,256,256]{2,1,0:T(8,128)(2,1)S(1)}, bf16[4,256,256]{2,1,0:T(8,128)(2,1)}, u32[]{:S(2)}, u32[]{:S(2)}) collective-permute-start(bf16[4,256,256]{2,1,0:T(8,128)(2,1)S(1)} %get-tuple-element.57), channel_id=1, source_target_pairs={{0,4},{1,5},{2,6},{3,7},{4,0},{5,1},{6,2},{7,3},{8,12},{9,13},{10,... | collective-permute-start | bytes 1572872 | tf_op jit(solution)/shard_map/ppermute | solution.py:51
  50.5 9.3 %collective-permute-start.9 = (bf16[4,256,256]{2,1,0:T(8,128)(2,1)S(1)}, bf16[4,256,256]{2,1,0:T(8,128)(2,1)}, u32[]{:S(2)}, u32[]{:S(2)}) collective-permute-start(bf16[4,256,256]{2,1,0:T(8,128)(2,1)S(1)} %get-tuple-element.55), channel_id=1, source_target_pairs={{0,1},{1,0},{2,3},{3,2},{4,5},{5,4},{6,7},{7,6},{8,9},{9,8},{10,11... | collective-permute-start | bytes 1572872 | tf_op jit(solution)/shard_map/ppermute | solution.py:51
  50.5 15.1 %collective-permute-start.14 = (bf16[4,256,256]{2,1,0:T(8,128)(2,1)}, bf16[4,256,256]{2,1,0:T(8,128)(2,1)}, u32[]{:S(2)}, u32[]{:S(2)}) collective-permute-start(bf16[4,256,256]{2,1,0:T(8,128)(2,1)} %get-tuple-element.54), channel_id=1, source_target_pairs={{0,1},{1,0},{2,3},{3,2},{4,5},{5,4},{6,7},{7,6},{8,9},{9,8},{10,11... | collective-permute-start | bytes 1572872 | tf_op jit(solution)/shard_map/ppermute | solution.py:51
  53.1 12.5 %collective-permute-start.13 = (bf16[4,256,256]{2,1,0:T(8,128)(2,1)}, bf16[4,256,256]{2,1,0:T(8,128)(2,1)}, u32[]{:S(2)}, u32[]{:S(2)}) collective-permute-start(bf16[4,256,256]{2,1,0:T(8,128)(2,1)} %get-tuple-element.56), channel_id=1, source_target_pairs={{0,4},{1,5},{2,6},{3,7},{4,0},{5,1},{6,2},{7,3},{8,12},{9,13},{10,... | collective-permute-start | bytes 1572872 | tf_op jit(solution)/shard_map/ppermute | solution.py:51
  57.5 21.3 %collective-permute-start.8 = (bf16[8,256,256]{2,1,0:T(8,128)(2,1)S(1)}, bf16[8,256,256]{2,1,0:T(8,128)(2,1)S(1)}, u32[]{:S(2)}, u32[]{:S(2)}) collective-permute-start(bf16[8,256,256]{2,1,0:T(8,128)(2,1)S(1)} %pad_maximum_fusion.2.refs_0_), channel_id=1, source_target_pairs={{0,12},{1,13},{2,14},{3,15},{4,8},{5,9},{6,10},{7,11},{8,4},{9,5},... | collective-permute-start | bytes 3145736 | tf_op jit(solution)/shard_map/ppermute | solution.py:51
  61.1 20.1 %collective-permute-start.10 = (bf16[8,256,256]{2,1,0:T(8,128)(2,1)S(1)}, bf16[8,256,256]{2,1,0:T(8,128)(2,1)}, u32[]{:S(2)}, u32[]{:S(2)}) collective-permute-start(bf16[8,256,256]{2,1,0:T(8,128)(2,1)S(1)} %pad_maximum_fusion.3.refs_1_), channel_id=1, source_target_pairs={{0,3},{1,2},{2,1},{3,0},{4,7},{5,6},{6,5},{7,4},{8,11},{9,10},{10,... | collective-permute-start | bytes 3145736 | tf_op jit(solution)/shard_map/ppermute | solution.py:51
  66.0 21.0 %collective-permute-start.18 = (bf16[4,512,256]{2,1,0:T(8,128)(2,1)S(1)}, bf16[4,512,256]{2,1,0:T(8,128)(2,1)}, u32[]{:S(2)}, u32[]{:S(2)}) collective-permute-start(bf16[4,512,256]{2,1,0:T(8,128)(2,1)S(1)} %pad_maximum_fusion.4.refs_4_), channel_id=1, source_target_pairs={{0,16},{1,17},{2,18},{3,19},{4,20},{5,21},{6,22},{7,23},{8,24},{9,... | collective-permute-start | bytes 3145736 | tf_op jit(solution)/shard_map/ppermute | solution.py:51
  70.5 48.9 %collective-permute-start.23 = (bf16[128,8192]{1,0:T(8,128)(2,1)}, bf16[128,8192]{1,0:T(8,128)(2,1)}, u32[]{:S(2)}, u32[]{:S(2)}) collective-permute-start(bf16[128,8192]{1,0:T(8,128)(2,1)} %broadcast_select_fusion.1), channel_id=1, source_target_pairs={{0,96},{1,97},{2,98},{3,99},{4,100},{5,101},{6,102},{7,103},{8,104... | collective-permute-start | bytes 6291464 | tf_op jit(solution)/shard_map/ppermute | solution.py:51
  75.0 15.3 %collective-permute-start.17 = (bf16[8,256,256]{2,1,0:T(8,128)(2,1)}, bf16[8,256,256]{2,1,0:T(8,128)(2,1)}, u32[]{:S(2)}, u32[]{:S(2)}) collective-permute-start(bf16[8,256,256]{2,1,0:T(8,128)(2,1)} %pad_maximum_fusion.6.refs_3_), channel_id=1, source_target_pairs={{0,3},{1,2},{2,1},{3,0},{4,7},{5,6},{6,5},{7,4},{8,11},{9,10},{10,... | collective-permute-start | bytes 3145736 | tf_op jit(solution)/shard_map/ppermute | solution.py:51
  79.7 16.8 %collective-permute-start.16 = (bf16[8,256,256]{2,1,0:T(8,128)(2,1)}, bf16[8,256,256]{2,1,0:T(8,128)(2,1)}, u32[]{:S(2)}, u32[]{:S(2)}) collective-permute-start(bf16[8,256,256]{2,1,0:T(8,128)(2,1)} %pad_maximum_fusion.5.refs_2_), channel_id=1, source_target_pairs={{0,12},{1,13},{2,14},{3,15},{4,8},{5,9},{6,10},{7,11},{8,4},{9,5},... | collective-permute-start | bytes 3145736 | tf_op jit(solution)/shard_map/ppermute | solution.py:51
  84.9 24.6 %collective-permute-start.12 = (bf16[4,256,256]{2,1,0:T(8,128)(2,1)}, bf16[4,256,256]{2,1,0:T(8,128)(2,1)}, u32[]{:S(2)}, u32[]{:S(2)}) collective-permute-start(bf16[4,256,256]{2,1,0:T(8,128)(2,1)} %slice.37), channel_id=1, source_target_pairs={{0,1},{1,0},{2,3},{3,2},{4,5},{5,4},{6,7},{7,6},{8,9},{9,8},{10,11... | collective-permute-start | bytes 1572872 | tf_op jit(solution)/shard_map/ppermute | solution.py:51
  87.1 22.4 %collective-permute-start.11 = (bf16[4,256,256]{2,1,0:T(8,128)(2,1)}, bf16[4,256,256]{2,1,0:T(8,128)(2,1)}, u32[]{:S(2)}, u32[]{:S(2)}) collective-permute-start(bf16[4,256,256]{2,1,0:T(8,128)(2,1)} %slice.36), channel_id=1, source_target_pairs={{0,4},{1,5},{2,6},{3,7},{4,0},{5,1},{6,2},{7,3},{8,12},{9,13},{10,... | collective-permute-start | bytes 1572872 | tf_op jit(solution)/shard_map/ppermute | solution.py:51
  100.2 10.8 %collective-permute-start.20 = (bf16[2,512,256]{2,1,0:T(8,128)(2,1)S(1)}, bf16[2,512,256]{2,1,0:T(8,128)(2,1)S(1)}, u32[]{:S(2)}, u32[]{:S(2)}) collective-permute-start(bf16[2,512,256]{2,1,0:T(8,128)(2,1)S(1)} %response.3.refs_4_), channel_id=1, source_target_pairs={{0,16},{1,17},{2,18},{3,19},{4,20},{5,21},{6,22},{7,23},{8,24},{9,... | collective-permute-start | bytes 1572872 | tf_op jit(solution)/shard_map/ppermute | solution.py:51
  109.5 9.2 %collective-permute-start.19 = (bf16[2,512,256]{2,1,0:T(8,128)(2,1)S(1)}, bf16[2,512,256]{2,1,0:T(8,128)(2,1)S(1)}, u32[]{:S(2)}, u32[]{:S(2)}) collective-permute-start(bf16[2,512,256]{2,1,0:T(8,128)(2,1)S(1)} %response.3.refs_4_), channel_id=1, source_target_pairs={{0,32},{1,33},{2,34},{3,35},{4,36},{5,37},{6,38},{7,39},{8,40},{9,... | collective-permute-start | bytes 1572872 | tf_op jit(solution)/shard_map/ppermute | solution.py:51
  118.8 14.1 %collective-permute-start.24 = (bf16[2,2,512,256]{3,2,1,0:T(8,128)(2,1)S(1)}, bf16[2,2,512,256]{3,2,1,0:T(8,128)(2,1)}, u32[]{:S(2)}, u32[]{:S(2)}) collective-permute-start(bf16[2,2,512,256]{3,2,1,0:T(8,128)(2,1)S(1)} %pad_maximum_fusion.9), channel_id=1, source_target_pairs={{0,96},{1,97},{2,98},{3,99},{4,100},{5,101},{6,102},{7,103},{8,104... | collective-permute-start | bytes 3145736 | tf_op jit(solution)/shard_map/ppermute | solution.py:51
  122.6 17.1 %collective-permute-start.27 = (bf16[128,8192]{1,0:T(8,128)(2,1)}, bf16[128,8192]{1,0:T(8,128)(2,1)}, u32[]{:S(2)}, u32[]{:S(2)}) collective-permute-start(bf16[128,8192]{1,0:T(8,128)(2,1)} %broadcast_select_fusion.refs_11_), channel_id=1, source_target_pairs={{0,16},{1,17},{2,18},{3,19},{4,20},{5,21},{6,22},{7,23},{8,24},{9,... | collective-permute-start | bytes 6291464 | tf_op jit(solution)/shard_map/ppermute | solution.py:51
  124.1 14.1 %collective-permute-start.22 = (bf16[8,256,256]{2,1,0:T(8,128)(2,1)S(1)}, bf16[8,256,256]{2,1,0:T(8,128)(2,1)}, u32[]{:S(2)}, u32[]{:S(2)}) collective-permute-start(bf16[8,256,256]{2,1,0:T(8,128)(2,1)S(1)} %pad_maximum_fusion.8.refs_2_), channel_id=1, source_target_pairs={{0,3},{1,2},{2,1},{3,0},{4,7},{5,6},{6,5},{7,4},{8,11},{9,10},{10,... | collective-permute-start | bytes 3145736 | tf_op jit(solution)/shard_map/ppermute | solution.py:51
  125.5 14.1 %collective-permute-start.21 = (bf16[8,256,256]{2,1,0:T(8,128)(2,1)S(1)}, bf16[8,256,256]{2,1,0:T(8,128)(2,1)}, u32[]{:S(2)}, u32[]{:S(2)}) collective-permute-start(bf16[8,256,256]{2,1,0:T(8,128)(2,1)S(1)} %pad_maximum_fusion.7.refs_0_), channel_id=1, source_target_pairs={{0,12},{1,13},{2,14},{3,15},{4,8},{5,9},{6,10},{7,11},{8,4},{9,5},... | collective-permute-start | bytes 3145736 | tf_op jit(solution)/shard_map/ppermute | solution.py:51
  (17 other events, 122.9 us)

commit v4 on v3

v4 whole, which is shorter than its diff:
```python
import functools

import jax
import jax.numpy as jnp
from jax import lax
from jax.experimental import pallas as pl
from jax.experimental.pallas import tpu as pltpu
from jax.sharding import PartitionSpec as P

BS = 128
NB = 32
SPAN = 16
SP = 512
NSLAB = 128
RING = 4
N_COL = 16
WIDE = 2
BF16 = jnp.bfloat16
F32 = jnp.float32
AXES = ("row", "col")


def place(x, core, y, z):
    return ((x % RING) * 2 + core) * N_COL + (y % RING) * RING + z % RING


def pairs(move):
    out = []
    for x in range(RING):
        for core in range(2):
            for y in range(RING):
                for z in range(RING):
                    target = move(x, core, y, z)
                    if target is not None:
                        out.append((place(x, core, y, z), place(*target)))
    return out


def along(axis, step):
    def move(x, core, y, z, flip):
        at = [x, y, z]
        at["xyz".index(axis)] ^= flip
        return at[0], core, at[1], at[2]

    return pairs(lambda x, core, y, z: move(x, core, y, z, 1 if core == step else 3))


OTHER_CORE = pairs(lambda x, core, y, z: (x, 1 - core, y, z))

def send(value, route):
    return lax.ppermute(value, AXES, route)


def together(*values):
    return lax.optimization_barrier(values)


def neighbours(value, axis):
    return [send(value, along(axis, 0)), send(value, along(axis, 1))]


def gather(value, axis):
    first, second = neighbours(value, axis)
    return [value, first, second, send(first, along(axis, 1))]


def masked(values, block_mask, row_index, col_index):
    row_blocks, col_blocks = values.shape[0] // BS, values.shape[1] // BS
    tile_mask = lax.dynamic_slice(
        block_mask, (row_index * row_blocks, col_index * col_blocks), (row_blocks, col_blocks)
    ).astype(values.dtype)
    shaped = values.reshape(row_blocks, BS, col_blocks, BS)
    return (shaped * tile_mask[:, None, :, None]).reshape(values.shape)


def offset(core, g):
    return (0, 1 + 2 * core, 3 - 2 * core, 2)[g]


def source(idx, first, h, g):
    dy, dz = (h, g) if first == 0 else (g, h)
    return idx[2] ^ offset(idx[1], dy), idx[3] ^ offset(idx[1], dz)


def place_of(core, flip):
    return jnp.where(flip == 2, 3, jnp.where(flip == 0, 0, jnp.where(flip == 1 + 2 * core, 1, 2)))


def piece_scale(mask, row_block, col_block, rows, dtype):
    first_lanes = lax.broadcasted_iota(jnp.int32, (BS, 2 * BS), 1) < BS
    scales = []
    for i in range(rows):
        at = (row_block + i) * NB + col_block
        scales.append(jnp.where(first_lanes, mask[at].astype(F32), mask[at + 1].astype(F32)).astype(dtype))
    return jnp.concatenate(scales, axis=0)


def half_rows(zs):
    return pl.ds(pl.multiple_of((zs & 1) * 2 * BS, 2 * BS), 2 * BS)


def response_kernel(part, idx, mask, *refs):
    groups = ((0, 1, 2), (3,))[part]
    count = 2 * len(groups)
    t_refs, c_own, c_other = refs[:count], refs[count], refs[count + 1]
    before, out, panel = (None, *refs[count + 2:]) if part == 0 else refs[count + 2:]
    x, core, row = idx[0], idx[1], idx[4]
    for g in range(RING):
        panel[(x ^ offset(core, g)) * 2 + core] = c_own[g]
        panel[(x ^ offset(1 - core, g)) * 2 + 1 - core] = c_other[g]
    for v in range(2):
        total = jnp.zeros((4 * BS, 2 * BS), F32) if part == 0 else before[v]
        for k, h in enumerate(groups):
            lefts, rights = [], []
            for g in range(RING):
                ys, zs = source(idx, v, h, g)
                col = ys * RING + zs
                lefts.append(t_refs[v * len(groups) + k][g] * piece_scale(mask, row * 4, col * 2, 4, BF16))
                rights.append(panel[col // 2, half_rows(zs), :])
            total += jnp.dot(
                jnp.concatenate(lefts, axis=1), jnp.concatenate(rights, axis=0), preferred_element_type=F32
            )
        out[v] = total.astype(out.dtype)


def kernel_terms(idx, mask_v, valence, r_panel, flips):
    x, core, z, row = idx[0], idx[1], idx[3], idx[4]
    totals = [[0.0, 0.0], [0.0, 0.0]]
    for slot, flip in enumerate(flips):
        ys = x ^ flip
        for half in range(2):
            lefts, places = [], []
            for g in range(RING):
                zs = z ^ offset(core, g)
                lefts.append(valence(half, ys, g) * piece_scale(mask_v, row * 4 + half * 2, (ys * RING + zs) * 2, 2, BF16))
                places.append(zs)
            left = jnp.concatenate(lefts, axis=1)
            for v in range(2):
                rights = [r_panel[slot * 2 + zs // 2, v, half_rows(zs), :] for zs in places]
                totals[half][v] += jnp.dot(left, jnp.concatenate(rights, axis=0), preferred_element_type=F32)
    return totals


def panel_copies(idx, v_refs, v_panel):
    out = [(v_refs[h], v_panel.at[0, idx[2] ^ offset(idx[1], h)]) for h in range(RING)]
    out += [(v_refs[RING + g], v_panel.at[1, g]) for g in range(RING)]
    return out


def start_all(copies, sems):
    copies = [pltpu.make_async_copy(a, b, sems.at[k]) for k, (a, b) in enumerate(copies)]
    for copy in copies:
        copy.start()
    return copies


def early_kernel(idx, mask_v, *refs):
    v_refs, r_refs, out, v_last, v_panel, r_panel, sems = refs[:8], refs[8:14], *refs[14:]
    core, y = idx[1], idx[2]
    copies = panel_copies(idx, v_refs, v_panel)
    for side in range(2):
        own = core ^ side
        copies.append((r_refs[3 * side], r_panel.at[own]))
        copies.append((r_refs[3 * side + 1], r_panel.at[(1 + own) * 2 + own]))
        copies.append((r_refs[3 * side + 2], r_panel.at[(2 - own) * 2 + own]))
    for copy in start_all(copies, sems):
        copy.wait()

    def valence(half, ys, g):
        return v_panel[0, ys, g] if half == 0 else v_panel[1, g, place_of(core, y ^ ys)]

    for half in range(2):
        for g in range(RING):
            v_last[half, g] = valence(half, idx[0] ^ 2, g)
    totals = kernel_terms(idx, mask_v, valence, r_panel, (0, 1, 3))
    for half in range(2):
        for v in range(2):
            out[v, half * 2 * BS:(half + 1) * 2 * BS, :] = totals[half][v]


def density_kernel(idx, mask, mask_v, starts, *refs):
    v_last, r_own, r_other, before, orb_hbm, near_hbm, far_hbm, k_out, dens, r_panel, orb, partner, sems = refs
    core, row, col = idx[1], idx[4], idx[5]
    copies = [(near_hbm, partner.at[core]), (far_hbm, partner.at[1 - core])]
    copies = start_all(copies + [(orb_hbm.at[i], orb.at[i]) for i in range(4)], sems)
    r_panel[core] = r_own[...]
    r_panel[1 - core] = r_other[...]
    totals = kernel_terms(idx, mask_v, lambda half, ys, g: v_last[half, g], r_panel, (2,))
    for half in range(2):
        scale = piece_scale(mask, row * 4 + half * 2, col * 2, 2, F32)
        rows = slice(half * 2 * BS, (half + 1) * 2 * BS)
        for v in range(2):
            k_out[v, rows, :] = ((before[v, rows, :] + totals[half][v]) * scale).astype(BF16)
    dens[...] = jnp.zeros_like(dens)
    copies[0].wait()
    copies[1].wait()
    starts_j = [starts[col * 2 + j] for j in range(2)]
    for i in range(4):
        copies[2 + i].wait()
        left = jnp.concatenate([k_out[v, i * BS:(i + 1) * BS, :] for v in range(2)], axis=0)
        start_i = starts[row * 4 + i]

        def slabs(step, carry, left=left, start_i=start_i, i=i):
            begin = step * WIDE
            offsets = [start_i + begin - starts_j[j] for j in range(2)]
            touched = [(o > -WIDE) & (o < SPAN) for o in offsets]

            @pl.when(touched[0] | touched[1])
            def _():
                for k in range(WIDE):
                    frames = []
                    for j in range(2):
                        o = offsets[j] + k
                        at = pl.multiple_of(jnp.clip(o, 0, SPAN - 1) * SP, SP)
                        inside = jnp.where((o >= 0) & (o < SPAN), 1.0, 0.0).astype(BF16)
                        frames.append(partner[j, :, pl.ds(at, SP)] * inside)
                    applied = jnp.dot(left, jnp.concatenate(frames, axis=0), preferred_element_type=F32)
                    own = orb[i, :, pl.ds(pl.multiple_of((begin + k) * SP, SP), SP)].astype(F32)
                    for v in range(2):
                        terms = jnp.sum(own * applied[v * BS:(v + 1) * BS], axis=0, keepdims=True)
                        for q in range(4):
                            dens[start_i + begin + k, pl.ds(v * 4 + q, 1), :] += terms[:, q * BS:(q + 1) * BS]

            return carry

        lax.fori_loop(0, SPAN // WIDE, slabs, 0)


SMEM = pl.BlockSpec(memory_space=pltpu.SMEM)
VMEM = pl.BlockSpec(memory_space=pltpu.VMEM)
ANY = pl.BlockSpec(memory_space=pl.ANY)


def local(p_valence, p_conduction, trial_vectors, mask_valence, mask_conduction, mask_trial, orbitals, sphere_starts):
    row, col = lax.axis_index("row"), lax.axis_index("col")
    x, core, y, z = row // 2, row % 2, col // RING, col % RING
    idx = jnp.stack([x, core, y, z, row, col]).astype(jnp.int32)
    mask_flat = mask_trial.reshape(-1)

    first = 2 * (col % 2)
    conduction = masked(p_conduction, mask_conduction, row, col)
    both_z = jnp.concatenate([trial_vectors[0], p_valence[:2 * BS]])
    both_y = jnp.concatenate([trial_vectors[1], p_valence[2 * BS:]])

    theirs = lax.dynamic_slice_in_dim(orbitals, first + 1 - core, 1, 0)[0]
    z_first, y_first, z_second, y_second, given, conduction, first = together(
        send(both_z, along("z", 0)), send(both_y, along("y", 0)),
        send(both_z, along("z", 1)), send(both_y, along("y", 1)),
        send(theirs, OTHER_CORE), conduction, first,
    )
    mine = lax.dynamic_slice_in_dim(orbitals, first + core, 1, 0)[0]
    seed = jnp.where(core == z // 2, mine, given)
    reached = send(seed, along("x", 0))
    z_third, y_third, x_first, x_second = together(
        send(z_first, along("z", 1)), send(y_first, along("y", 1)), *neighbours(conduction, "x")
    )
    by_z, by_y = [both_z, z_first, z_second, z_third], [both_y, y_first, y_second, y_third]
    own_0 = jnp.stack([piece[:4 * BS] for piece in by_z])
    own_1 = jnp.stack([piece[:4 * BS] for piece in by_y])
    *others, x_third = together(
        *neighbours(own_0, "y"), *neighbours(own_1, "z"), send(x_first, along("x", 1))
    )
    trials_0, trials_1 = [own_0] + others[:2], [own_1] + others[2:]
    trials_0.append(send(trials_0[1], along("y", 1)))
    trials_1.append(send(trials_1[1], along("z", 1)))
    c_own = jnp.stack([conduction, x_first, x_second, x_third])
    c_other = send(c_own, OTHER_CORE)
    passed = jnp.where(x == y, seed, reached)
    arrived = send(passed, along("x", 1))


    response = None
    for part in range(2):
        if part == 1:
            *ends, trials_0[3], trials_1[3], response = together(
                *[piece[4 * BS:] for piece in by_z + by_y], trials_0[3], trials_1[3], response
            )
        groups = (slice(0, 3), slice(3, 4))[part]
        pieces = trials_0[groups] + trials_1[groups]
        response = pl.pallas_call(
            functools.partial(response_kernel, part),
            name="response",
            out_shape=jax.ShapeDtypeStruct((2, 4 * BS, 2 * BS), (F32, BF16)[part]),
            in_specs=[SMEM, SMEM] + [VMEM] * (len(pieces) + 2 + part),
            out_specs=VMEM,
            scratch_shapes=[pltpu.VMEM((8, 4 * BS, 2 * BS), BF16)],
            compiler_params=pltpu.CompilerParams(vmem_limit_bytes=24 * 2**20),
            cost_estimate=pl.CostEstimate(flops=2**(32 + 4 * part), bytes_accessed=9 * 2**20, transcendentals=0),
        )(idx, mask_flat, *pieces, c_own, c_other, *([response] if part else []))

    valences = [jnp.stack(ends[:4]), jnp.stack(ends[4:8])]
    valences = [valences[0], send(valences[0], along("y", 0)), valences[1], send(valences[1], along("z", 0))]
    responses = gather(response, "x")
    valences[1], valences[3], *responses[1:3], arrived = together(valences[1], valences[3], *responses[1:3], arrived)
    for at, axis in ((0, "y"), (4, "z")):
        valences[at + 2:at + 2] = [send(valences[at], along(axis, 1)), send(valences[at + 1], along(axis, 1))]
    swapped = [send(piece, OTHER_CORE) for piece in responses]
    near = jnp.where((x == y) | (x ^ (1 + 2 * core) == y), passed, arrived)
    far = send(near, OTHER_CORE)
    mask_v = mask_valence.reshape(-1)

    early, v_last = pl.pallas_call(
        early_kernel,
        name="early",
        out_shape=(
            jax.ShapeDtypeStruct((2, 4 * BS, 2 * BS), F32),
            jax.ShapeDtypeStruct((2, RING, 2 * BS, 2 * BS), BF16),
        ),
        in_specs=[SMEM, SMEM] + [ANY] * 14,
        out_specs=(VMEM, VMEM),
        scratch_shapes=[
            pltpu.VMEM((2, RING, RING, 2 * BS, 2 * BS), BF16),
            pltpu.VMEM((6, 2, 4 * BS, 2 * BS), BF16),
            pltpu.SemaphoreType.DMA((14,)),
        ],
        compiler_params=pltpu.CompilerParams(vmem_limit_bytes=20 * 2**20),
        cost_estimate=pl.CostEstimate(flops=2**36, bytes_accessed=8 * 2**20, transcendentals=0),
    )(idx, mask_v, *valences, *responses[:3], *swapped[:3])

    kernel, density = pl.pallas_call(
        density_kernel,
        name="density",
        out_shape=(
            jax.ShapeDtypeStruct((2, 4 * BS, 2 * BS), BF16),
            jax.ShapeDtypeStruct((NSLAB, 8, BS), F32),
        ),
        in_specs=[SMEM] * 4 + [VMEM] * 4 + [ANY] * 3,
        out_specs=(VMEM, VMEM),
        scratch_shapes=[
            pltpu.VMEM((2, 2, 4 * BS, 2 * BS), BF16),
            pltpu.VMEM((4, BS, SPAN * SP), BF16),
            pltpu.VMEM((2, BS, SPAN * SP), BF16),
            pltpu.SemaphoreType.DMA((6,)),
        ],
        compiler_params=pltpu.CompilerParams(vmem_limit_bytes=28 * 2**20),
        cost_estimate=pl.CostEstimate(flops=2**33, bytes_accessed=22 * 2**20, transcendentals=0),
    )(idx, mask_flat, mask_v, sphere_starts, v_last, responses[3], swapped[3], early, orbitals, near, far)

    terms = lax.all_to_all(density, AXES, 0, 0, tiled=True)
    return kernel, jnp.sum(terms, axis=0).reshape(2, SP)


def solution(mesh):
    placed = (
        P("row", "col"),
        P("row", "col"),
        P(None, "row", "col"),
        P(),
        P(),
        P(),
        P("row", None, None),
        P(),
    )
    return jax.shard_map(
        local,
        mesh=mesh,
        in_specs=placed,
        out_specs=(P(None, "row", "col"), P(None, AXES)),
        check_vma=False,
    )
```

time: 179 us -> 165 us (0.922)
  other arithmetic: 30.9 us -> 12.5 us
  waiting for transfers between devices: 48.5 us -> 57.1 us
  blocking collectives: 25 us -> 21.1 us
  starting transfers between devices: 40.2 us -> 42.7 us
  Pallas kernels: 18.2 us -> 16 us
    concatenate x12 -> x2, other arithmetic: 19.5 us -> 1.57 us  [the longest x1 0.8 us: local(): both_y = jnp.concatenate([trial_vectors[1], p_valence[2 * BS:]])]
    ppermute x28 -> x33, waiting for transfers between devices: 48.5 us -> 57.1 us  [send(): return lax.ppermute(value, AXES, route)]
    pallas_call x1, Pallas kernels: 11.4 us -> 6.51 us  [local(): pl.pallas_call(density_kernel, name='density', out_shape=(jax.ShapeDtypeS...]
    pallas_call x0 -> x1, Pallas kernels: none -> 4.24 us  [local(): pl.pallas_call(early_kernel, name='early', out_shape=(jax.ShapeDtypeStruc...]
    another operation x0 -> x4, local copies, waits for them, and re-layouts: none -> 4.06 us  [the longest x2 2.1 us: local(): own_1 = jnp.stack([piece[:4 * BS] for piece in by_y])]
    all_to_all x1, blocking collectives: 25 us -> 21.1 us  [local(): terms = lax.all_to_all(density, AXES, 0, 0, tiled=True)]
    unnamed x26 -> x24, local copies, waits for them, and re-layouts: 3.2 us -> 0.06 us
    ppermute x28 -> x33, starting transfers between devices: 40.2 us -> 42.7 us  [send(): return lax.ppermute(value, AXES, route)]
  transfers between devices with their start and end apart: 28 -> 33, of which waited for: 13 -> 12; matrix products, arithmetic and copies ran while one was open for 17% -> 14% of each run, Pallas kernels for 4% -> 6%
where the time goes in v4:
time: 165 us; the launch traced here: 164 us
  waiting for transfers between devices  57.1 us (35%)
  starting transfers between devices  42.7 us (26%)
  blocking collectives  21.1 us (13%)
  Pallas kernels  16 us (10%)
  local copies, waits for them, and re-layouts  13.7 us (8%)
  other arithmetic  12.5 us (8%)
    ppermute x33, waiting for transfers between devices, send(): return lax.ppermute(value, AXES, route)  57.1 us
    ppermute x33, starting transfers between devices, send(): return lax.ppermute(value, AXES, route)  42.7 us
    all_to_all x1, blocking collectives, local(): terms = lax.all_to_all(density, AXES, 0, 0, tiled=True)  21.1 us
    pallas_call x1, Pallas kernels, local(): pl.pallas_call(density_kernel, name='density', out_shape=(jax.ShapeDtypeS...  6.51 us
    pallas_call x2, Pallas kernels, local(): pl.pallas_call(functools.partial(response_kernel, part), name='response',...  5.26 us
    slice x7, local copies, waits for them, and re-layouts, local(): piece[4 * BS:]  4.58 us
    pallas_call x1, Pallas kernels, local(): pl.pallas_call(early_kernel, name='early', out_shape=(jax.ShapeDtypeStruc...  4.24 us
  transfers between devices with their start and end apart: 33, of which 12 were waited for; matrix products, arithmetic and copies ran while one was open for 14% of the time, Pallas kernels for 6%

profile of v4, /device:TPU:1, one launch (start us, length us, event | category | flops | bytes accessed | tf_op | source)
XLA Modules:
  0.0 164.1 jit_solution(14460193110094238658)
XLA Ops:
  0.7 3.2 %dynamic-slice_bitcast_fusion = bf16[128,8192]{1,0:T(8,128)(2,1)} fusion(bf16[4,128,8192]{2,1,0:T(8,128)(2,1)} %refs_4_.1, s32[]{:T(128)S(6)} %select_n.62), kind=kLoop, calls=%fused_computation.1 | loop fusion | bytes 4194308 | tf_op jit(solution)/shard_map/squeeze | solution.py:245
  12.6 2.2 %collective-permute-start = (bf16[768,256]{1,0:T(8,128)(2,1)}, bf16[768,256]{1,0:T(8,128)(2,1)}, u32[]{:S(2)}, u32[]{:S(2)}) collective-permute-start(bf16[768,256]{1,0:T(8,128)(2,1)} %pad_maximum_fusion.5), channel_id=1, source_target_pairs={{0,1},{1,0},{2,3},{3,2},{4,5},{5,4},{6,7},{7,6},{8,9},{9,8},{10,11... | collective-permute-start | bytes 1179656 | tf_op jit(solution)/shard_map/ppermute | solution.py:51
  15.9 4.0 %collective-permute-done.1 = bf16[768,256]{1,0:T(8,128)(2,1)} collective-permute-done((bf16[768,256]{1,0:T(8,128)(2,1)}, bf16[768,256]{1,0:T(8,128)(2,1)}, u32[]{:S(2)}, u32[]{:S(2)}) %collective-permute-start.1) | collective-permute-done | bytes 393248 | tf_op jit(solution)/shard_map/ppermute | solution.py:51
  19.9 4.6 %collective-permute-done = bf16[768,256]{1,0:T(8,128)(2,1)} collective-permute-done((bf16[768,256]{1,0:T(8,128)(2,1)}, bf16[768,256]{1,0:T(8,128)(2,1)}, u32[]{:S(2)}, u32[]{:S(2)}) %collective-permute-start) | collective-permute-done | bytes 393248 | tf_op jit(solution)/shard_map/ppermute | solution.py:51
  28.8 3.1 %bitcast_select_fusion = bf16[128,8192]{1,0:T(8,128)(2,1)} fusion(bf16[128,8192]{1,0:T(8,128)(2,1)S(1)} %collective-permute-done.4, bf16[4,128,8192]{2,1,0:T(8,128)(2,1)} %refs_4_.1, s32[]{:T(128)S(6)} %select_n.68, pred[]{:T(512)S(6)} %eq.15), kind=kLoop, calls=%fused_computation | loop fusion | flops 1048576 | bytes 6291461 | tf_op jit(solution)/shard_map/jit(_where)/select_n | solution.py:252
  37.5 2.5 %collective-permute-start.11 = (bf16[4,512,256]{2,1,0:T(8,128)(2,1)S(1)}, bf16[4,512,256]{2,1,0:T(8,128)(2,1)S(1)}, u32[]{:S(2)}, u32[]{:S(2)}) collective-permute-start(bf16[4,512,256]{2,1,0:T(8,128)(2,1)S(1)} %pad_maximum_fusion.1.refs_3_), channel_id=1, source_target_pairs={{0,1},{1,0},{2,3},{3,2},{4,5},{5,4},{6,7},{7,6},{8,9},{9,8},{10,11... | collective-permute-start | bytes 3145736 | tf_op jit(solution)/shard_map/ppermute | solution.py:51
  41.8 7.0 %collective-permute-done.13 = bf16[512,256]{1,0:T(8,128)(2,1)} collective-permute-done((bf16[512,256]{1,0:T(8,128)(2,1)}, bf16[512,256]{1,0:T(8,128)(2,1)}, u32[]{:S(2)}, u32[]{:S(2)}) %collective-permute-start.13) | collective-permute-done | bytes 262176 | tf_op jit(solution)/shard_map/ppermute | solution.py:51
  56.0 5.2 %collective-permute-done.11.refs_4_ = bf16[4,512,256]{2,1,0:T(8,128)(2,1)S(1)} collective-permute-done((bf16[4,512,256]{2,1,0:T(8,128)(2,1)S(1)}, bf16[4,512,256]{2,1,0:T(8,128)(2,1)S(1)}, u32[]{:S(2)}, u32[]{:S(2)}) %collective-permute-start.11) | collective-permute-done | bytes 1048608 | tf_op jit(solution)/shard_map/ppermute | solution.py:51
  61.1 9.7 %collective-permute-done.9.refs_1_ = bf16[4,512,256]{2,1,0:T(8,128)(2,1)} collective-permute-done((bf16[4,512,256]{2,1,0:T(8,128)(2,1)S(1)}, bf16[4,512,256]{2,1,0:T(8,128)(2,1)}, u32[]{:S(2)}, u32[]{:S(2)}) %collective-permute-start.9) | collective-permute-done | bytes 1048608 | tf_op jit(solution)/shard_map/ppermute | solution.py:51
  74.1 3.1 %broadcast_select_fusion.1 = bf16[128,8192]{1,0:T(8,128)(2,1)} fusion(bf16[128,8192]{1,0:T(8,128)(2,1)} %bitcast_select_fusion, bf16[128,8192]{1,0:T(8,128)(2,1)} %collective-permute-done.21, pred[]{:T(512)S(6)} %eq.14), kind=kLoop, calls=%fused_computation.3 | loop fusion | flops 1048576 | bytes 6291457 | tf_op jit(solution)/shard_map/jit(_where)/select_n | solution.py:268
  77.6 3.8 %response.2.refs_4_ = f32[2,512,256]{2,1,0:T(8,128)S(1)} custom-call(s32[6]{0:T(128)S(1)} %stack.96.idx, s32[1024]{0:T(1024)S(1)} %reshape.17.mask, bf16[4,512,256]{2,1,0:T(8,128)(2,1)S(1)} %pad_maximum_fusion.refs_0_, bf16[4,512,256]{2,1,0:T(8,128)(2,1)} %collective-permute-done.9.refs_1_, bf16[4,512,256]{2,1,0:T(8,128)(2,1)} %collective-permute-done.10.refs_2_, ...), custom_call_target="tpu_custom_call" | custom-call | flops 4294967296 | bytes 9437184 | tf_op jit(solution)/shard_map/response/pallas_call | solution.py:280
  81.5 5.2 %collective-permute-done.14.refs_0_ = bf16[4,512,256]{2,1,0:T(8,128)(2,1)S(1)} collective-permute-done((bf16[4,512,256]{2,1,0:T(8,128)(2,1)}, bf16[4,512,256]{2,1,0:T(8,128)(2,1)S(1)}, u32[]{:S(2)}, u32[]{:S(2)}) %collective-permute-start.14) | collective-permute-done | bytes 1048608 | tf_op jit(solution)/shard_map/ppermute | solution.py:51
  86.8 3.3 %collective-permute-start.18 = (bf16[4,256,256]{2,1,0:T(8,128)(2,1)S(1)}, bf16[4,256,256]{2,1,0:T(8,128)(2,1)S(1)}, u32[]{:S(2)}, u32[]{:S(2)}) collective-permute-start(bf16[4,256,256]{2,1,0:T(8,128)(2,1)S(1)} %pad_maximum_fusion.4.refs_4_), channel_id=1, source_target_pairs={{0,1},{1,0},{2,3},{3,2},{4,5},{5,4},{6,7},{7,6},{8,9},{9,8},{10,11... | collective-permute-start | bytes 1572872 | tf_op jit(solution)/shard_map/ppermute | solution.py:51
  92.8 2.3 %collective-permute-start.19 = (bf16[2,512,256]{2,1,0:T(8,128)(2,1)S(1)}, bf16[2,512,256]{2,1,0:T(8,128)(2,1)}, u32[]{:S(2)}, u32[]{:S(2)}) collective-permute-start(bf16[2,512,256]{2,1,0:T(8,128)(2,1)S(1)} %response.3.refs_8_), channel_id=1, source_target_pairs={{0,32},{1,33},{2,34},{3,35},{4,36},{5,37},{6,38},{7,39},{8,40},{9,... | collective-permute-start | bytes 1572872 | tf_op jit(solution)/shard_map/ppermute | solution.py:51
  95.1 2.0 %collective-permute-done.18.refs_5_ = bf16[4,256,256]{2,1,0:T(8,128)(2,1)S(1)} collective-permute-done((bf16[4,256,256]{2,1,0:T(8,128)(2,1)S(1)}, bf16[4,256,256]{2,1,0:T(8,128)(2,1)S(1)}, u32[]{:S(2)}, u32[]{:S(2)}) %collective-permute-start.18) | collective-permute-done | bytes 524320 | tf_op jit(solution)/shard_map/ppermute | solution.py:51
  100.2 13.7 %collective-permute-done.20.refs_10_ = bf16[2,512,256]{2,1,0:T(8,128)(2,1)S(1)} collective-permute-done((bf16[2,512,256]{2,1,0:T(8,128)(2,1)S(1)}, bf16[2,512,256]{2,1,0:T(8,128)(2,1)S(1)}, u32[]{:S(2)}, u32[]{:S(2)}) %collective-permute-start.20) | collective-permute-done | bytes 524320 | tf_op jit(solution)/shard_map/ppermute | solution.py:51
  113.9 4.8 %collective-permute-start.27 = (bf16[2,512,256]{2,1,0:T(8,128)(2,1)S(1)}, bf16[2,512,256]{2,1,0:T(8,128)(2,1)}, u32[]{:S(2)}, u32[]{:S(2)}) collective-permute-start(bf16[2,512,256]{2,1,0:T(8,128)(2,1)S(1)} %response.3.refs_8_), channel_id=1, source_target_pairs={{0,16},{1,17},{2,18},{3,19},{4,20},{5,21},{6,22},{7,23},{8,24},{9,... | collective-permute-start | bytes 1572872 | tf_op jit(solution)/shard_map/ppermute | solution.py:51
  120.5 2.8 %collective-permute-start.28 = (bf16[2,512,256]{2,1,0:T(8,128)(2,1)}, bf16[2,512,256]{2,1,0:T(8,128)(2,1)S(1)}, u32[]{:S(2)}, u32[]{:S(2)}) collective-permute-start(bf16[2,512,256]{2,1,0:T(8,128)(2,1)} %collective-permute-done.19.refs_9_), channel_id=1, source_target_pairs={{0,16},{1,17},{2,18},{3,19},{4,20},{5,21},{6,22},{7,23},{8,24},{9,... | collective-permute-start | bytes 1572872 | tf_op jit(solution)/shard_map/ppermute | solution.py:51
  125.4 2.0 %collective-permute-done.30.refs_1_ = bf16[2,512,256]{2,1,0:T(8,128)(2,1)S(1)} collective-permute-done((bf16[2,512,256]{2,1,0:T(8,128)(2,1)}, bf16[2,512,256]{2,1,0:T(8,128)(2,1)S(1)}, u32[]{:S(2)}, u32[]{:S(2)}) %collective-permute-start.30) | collective-permute-done | bytes 524320 | tf_op jit(solution)/shard_map/ppermute | solution.py:51
  127.4 2.1 %collective-permute-start.31 = (bf16[2,512,256]{2,1,0:T(8,128)(2,1)S(1)}, bf16[2,512,256]{2,1,0:T(8,128)(2,1)S(1)}, u32[]{:S(2)}, u32[]{:S(2)}) collective-permute-start(bf16[2,512,256]{2,1,0:T(8,128)(2,1)S(1)} %collective-permute-done.30.refs_1_), channel_id=1, source_target_pairs={{0,16},{1,17},{2,18},{3,19},{4,20},{5,21},{6,22},{7,23},{8,24},{9,... | collective-permute-start | bytes 1572872 | tf_op jit(solution)/shard_map/ppermute | solution.py:51
  129.4 2.0 %collective-permute-start.32 = (bf16[128,8192]{1,0:T(8,128)(2,1)S(1)}, bf16[128,8192]{1,0:T(8,128)(2,1)S(1)}, u32[]{:S(2)}, u32[]{:S(2)}) collective-permute-start(bf16[128,8192]{1,0:T(8,128)(2,1)S(1)} %broadcast_select_fusion.refs_5_), channel_id=1, source_target_pairs={{0,16},{1,17},{2,18},{3,19},{4,20},{5,21},{6,22},{7,23},{8,24},{9,... | collective-permute-start | bytes 6291464 | tf_op jit(solution)/shard_map/ppermute | solution.py:51
  131.4 4.2 %early.1 = (f32[2,512,256]{2,1,0:T(8,128)S(1)}, bf16[2,4,256,256]{3,2,1,0:T(8,128)(2,1)S(1)}) custom-call(s32[6]{0:T(128)S(1)} %stack.96.idx, s32[1024]{0:T(1024)S(1)} %reshape.18.mask_v, bf16[4,256,256]{2,1,0:T(8,128)(2,1)S(1)} %pad_maximum_fusion.3.refs_0_, bf16[4,256,256]{2,1,0:T(8,128)(2,1)S(1)} %collective-permute-done.17.refs_1_, ...), custom_call_target="tpu_custom_call" | custom-call | flops 68719476736 | bytes 8388608 | tf_op jit(solution)/shard_map/early/pallas_call | solution.py:302
  135.7 6.5 %density.1 = (bf16[2,512,256]{2,1,0:T(8,128)(2,1)}, f32[128,8,128]{2,1,0:T(8,128)S(1)}) custom-call(s32[6]{0:T(128)S(1)} %stack.96.idx, s32[1024]{0:T(1024)S(1)} %reshape.17.mask, s32[1024]{0:T(1024)S(1)} %reshape.18.mask_v, s32[32]{0:T(128)S(1)} %copy-done, bf16[2,4,256,256]{3,2,1,0:T(8,128)(2,1)S(1)} %get-tuple-element.69.refs_0_, ...), custom_call_target="tpu_custom_call" | custom-call | flops 8589934592 | bytes 23068672 | tf_op jit(solution)/shard_map/density/pallas_call | solution.py:320
  142.3 21.1 %all_to_all.5 = f32[128,8,128]{2,1,0:T(8,128)S(1)} all-to-all(f32[128,8,128]{2,1,0:T(8,128)S(1)} %get-tuple-element.73), channel_id=1, replica_groups=mesh['row'=8,'col'=16] {'row','col'}, dimensions={0} | all-to-all | bytes 1048576 | tf_op jit(solution)/shard_map/all_to_all | solution.py:339
  (104 shorter events, 42.5 us)
Async XLA Ops:
  3.9 20.7 %collective-permute-start.4 = (bf16[128,8192]{1,0:T(8,128)(2,1)}, bf16[128,8192]{1,0:T(8,128)(2,1)S(1)}, u32[]{:S(2)}, u32[]{:S(2)}) collective-permute-start(bf16[128,8192]{1,0:T(8,128)(2,1)} %dynamic-slice_bitcast_fusion), channel_id=1, source_target_pairs={{0,16},{1,17},{2,18},{3,19},{4,20},{5,21},{6,22},{7,23},{8,24},{9,... | collective-permute-start | bytes 6291464 | tf_op jit(solution)/shard_map/ppermute | solution.py:51
  6.9 9.0 %collective-permute-start.3 = (bf16[768,256]{1,0:T(8,128)(2,1)}, bf16[768,256]{1,0:T(8,128)(2,1)}, u32[]{:S(2)}, u32[]{:S(2)}) collective-permute-start(bf16[768,256]{1,0:T(8,128)(2,1)} %pad_maximum_fusion.6), channel_id=1, source_target_pairs={{0,12},{1,13},{2,14},{3,15},{4,8},{5,9},{6,10},{7,11},{8,4},{9,5},... | collective-permute-start | bytes 1179656 | tf_op jit(solution)/shard_map/ppermute | solution.py:51
  8.3 11.6 %collective-permute-start.1 = (bf16[768,256]{1,0:T(8,128)(2,1)}, bf16[768,256]{1,0:T(8,128)(2,1)}, u32[]{:S(2)}, u32[]{:S(2)}) collective-permute-start(bf16[768,256]{1,0:T(8,128)(2,1)} %pad_maximum_fusion.6), channel_id=1, source_target_pairs={{0,4},{1,5},{2,6},{3,7},{4,0},{5,1},{6,2},{7,3},{8,12},{9,13},{10,... | collective-permute-start | bytes 1179656 | tf_op jit(solution)/shard_map/ppermute | solution.py:51
  12.6 12.0 %collective-permute-start = (bf16[768,256]{1,0:T(8,128)(2,1)}, bf16[768,256]{1,0:T(8,128)(2,1)}, u32[]{:S(2)}, u32[]{:S(2)}) collective-permute-start(bf16[768,256]{1,0:T(8,128)(2,1)} %pad_maximum_fusion.5), channel_id=1, source_target_pairs={{0,1},{1,0},{2,3},{3,2},{4,5},{5,4},{6,7},{7,6},{8,9},{9,8},{10,11... | collective-permute-start | bytes 1179656 | tf_op jit(solution)/shard_map/ppermute | solution.py:51
  24.6 10.4 %collective-permute-start.8 = (bf16[512,256]{1,0:T(8,128)(2,1)S(1)}, bf16[512,256]{1,0:T(8,128)(2,1)S(1)}, u32[]{:S(2)}, u32[]{:S(2)}) collective-permute-start(bf16[512,256]{1,0:T(8,128)(2,1)S(1)} %bitcast_multiply_fusion), channel_id=1, source_target_pairs={{0,96},{1,97},{2,98},{3,99},{4,100},{5,101},{6,102},{7,103},{8,104... | collective-permute-start | bytes 786440 | tf_op jit(solution)/shard_map/ppermute | solution.py:51
  25.8 9.2 %collective-permute-start.7 = (bf16[512,256]{1,0:T(8,128)(2,1)S(1)}, bf16[512,256]{1,0:T(8,128)(2,1)}, u32[]{:S(2)}, u32[]{:S(2)}) collective-permute-start(bf16[512,256]{1,0:T(8,128)(2,1)S(1)} %bitcast_multiply_fusion), channel_id=1, source_target_pairs={{0,32},{1,33},{2,34},{3,35},{4,36},{5,37},{6,38},{7,39},{8,40},{9,... | collective-permute-start | bytes 786440 | tf_op jit(solution)/shard_map/ppermute | solution.py:51
  33.1 41.1 %collective-permute-start.21 = (bf16[128,8192]{1,0:T(8,128)(2,1)}, bf16[128,8192]{1,0:T(8,128)(2,1)}, u32[]{:S(2)}, u32[]{:S(2)}) collective-permute-start(bf16[128,8192]{1,0:T(8,128)(2,1)} %bitcast_select_fusion), channel_id=1, source_target_pairs={{0,32},{1,33},{2,34},{3,35},{4,36},{5,37},{6,38},{7,39},{8,40},{9,... | collective-permute-start | bytes 6291464 | tf_op jit(solution)/shard_map/ppermute | solution.py:51
  36.2 19.7 %collective-permute-start.12 = (bf16[4,512,256]{2,1,0:T(8,128)(2,1)S(1)}, bf16[4,512,256]{2,1,0:T(8,128)(2,1)}, u32[]{:S(2)}, u32[]{:S(2)}) collective-permute-start(bf16[4,512,256]{2,1,0:T(8,128)(2,1)S(1)} %pad_maximum_fusion.1.refs_3_), channel_id=1, source_target_pairs={{0,3},{1,2},{2,1},{3,0},{4,7},{5,6},{6,5},{7,4},{8,11},{9,10},{10,... | collective-permute-start | bytes 3145736 | tf_op jit(solution)/shard_map/ppermute | solution.py:51
  37.5 23.6 %collective-permute-start.11 = (bf16[4,512,256]{2,1,0:T(8,128)(2,1)S(1)}, bf16[4,512,256]{2,1,0:T(8,128)(2,1)S(1)}, u32[]{:S(2)}, u32[]{:S(2)}) collective-permute-start(bf16[4,512,256]{2,1,0:T(8,128)(2,1)S(1)} %pad_maximum_fusion.1.refs_3_), channel_id=1, source_target_pairs={{0,1},{1,0},{2,3},{3,2},{4,5},{5,4},{6,7},{7,6},{8,9},{9,8},{10,11... | collective-permute-start | bytes 3145736 | tf_op jit(solution)/shard_map/ppermute | solution.py:51
  41.5 19.6 %collective-permute-start.10 = (bf16[4,512,256]{2,1,0:T(8,128)(2,1)S(1)}, bf16[4,512,256]{2,1,0:T(8,128)(2,1)}, u32[]{:S(2)}, u32[]{:S(2)}) collective-permute-start(bf16[4,512,256]{2,1,0:T(8,128)(2,1)S(1)} %pad_maximum_fusion.refs_0_), channel_id=1, source_target_pairs={{0,12},{1,13},{2,14},{3,15},{4,8},{5,9},{6,10},{7,11},{8,4},{9,5},... | collective-permute-start | bytes 3145736 | tf_op jit(solution)/shard_map/ppermute | solution.py:51
  48.7 22.1 %collective-permute-start.9 = (bf16[4,512,256]{2,1,0:T(8,128)(2,1)S(1)}, bf16[4,512,256]{2,1,0:T(8,128)(2,1)}, u32[]{:S(2)}, u32[]{:S(2)}) collective-permute-start(bf16[4,512,256]{2,1,0:T(8,128)(2,1)S(1)} %pad_maximum_fusion.refs_0_), channel_id=1, source_target_pairs={{0,4},{1,5},{2,6},{3,7},{4,0},{5,1},{6,2},{7,3},{8,12},{9,13},{10,... | collective-permute-start | bytes 3145736 | tf_op jit(solution)/shard_map/ppermute | solution.py:51
  72.3 14.3 %collective-permute-start.14 = (bf16[4,512,256]{2,1,0:T(8,128)(2,1)}, bf16[4,512,256]{2,1,0:T(8,128)(2,1)S(1)}, u32[]{:S(2)}, u32[]{:S(2)}) collective-permute-start(bf16[4,512,256]{2,1,0:T(8,128)(2,1)} %collective-permute-done.9.refs_1_), channel_id=1, source_target_pairs={{0,12},{1,13},{2,14},{3,15},{4,8},{5,9},{6,10},{7,11},{8,4},{9,5},... | collective-permute-start | bytes 3145736 | tf_op jit(solution)/shard_map/ppermute | solution.py:51
  72.4 14.3 %collective-permute-start.15 = (bf16[4,512,256]{2,1,0:T(8,128)(2,1)S(1)}, bf16[4,512,256]{2,1,0:T(8,128)(2,1)S(1)}, u32[]{:S(2)}, u32[]{:S(2)}) collective-permute-start(bf16[4,512,256]{2,1,0:T(8,128)(2,1)S(1)} %collective-permute-done.11.refs_4_), channel_id=1, source_target_pairs={{0,3},{1,2},{2,1},{3,0},{4,7},{5,6},{6,5},{7,4},{8,11},{9,10},{10,... | collective-permute-start | bytes 3145736 | tf_op jit(solution)/shard_map/ppermute | solution.py:51
  77.3 41.6 %collective-permute-start.22 = (bf16[128,8192]{1,0:T(8,128)(2,1)}, bf16[128,8192]{1,0:T(8,128)(2,1)}, u32[]{:S(2)}, u32[]{:S(2)}) collective-permute-start(bf16[128,8192]{1,0:T(8,128)(2,1)} %broadcast_select_fusion.1), channel_id=1, source_target_pairs={{0,96},{1,97},{2,98},{3,99},{4,100},{5,101},{6,102},{7,103},{8,104... | collective-permute-start | bytes 6291464 | tf_op jit(solution)/shard_map/ppermute | solution.py:51
  86.8 10.3 %collective-permute-start.18 = (bf16[4,256,256]{2,1,0:T(8,128)(2,1)S(1)}, bf16[4,256,256]{2,1,0:T(8,128)(2,1)S(1)}, u32[]{:S(2)}, u32[]{:S(2)}) collective-permute-start(bf16[4,256,256]{2,1,0:T(8,128)(2,1)S(1)} %pad_maximum_fusion.4.refs_4_), channel_id=1, source_target_pairs={{0,1},{1,0},{2,3},{3,2},{4,5},{5,4},{6,7},{7,6},{8,9},{9,8},{10,11... | collective-permute-start | bytes 1572872 | tf_op jit(solution)/shard_map/ppermute | solution.py:51
  90.2 9.7 %collective-permute-start.17 = (bf16[4,256,256]{2,1,0:T(8,128)(2,1)S(1)}, bf16[4,256,256]{2,1,0:T(8,128)(2,1)S(1)}, u32[]{:S(2)}, u32[]{:S(2)}) collective-permute-start(bf16[4,256,256]{2,1,0:T(8,128)(2,1)S(1)} %pad_maximum_fusion.3.refs_0_), channel_id=1, source_target_pairs={{0,4},{1,5},{2,6},{3,7},{4,0},{5,1},{6,2},{7,3},{8,12},{9,13},{10,... | collective-permute-start | bytes 1572872 | tf_op jit(solution)/shard_map/ppermute | solution.py:51
  92.5 21.4 %collective-permute-start.20 = (bf16[2,512,256]{2,1,0:T(8,128)(2,1)S(1)}, bf16[2,512,256]{2,1,0:T(8,128)(2,1)S(1)}, u32[]{:S(2)}, u32[]{:S(2)}) collective-permute-start(bf16[2,512,256]{2,1,0:T(8,128)(2,1)S(1)} %response.3.refs_8_), channel_id=1, source_target_pairs={{0,96},{1,97},{2,98},{3,99},{4,100},{5,101},{6,102},{7,103},{8,104... | collective-permute-start | bytes 1572872 | tf_op jit(solution)/shard_map/ppermute | solution.py:51
  92.8 26.0 %collective-permute-start.19 = (bf16[2,512,256]{2,1,0:T(8,128)(2,1)S(1)}, bf16[2,512,256]{2,1,0:T(8,128)(2,1)}, u32[]{:S(2)}, u32[]{:S(2)}) collective-permute-start(bf16[2,512,256]{2,1,0:T(8,128)(2,1)S(1)} %response.3.refs_8_), channel_id=1, source_target_pairs={{0,32},{1,33},{2,34},{3,35},{4,36},{5,37},{6,38},{7,39},{8,40},{9,... | collective-permute-start | bytes 1572872 | tf_op jit(solution)/shard_map/ppermute | solution.py:51
  97.1 22.1 %collective-permute-start.25 = (bf16[4,256,256]{2,1,0:T(8,128)(2,1)S(1)}, bf16[4,256,256]{2,1,0:T(8,128)(2,1)}, u32[]{:S(2)}, u32[]{:S(2)}) collective-permute-start(bf16[4,256,256]{2,1,0:T(8,128)(2,1)S(1)} %pad_maximum_fusion.4.refs_4_), channel_id=1, source_target_pairs={{0,3},{1,2},{2,1},{3,0},{4,7},{5,6},{6,5},{7,4},{8,11},{9,10},{10,... | collective-permute-start | bytes 1572872 | tf_op jit(solution)/shard_map/ppermute | solution.py:51
  99.9 20.6 %collective-permute-start.23 = (bf16[4,256,256]{2,1,0:T(8,128)(2,1)S(1)}, bf16[4,256,256]{2,1,0:T(8,128)(2,1)}, u32[]{:S(2)}, u32[]{:S(2)}) collective-permute-start(bf16[4,256,256]{2,1,0:T(8,128)(2,1)S(1)} %pad_maximum_fusion.3.refs_0_), channel_id=1, source_target_pairs={{0,12},{1,13},{2,14},{3,15},{4,8},{5,9},{6,10},{7,11},{8,4},{9,5},... | collective-permute-start | bytes 1572872 | tf_op jit(solution)/shard_map/ppermute | solution.py:51
  113.9 9.4 %collective-permute-start.27 = (bf16[2,512,256]{2,1,0:T(8,128)(2,1)S(1)}, bf16[2,512,256]{2,1,0:T(8,128)(2,1)}, u32[]{:S(2)}, u32[]{:S(2)}) collective-permute-start(bf16[2,512,256]{2,1,0:T(8,128)(2,1)S(1)} %response.3.refs_8_), channel_id=1, source_target_pairs={{0,16},{1,17},{2,18},{3,19},{4,20},{5,21},{6,22},{7,23},{8,24},{9,... | collective-permute-start | bytes 1572872 | tf_op jit(solution)/shard_map/ppermute | solution.py:51
  118.9 10.6 %collective-permute-start.24 = (bf16[4,256,256]{2,1,0:T(8,128)(2,1)S(1)}, bf16[4,256,256]{2,1,0:T(8,128)(2,1)S(1)}, u32[]{:S(2)}, u32[]{:S(2)}) collective-permute-start(bf16[4,256,256]{2,1,0:T(8,128)(2,1)S(1)} %collective-permute-done.17.refs_1_), channel_id=1, source_target_pairs={{0,12},{1,13},{2,14},{3,15},{4,8},{5,9},{6,10},{7,11},{8,4},{9,5},... | collective-permute-start | bytes 1572872 | tf_op jit(solution)/shard_map/ppermute | solution.py:51
  119.1 12.3 %collective-permute-start.26 = (bf16[4,256,256]{2,1,0:T(8,128)(2,1)S(1)}, bf16[4,256,256]{2,1,0:T(8,128)(2,1)S(1)}, u32[]{:S(2)}, u32[]{:S(2)}) collective-permute-start(bf16[4,256,256]{2,1,0:T(8,128)(2,1)S(1)} %collective-permute-done.18.refs_5_), channel_id=1, source_target_pairs={{0,3},{1,2},{2,1},{3,0},{4,7},{5,6},{6,5},{7,4},{8,11},{9,10},{10,... | collective-permute-start | bytes 1572872 | tf_op jit(solution)/shard_map/ppermute | solution.py:51
  120.5 10.9 %collective-permute-start.28 = (bf16[2,512,256]{2,1,0:T(8,128)(2,1)}, bf16[2,512,256]{2,1,0:T(8,128)(2,1)S(1)}, u32[]{:S(2)}, u32[]{:S(2)}) collective-permute-start(bf16[2,512,256]{2,1,0:T(8,128)(2,1)} %collective-permute-done.19.refs_9_), channel_id=1, source_target_pairs={{0,16},{1,17},{2,18},{3,19},{4,20},{5,21},{6,22},{7,23},{8,24},{9,... | collective-permute-start | bytes 1572872 | tf_op jit(solution)/shard_map/ppermute | solution.py:51
  (22 other events, 230.3 us)

commit v5 on v4

--- a/solution.py
+++ b/solution.py
@@ -242,14 +242,13 @@
     both_z = jnp.concatenate([trial_vectors[0], p_valence[:2 * BS]])
     both_y = jnp.concatenate([trial_vectors[1], p_valence[2 * BS:]])
 
-    theirs = lax.dynamic_slice_in_dim(orbitals, first + 1 - core, 1, 0)[0]
-    z_first, y_first, z_second, y_second, given, conduction, first = together(
+    mine, theirs = (lax.dynamic_slice_in_dim(orbitals, first + at, 1, 0)[0] for at in (core, 1 - core))
+    seed = jnp.where(core == z // 2, mine, send(theirs, OTHER_CORE))
+    z_first, y_first, z_second, y_second, seed, conduction = together(
         send(both_z, along("z", 0)), send(both_y, along("y", 0)),
         send(both_z, along("z", 1)), send(both_y, along("y", 1)),
-        send(theirs, OTHER_CORE), conduction, first,
-    )
-    mine = lax.dynamic_slice_in_dim(orbitals, first + core, 1, 0)[0]
-    seed = jnp.where(core == z // 2, mine, given)
+        seed, conduction,
+    )
     reached = send(seed, along("x", 0))
     z_third, y_third, x_first, x_second = together(
         send(z_first, along("z", 1)), send(y_first, along("y", 1)), *neighbours(conduction, "x")
@@ -290,11 +289,14 @@
 
     valences = [jnp.stack(ends[:4]), jnp.stack(ends[4:8])]
     valences = [valences[0], send(valences[0], along("y", 0)), valences[1], send(valences[1], along("z", 0))]
-    responses = gather(response, "x")
-    valences[1], valences[3], *responses[1:3], arrived = together(valences[1], valences[3], *responses[1:3], arrived)
-    for at, axis in ((0, "y"), (4, "z")):
-        valences[at + 2:at + 2] = [send(valences[at], along(axis, 1)), send(valences[at + 1], along(axis, 1))]
-    swapped = [send(piece, OTHER_CORE) for piece in responses]
+    responses = [response, *neighbours(response, "x"), None]
+    valences = [
+        valences[0], valences[1], send(valences[0], along("y", 1)), send(valences[1], along("y", 1)),
+        valences[2], valences[3], send(valences[2], along("z", 1)), send(valences[3], along("z", 1)),
+    ]
+    *valences, responses[1], responses[2], arrived = together(*valences, *responses[1:3], arrived)
+    responses[3] = send(responses[1], along("x", 1))
+    swapped = [send(piece, OTHER_CORE) for piece in responses[:3]]
     near = jnp.where((x == y) | (x ^ (1 + 2 * core) == y), passed, arrived)
     far = send(near, OTHER_CORE)
     mask_v = mask_valence.reshape(-1)
@@ -316,6 +318,9 @@
         compiler_params=pltpu.CompilerParams(vmem_limit_bytes=20 * 2**20),
         cost_estimate=pl.CostEstimate(flops=2**36, bytes_accessed=8 * 2**20, transcendentals=0),
     )(idx, mask_v, *valences, *responses[:3], *swapped[:3])
+
+    responses[3], early = together(responses[3], early)
+    swapped.append(send(responses[3], OTHER_CORE))
 
     kernel, density = pl.pallas_call(
         density_kernel,

time: 165 us -> 159 us (0.964)
  waiting for transfers between devices: 57.1 us -> 49.2 us
  local copies, waits for them, and re-layouts: 13.7 us -> 8.9 us
  starting transfers between devices: 42.7 us -> 47.1 us
  other arithmetic: 12.5 us -> 14.2 us
    ppermute x33, waiting for transfers between devices: 57.1 us -> 49.2 us  [send(): return lax.ppermute(value, AXES, route)]
    ppermute x33, starting transfers between devices: 42.7 us -> 47.1 us  [send(): return lax.ppermute(value, AXES, route)]
    slice x7 -> x10, local copies, waits for them, and re-layouts: 4.58 us -> 1.85 us  [local(): piece[4 * BS:]]
  transfers between devices with their start and end apart: 33 -> 33, of which waited for: 12 -> 12; matrix products, arithmetic and copies ran while one was open for 14% -> 12% of each run, Pallas kernels for 6% -> 7%
where the time goes in v5:
time: 159 us; the launch traced here: 158 us
  waiting for transfers between devices  49.2 us (31%)
  starting transfers between devices  47.1 us (30%)
  blocking collectives  20.9 us (13%)
  Pallas kernels  16.4 us (10%)
  other arithmetic  14.2 us (9%)
  local copies, waits for them, and re-layouts  8.9 us (6%)
    ppermute x33, waiting for transfers between devices, send(): return lax.ppermute(value, AXES, route)  49.2 us
    ppermute x33, starting transfers between devices, send(): return lax.ppermute(value, AXES, route)  47.1 us
    all_to_all x1, blocking collectives, local(): terms = lax.all_to_all(density, AXES, 0, 0, tiled=True)  20.9 us
    pallas_call x2, Pallas kernels, local(): pl.pallas_call(functools.partial(response_kernel, part), name='response',...  6.06 us
    pallas_call x1, Pallas kernels, local(): pl.pallas_call(density_kernel, name='density', out_shape=(jax.ShapeDtypeS...  5.88 us
    pallas_call x1, Pallas kernels, local(): pl.pallas_call(early_kernel, name='early', out_shape=(jax.ShapeDtypeStruc...  4.51 us
    select_n x1, other arithmetic, local(): seed = jnp.where(core == z // 2, mine, send(theirs, OTHER_CORE))  3.89 us
  transfers between devices with their start and end apart: 33, of which 12 were waited for; matrix products, arithmetic and copies ran while one was open for 12% of the time, Pallas kernels for 7%

profile of v5, /device:TPU:1, one launch (start us, length us, event | category | flops | bytes accessed | tf_op | source)
XLA Modules:
  0.0 157.7 jit_solution(17622249715384737867)
XLA Ops:
  7.0 1.9 %collective-permute-start.1 = (bf16[768,256]{1,0:T(8,128)(2,1)}, bf16[768,256]{1,0:T(8,128)(2,1)}, u32[]{:S(2)}, u32[]{:S(2)}) collective-permute-start(bf16[768,256]{1,0:T(8,128)(2,1)} %pad_maximum_fusion.6), channel_id=1, source_target_pairs={{0,4},{1,5},{2,6},{3,7},{4,0},{5,1},{6,2},{7,3},{8,12},{9,13},{10,... | collective-permute-start | bytes 1179656 | tf_op jit(solution)/shard_map/ppermute | solution.py:51
  11.3 2.3 %collective-permute-start = (bf16[768,256]{1,0:T(8,128)(2,1)}, bf16[768,256]{1,0:T(8,128)(2,1)}, u32[]{:S(2)}, u32[]{:S(2)}) collective-permute-start(bf16[768,256]{1,0:T(8,128)(2,1)} %pad_maximum_fusion.5), channel_id=1, source_target_pairs={{0,1},{1,0},{2,3},{3,2},{4,5},{5,4},{6,7},{7,6},{8,9},{9,8},{10,11... | collective-permute-start | bytes 1179656 | tf_op jit(solution)/shard_map/ppermute | solution.py:51
  15.6 3.9 %bitcast_select_fusion = bf16[128,8192]{1,0:T(8,128)(2,1)} fusion(bf16[128,8192]{1,0:T(8,128)(2,1)} %collective-permute-done.4, bf16[4,128,8192]{2,1,0:T(8,128)(2,1)} %refs_4_.1, s32[]{:T(128)S(6)} %select_n.64, pred[]{:T(512)S(6)} %eq.14), kind=kLoop, calls=%fused_computation | loop fusion | flops 1048576 | bytes 6291461 | tf_op jit(solution)/shard_map/jit(_where)/select_n | solution.py:246
  19.5 3.8 %collective-permute-done = bf16[768,256]{1,0:T(8,128)(2,1)} collective-permute-done((bf16[768,256]{1,0:T(8,128)(2,1)}, bf16[768,256]{1,0:T(8,128)(2,1)}, u32[]{:S(2)}, u32[]{:S(2)}) %collective-permute-start) | collective-permute-done | bytes 393248 | tf_op jit(solution)/shard_map/ppermute | solution.py:51
  30.5 3.1 %collective-permute-done.7 = bf16[512,256]{1,0:T(8,128)(2,1)S(1)} collective-permute-done((bf16[512,256]{1,0:T(8,128)(2,1)S(1)}, bf16[512,256]{1,0:T(8,128)(2,1)S(1)}, u32[]{:S(2)}, u32[]{:S(2)}) %collective-permute-start.7) | collective-permute-done | bytes 262176 | tf_op jit(solution)/shard_map/ppermute | solution.py:51
  35.8 2.5 %collective-permute-start.11 = (bf16[4,512,256]{2,1,0:T(8,128)(2,1)S(1)}, bf16[4,512,256]{2,1,0:T(8,128)(2,1)S(1)}, u32[]{:S(2)}, u32[]{:S(2)}) collective-permute-start(bf16[4,512,256]{2,1,0:T(8,128)(2,1)S(1)} %pad_maximum_fusion.1.refs_3_), channel_id=1, source_target_pairs={{0,1},{1,0},{2,3},{3,2},{4,5},{5,4},{6,7},{7,6},{8,9},{9,8},{10,11... | collective-permute-start | bytes 3145736 | tf_op jit(solution)/shard_map/ppermute | solution.py:51
  38.9 7.9 %collective-permute-done.13 = bf16[512,256]{1,0:T(8,128)(2,1)S(1)} collective-permute-done((bf16[512,256]{1,0:T(8,128)(2,1)S(1)}, bf16[512,256]{1,0:T(8,128)(2,1)S(1)}, u32[]{:S(2)}, u32[]{:S(2)}) %collective-permute-start.13) | collective-permute-done | bytes 262176 | tf_op jit(solution)/shard_map/ppermute | solution.py:51
  50.3 4.2 %collective-permute-done.12.refs_5_ = bf16[4,512,256]{2,1,0:T(8,128)(2,1)} collective-permute-done((bf16[4,512,256]{2,1,0:T(8,128)(2,1)S(1)}, bf16[4,512,256]{2,1,0:T(8,128)(2,1)}, u32[]{:S(2)}, u32[]{:S(2)}) %collective-permute-start.12) | collective-permute-done | bytes 1048608 | tf_op jit(solution)/shard_map/ppermute | solution.py:51
  54.5 5.1 %collective-permute-done.11.refs_4_ = bf16[4,512,256]{2,1,0:T(8,128)(2,1)S(1)} collective-permute-done((bf16[4,512,256]{2,1,0:T(8,128)(2,1)S(1)}, bf16[4,512,256]{2,1,0:T(8,128)(2,1)S(1)}, u32[]{:S(2)}, u32[]{:S(2)}) %collective-permute-start.11) | collective-permute-done | bytes 1048608 | tf_op jit(solution)/shard_map/ppermute | solution.py:51
  59.6 8.3 %collective-permute-done.9.refs_1_ = bf16[4,512,256]{2,1,0:T(8,128)(2,1)} collective-permute-done((bf16[4,512,256]{2,1,0:T(8,128)(2,1)S(1)}, bf16[4,512,256]{2,1,0:T(8,128)(2,1)}, u32[]{:S(2)}, u32[]{:S(2)}) %collective-permute-start.9) | collective-permute-done | bytes 1048608 | tf_op jit(solution)/shard_map/ppermute | solution.py:51
  71.2 3.2 %broadcast_select_fusion.1 = bf16[128,8192]{1,0:T(8,128)(2,1)} fusion(bf16[128,8192]{1,0:T(8,128)(2,1)} %bitcast_select_fusion, bf16[128,8192]{1,0:T(8,128)(2,1)} %collective-permute-done.25, pred[]{:T(512)S(6)} %eq.15), kind=kLoop, calls=%fused_computation.3 | loop fusion | flops 1048576 | bytes 6291457 | tf_op jit(solution)/shard_map/jit(_where)/select_n | solution.py:267
  74.9 3.8 %response.2.refs_4_ = f32[2,512,256]{2,1,0:T(8,128)S(1)} custom-call(s32[6]{0:T(128)S(1)} %stack.96.idx, s32[1024]{0:T(1024)S(1)} %reshape.17.mask, bf16[4,512,256]{2,1,0:T(8,128)(2,1)S(1)} %pad_maximum_fusion.refs_0_, bf16[4,512,256]{2,1,0:T(8,128)(2,1)} %collective-permute-done.9.refs_1_, bf16[4,512,256]{2,1,0:T(8,128)(2,1)} %collective-permute-done.10.refs_2_, ...), custom_call_target="tpu_custom_call" | custom-call | flops 4294967296 | bytes 9437184 | tf_op jit(solution)/shard_map/response/pallas_call | solution.py:279
  78.7 5.0 %collective-permute-done.14.refs_0_ = bf16[4,512,256]{2,1,0:T(8,128)(2,1)S(1)} collective-permute-done((bf16[4,512,256]{2,1,0:T(8,128)(2,1)}, bf16[4,512,256]{2,1,0:T(8,128)(2,1)S(1)}, u32[]{:S(2)}, u32[]{:S(2)}) %collective-permute-start.14) | collective-permute-done | bytes 1048608 | tf_op jit(solution)/shard_map/ppermute | solution.py:51
  85.5 2.9 %collective-permute-start.20 = (bf16[4,256,256]{2,1,0:T(8,128)(2,1)S(1)}, bf16[4,256,256]{2,1,0:T(8,128)(2,1)S(1)}, u32[]{:S(2)}, u32[]{:S(2)}) collective-permute-start(bf16[4,256,256]{2,1,0:T(8,128)(2,1)S(1)} %pad_maximum_fusion.4.refs_4_), channel_id=1, source_target_pairs={{0,1},{1,0},{2,3},{3,2},{4,5},{5,4},{6,7},{7,6},{8,9},{9,8},{10,11... | collective-permute-start | bytes 1572872 | tf_op jit(solution)/shard_map/ppermute | solution.py:51
  90.7 2.2 %response.3.refs_8_ = bf16[2,512,256]{2,1,0:T(8,128)(2,1)} custom-call(s32[6]{0:T(128)S(1)} %stack.96.idx, s32[1024]{0:T(1024)S(1)} %reshape.17.mask, bf16[4,512,256]{2,1,0:T(8,128)(2,1)S(1)} %collective-permute-done.14.refs_0_, bf16[4,512,256]{2,1,0:T(8,128)(2,1)S(1)} %collective-permute-done.15.refs_1_, ...), custom_call_target="tpu_custom_call" | custom-call | flops 68719476736 | bytes 9437184 | tf_op jit(solution)/shard_map/response/pallas_call | solution.py:279
  93.3 6.0 %collective-permute-done.20.refs_5_ = bf16[4,256,256]{2,1,0:T(8,128)(2,1)S(1)} collective-permute-done((bf16[4,256,256]{2,1,0:T(8,128)(2,1)S(1)}, bf16[4,256,256]{2,1,0:T(8,128)(2,1)S(1)}, u32[]{:S(2)}, u32[]{:S(2)}) %collective-permute-start.20) | collective-permute-done | bytes 524320 | tf_op jit(solution)/shard_map/ppermute | solution.py:51
  101.1 2.4 %collective-permute-done.17.refs_1_ = bf16[4,256,256]{2,1,0:T(8,128)(2,1)} collective-permute-done((bf16[4,256,256]{2,1,0:T(8,128)(2,1)S(1)}, bf16[4,256,256]{2,1,0:T(8,128)(2,1)}, u32[]{:S(2)}, u32[]{:S(2)}) %collective-permute-start.17) | collective-permute-done | bytes 524320 | tf_op jit(solution)/shard_map/ppermute | solution.py:51
  105.4 10.8 %collective-permute-start.27 = (bf16[2,512,256]{2,1,0:T(8,128)(2,1)}, bf16[2,512,256]{2,1,0:T(8,128)(2,1)S(1)}, u32[]{:S(2)}, u32[]{:S(2)}) collective-permute-start(bf16[2,512,256]{2,1,0:T(8,128)(2,1)} %response.3.refs_8_), channel_id=1, source_target_pairs={{0,16},{1,17},{2,18},{3,19},{4,20},{5,21},{6,22},{7,23},{8,24},{9,... | collective-permute-start | bytes 1572872 | tf_op jit(solution)/shard_map/ppermute | solution.py:51
  116.2 2.4 %collective-permute-start.28 = (bf16[2,512,256]{2,1,0:T(8,128)(2,1)}, bf16[2,512,256]{2,1,0:T(8,128)(2,1)S(1)}, u32[]{:S(2)}, u32[]{:S(2)}) collective-permute-start(bf16[2,512,256]{2,1,0:T(8,128)(2,1)} %collective-permute-done.23.refs_9_), channel_id=1, source_target_pairs={{0,16},{1,17},{2,18},{3,19},{4,20},{5,21},{6,22},{7,23},{8,24},{9,... | collective-permute-start | bytes 1572872 | tf_op jit(solution)/shard_map/ppermute | solution.py:51
  118.7 2.0 %broadcast_select_fusion.refs_5_ = bf16[128,8192]{1,0:T(8,128)(2,1)S(1)} fusion(bf16[128,8192]{1,0:T(8,128)(2,1)} %broadcast_select_fusion.1, bf16[128,8192]{1,0:T(8,128)(2,1)} %collective-permute-done.26, pred[]{:T(512)S(6)} %or.3), kind=kLoop, calls=%fused_computation.2 | loop fusion | flops 1048576 | bytes 6291457 | tf_op jit(solution)/shard_map/jit(_where)/select_n | solution.py:300
  121.3 4.5 %early.1 = (f32[2,512,256]{2,1,0:T(8,128)S(1)}, bf16[2,4,256,256]{3,2,1,0:T(8,128)(2,1)S(1)}) custom-call(s32[6]{0:T(128)S(1)} %stack.96.idx, s32[1024]{0:T(1024)S(1)} %reshape.18.mask_v, bf16[4,256,256]{2,1,0:T(8,128)(2,1)S(1)} %pad_maximum_fusion.3.refs_0_, bf16[4,256,256]{2,1,0:T(8,128)(2,1)} %collective-permute-done.17.refs_1_, ...), custom_call_target="tpu_custom_call" | custom-call | flops 68719476736 | bytes 8388608 | tf_op jit(solution)/shard_map/early/pallas_call | solution.py:304
  125.8 2.9 %collective-permute-start.31 = (bf16[2,512,256]{2,1,0:T(8,128)(2,1)S(1)}, bf16[2,512,256]{2,1,0:T(8,128)(2,1)S(1)}, u32[]{:S(2)}, u32[]{:S(2)}) collective-permute-start(bf16[2,512,256]{2,1,0:T(8,128)(2,1)S(1)} %collective-permute-done.30.refs_1_), channel_id=1, source_target_pairs={{0,16},{1,17},{2,18},{3,19},{4,20},{5,21},{6,22},{7,23},{8,24},{9,... | collective-permute-start | bytes 1572872 | tf_op jit(solution)/shard_map/ppermute | solution.py:51
  130.2 5.9 %density.1 = (bf16[2,512,256]{2,1,0:T(8,128)(2,1)}, f32[128,8,128]{2,1,0:T(8,128)S(1)}) custom-call(s32[6]{0:T(128)S(1)} %stack.96.idx, s32[1024]{0:T(1024)S(1)} %reshape.17.mask, s32[1024]{0:T(1024)S(1)} %reshape.18.mask_v, s32[32]{0:T(128)S(1)} %copy-done, bf16[2,4,256,256]{3,2,1,0:T(8,128)(2,1)S(1)} %get-tuple-element.81.refs_0_, ...), custom_call_target="tpu_custom_call" | custom-call | flops 8589934592 | bytes 23068672 | tf_op jit(solution)/shard_map/density/pallas_call | solution.py:325
  136.1 20.9 %all_to_all.5 = f32[128,8,128]{2,1,0:T(8,128)S(1)} all-to-all(f32[128,8,128]{2,1,0:T(8,128)S(1)} %get-tuple-element.87), channel_id=1, replica_groups=mesh['row'=8,'col'=16] {'row','col'}, dimensions={0} | all-to-all | bytes 1048576 | tf_op jit(solution)/shard_map/all_to_all | solution.py:344
  (115 shorter events, 39.0 us)
Async XLA Ops:
  2.5 13.1 %collective-permute-start.4 = (bf16[128,8192]{1,0:T(8,128)(2,1)S(1)}, bf16[128,8192]{1,0:T(8,128)(2,1)}, u32[]{:S(2)}, u32[]{:S(2)}) collective-permute-start(bf16[128,8192]{1,0:T(8,128)(2,1)S(1)} %dynamic-slice_bitcast_fusion), channel_id=1, source_target_pairs={{0,16},{1,17},{2,18},{3,19},{4,20},{5,21},{6,22},{7,23},{8,24},{9,... | collective-permute-start | bytes 6291464 | tf_op jit(solution)/shard_map/ppermute | solution.py:51
  5.6 13.8 %collective-permute-start.3 = (bf16[768,256]{1,0:T(8,128)(2,1)}, bf16[768,256]{1,0:T(8,128)(2,1)S(1)}, u32[]{:S(2)}, u32[]{:S(2)}) collective-permute-start(bf16[768,256]{1,0:T(8,128)(2,1)} %pad_maximum_fusion.6), channel_id=1, source_target_pairs={{0,12},{1,13},{2,14},{3,15},{4,8},{5,9},{6,10},{7,11},{8,4},{9,5},... | collective-permute-start | bytes 1179656 | tf_op jit(solution)/shard_map/ppermute | solution.py:51
  7.0 12.5 %collective-permute-start.1 = (bf16[768,256]{1,0:T(8,128)(2,1)}, bf16[768,256]{1,0:T(8,128)(2,1)}, u32[]{:S(2)}, u32[]{:S(2)}) collective-permute-start(bf16[768,256]{1,0:T(8,128)(2,1)} %pad_maximum_fusion.6), channel_id=1, source_target_pairs={{0,4},{1,5},{2,6},{3,7},{4,0},{5,1},{6,2},{7,3},{8,12},{9,13},{10,... | collective-permute-start | bytes 1179656 | tf_op jit(solution)/shard_map/ppermute | solution.py:51
  9.7 9.8 %collective-permute-start.2 = (bf16[768,256]{1,0:T(8,128)(2,1)}, bf16[768,256]{1,0:T(8,128)(2,1)S(1)}, u32[]{:S(2)}, u32[]{:S(2)}) collective-permute-start(bf16[768,256]{1,0:T(8,128)(2,1)} %pad_maximum_fusion.5), channel_id=1, source_target_pairs={{0,3},{1,2},{2,1},{3,0},{4,7},{5,6},{6,5},{7,4},{8,11},{9,10},{10,... | collective-permute-start | bytes 1179656 | tf_op jit(solution)/shard_map/ppermute | solution.py:51
  11.3 12.0 %collective-permute-start = (bf16[768,256]{1,0:T(8,128)(2,1)}, bf16[768,256]{1,0:T(8,128)(2,1)}, u32[]{:S(2)}, u32[]{:S(2)}) collective-permute-start(bf16[768,256]{1,0:T(8,128)(2,1)} %pad_maximum_fusion.5), channel_id=1, source_target_pairs={{0,1},{1,0},{2,3},{3,2},{4,5},{5,4},{6,7},{7,6},{8,9},{9,8},{10,11... | collective-permute-start | bytes 1179656 | tf_op jit(solution)/shard_map/ppermute | solution.py:51
  24.5 9.1 %collective-permute-start.7 = (bf16[512,256]{1,0:T(8,128)(2,1)S(1)}, bf16[512,256]{1,0:T(8,128)(2,1)S(1)}, u32[]{:S(2)}, u32[]{:S(2)}) collective-permute-start(bf16[512,256]{1,0:T(8,128)(2,1)S(1)} %bitcast_multiply_fusion), channel_id=1, source_target_pairs={{0,32},{1,33},{2,34},{3,35},{4,36},{5,37},{6,38},{7,39},{8,40},{9,... | collective-permute-start | bytes 786440 | tf_op jit(solution)/shard_map/ppermute | solution.py:51
  28.6 42.7 %collective-permute-start.25 = (bf16[128,8192]{1,0:T(8,128)(2,1)}, bf16[128,8192]{1,0:T(8,128)(2,1)}, u32[]{:S(2)}, u32[]{:S(2)}) collective-permute-start(bf16[128,8192]{1,0:T(8,128)(2,1)} %bitcast_select_fusion), channel_id=1, source_target_pairs={{0,32},{1,33},{2,34},{3,35},{4,36},{5,37},{6,38},{7,39},{8,40},{9,... | collective-permute-start | bytes 6291464 | tf_op jit(solution)/shard_map/ppermute | solution.py:51
  34.4 20.1 %collective-permute-start.12 = (bf16[4,512,256]{2,1,0:T(8,128)(2,1)S(1)}, bf16[4,512,256]{2,1,0:T(8,128)(2,1)}, u32[]{:S(2)}, u32[]{:S(2)}) collective-permute-start(bf16[4,512,256]{2,1,0:T(8,128)(2,1)S(1)} %pad_maximum_fusion.1.refs_3_), channel_id=1, source_target_pairs={{0,3},{1,2},{2,1},{3,0},{4,7},{5,6},{6,5},{7,4},{8,11},{9,10},{10,... | collective-permute-start | bytes 3145736 | tf_op jit(solution)/shard_map/ppermute | solution.py:51
  35.8 23.8 %collective-permute-start.11 = (bf16[4,512,256]{2,1,0:T(8,128)(2,1)S(1)}, bf16[4,512,256]{2,1,0:T(8,128)(2,1)S(1)}, u32[]{:S(2)}, u32[]{:S(2)}) collective-permute-start(bf16[4,512,256]{2,1,0:T(8,128)(2,1)S(1)} %pad_maximum_fusion.1.refs_3_), channel_id=1, source_target_pairs={{0,1},{1,0},{2,3},{3,2},{4,5},{5,4},{6,7},{7,6},{8,9},{9,8},{10,11... | collective-permute-start | bytes 3145736 | tf_op jit(solution)/shard_map/ppermute | solution.py:51
  38.8 20.7 %collective-permute-start.10 = (bf16[4,512,256]{2,1,0:T(8,128)(2,1)S(1)}, bf16[4,512,256]{2,1,0:T(8,128)(2,1)}, u32[]{:S(2)}, u32[]{:S(2)}) collective-permute-start(bf16[4,512,256]{2,1,0:T(8,128)(2,1)S(1)} %pad_maximum_fusion.refs_0_), channel_id=1, source_target_pairs={{0,12},{1,13},{2,14},{3,15},{4,8},{5,9},{6,10},{7,11},{8,4},{9,5},... | collective-permute-start | bytes 3145736 | tf_op jit(solution)/shard_map/ppermute | solution.py:51
  47.5 20.3 %collective-permute-start.9 = (bf16[4,512,256]{2,1,0:T(8,128)(2,1)S(1)}, bf16[4,512,256]{2,1,0:T(8,128)(2,1)}, u32[]{:S(2)}, u32[]{:S(2)}) collective-permute-start(bf16[4,512,256]{2,1,0:T(8,128)(2,1)S(1)} %pad_maximum_fusion.refs_0_), channel_id=1, source_target_pairs={{0,4},{1,5},{2,6},{3,7},{4,0},{5,1},{6,2},{7,3},{8,12},{9,13},{10,... | collective-permute-start | bytes 3145736 | tf_op jit(solution)/shard_map/ppermute | solution.py:51
  69.3 14.3 %collective-permute-start.14 = (bf16[4,512,256]{2,1,0:T(8,128)(2,1)}, bf16[4,512,256]{2,1,0:T(8,128)(2,1)S(1)}, u32[]{:S(2)}, u32[]{:S(2)}) collective-permute-start(bf16[4,512,256]{2,1,0:T(8,128)(2,1)} %collective-permute-done.9.refs_1_), channel_id=1, source_target_pairs={{0,12},{1,13},{2,14},{3,15},{4,8},{5,9},{6,10},{7,11},{8,4},{9,5},... | collective-permute-start | bytes 3145736 | tf_op jit(solution)/shard_map/ppermute | solution.py:51
  69.4 14.4 %collective-permute-start.15 = (bf16[4,512,256]{2,1,0:T(8,128)(2,1)S(1)}, bf16[4,512,256]{2,1,0:T(8,128)(2,1)S(1)}, u32[]{:S(2)}, u32[]{:S(2)}) collective-permute-start(bf16[4,512,256]{2,1,0:T(8,128)(2,1)S(1)} %collective-permute-done.11.refs_4_), channel_id=1, source_target_pairs={{0,3},{1,2},{2,1},{3,0},{4,7},{5,6},{6,5},{7,4},{8,11},{9,10},{10,... | collective-permute-start | bytes 3145736 | tf_op jit(solution)/shard_map/ppermute | solution.py:51
  74.4 41.7 %collective-permute-start.26 = (bf16[128,8192]{1,0:T(8,128)(2,1)}, bf16[128,8192]{1,0:T(8,128)(2,1)}, u32[]{:S(2)}, u32[]{:S(2)}) collective-permute-start(bf16[128,8192]{1,0:T(8,128)(2,1)} %broadcast_select_fusion.1), channel_id=1, source_target_pairs={{0,96},{1,97},{2,98},{3,99},{4,100},{5,101},{6,102},{7,103},{8,104... | collective-permute-start | bytes 6291464 | tf_op jit(solution)/shard_map/ppermute | solution.py:51
  85.5 13.8 %collective-permute-start.20 = (bf16[4,256,256]{2,1,0:T(8,128)(2,1)S(1)}, bf16[4,256,256]{2,1,0:T(8,128)(2,1)S(1)}, u32[]{:S(2)}, u32[]{:S(2)}) collective-permute-start(bf16[4,256,256]{2,1,0:T(8,128)(2,1)S(1)} %pad_maximum_fusion.4.refs_4_), channel_id=1, source_target_pairs={{0,1},{1,0},{2,3},{3,2},{4,5},{5,4},{6,7},{7,6},{8,9},{9,8},{10,11... | collective-permute-start | bytes 1572872 | tf_op jit(solution)/shard_map/ppermute | solution.py:51
  88.6 12.6 %collective-permute-start.18 = (bf16[4,256,256]{2,1,0:T(8,128)(2,1)S(1)}, bf16[4,256,256]{2,1,0:T(8,128)(2,1)S(1)}, u32[]{:S(2)}, u32[]{:S(2)}) collective-permute-start(bf16[4,256,256]{2,1,0:T(8,128)(2,1)S(1)} %pad_maximum_fusion.3.refs_0_), channel_id=1, source_target_pairs={{0,12},{1,13},{2,14},{3,15},{4,8},{5,9},{6,10},{7,11},{8,4},{9,5},... | collective-permute-start | bytes 1572872 | tf_op jit(solution)/shard_map/ppermute | solution.py:51
  89.9 13.6 %collective-permute-start.17 = (bf16[4,256,256]{2,1,0:T(8,128)(2,1)S(1)}, bf16[4,256,256]{2,1,0:T(8,128)(2,1)}, u32[]{:S(2)}, u32[]{:S(2)}) collective-permute-start(bf16[4,256,256]{2,1,0:T(8,128)(2,1)S(1)} %pad_maximum_fusion.3.refs_0_), channel_id=1, source_target_pairs={{0,4},{1,5},{2,6},{3,7},{4,0},{5,1},{6,2},{7,3},{8,12},{9,13},{10,... | collective-permute-start | bytes 1572872 | tf_op jit(solution)/shard_map/ppermute | solution.py:51
  92.9 12.4 %collective-permute-start.24 = (bf16[2,512,256]{2,1,0:T(8,128)(2,1)}, bf16[2,512,256]{2,1,0:T(8,128)(2,1)}, u32[]{:S(2)}, u32[]{:S(2)}) collective-permute-start(bf16[2,512,256]{2,1,0:T(8,128)(2,1)} %response.3.refs_8_), channel_id=1, source_target_pairs={{0,96},{1,97},{2,98},{3,99},{4,100},{5,101},{6,102},{7,103},{8,104... | collective-permute-start | bytes 1572872 | tf_op jit(solution)/shard_map/ppermute | solution.py:51
  99.3 16.8 %collective-permute-start.23 = (bf16[2,512,256]{2,1,0:T(8,128)(2,1)}, bf16[2,512,256]{2,1,0:T(8,128)(2,1)}, u32[]{:S(2)}, u32[]{:S(2)}) collective-permute-start(bf16[2,512,256]{2,1,0:T(8,128)(2,1)} %response.3.refs_8_), channel_id=1, source_target_pairs={{0,32},{1,33},{2,34},{3,35},{4,36},{5,37},{6,38},{7,39},{8,40},{9,... | collective-permute-start | bytes 1572872 | tf_op jit(solution)/shard_map/ppermute | solution.py:51
  101.1 15.0 %collective-permute-start.22 = (bf16[4,256,256]{2,1,0:T(8,128)(2,1)S(1)}, bf16[4,256,256]{2,1,0:T(8,128)(2,1)}, u32[]{:S(2)}, u32[]{:S(2)}) collective-permute-start(bf16[4,256,256]{2,1,0:T(8,128)(2,1)S(1)} %collective-permute-done.20.refs_5_), channel_id=1, source_target_pairs={{0,3},{1,2},{2,1},{3,0},{4,7},{5,6},{6,5},{7,4},{8,11},{9,10},{10,... | collective-permute-start | bytes 1572872 | tf_op jit(solution)/shard_map/ppermute | solution.py:51
  103.5 12.6 %collective-permute-start.19 = (bf16[4,256,256]{2,1,0:T(8,128)(2,1)}, bf16[4,256,256]{2,1,0:T(8,128)(2,1)}, u32[]{:S(2)}, u32[]{:S(2)}) collective-permute-start(bf16[4,256,256]{2,1,0:T(8,128)(2,1)} %collective-permute-done.17.refs_1_), channel_id=1, source_target_pairs={{0,12},{1,13},{2,14},{3,15},{4,8},{5,9},{6,10},{7,11},{8,4},{9,5},... | collective-permute-start | bytes 1572872 | tf_op jit(solution)/shard_map/ppermute | solution.py:51
  105.4 15.9 %collective-permute-start.27 = (bf16[2,512,256]{2,1,0:T(8,128)(2,1)}, bf16[2,512,256]{2,1,0:T(8,128)(2,1)S(1)}, u32[]{:S(2)}, u32[]{:S(2)}) collective-permute-start(bf16[2,512,256]{2,1,0:T(8,128)(2,1)} %response.3.refs_8_), channel_id=1, source_target_pairs={{0,16},{1,17},{2,18},{3,19},{4,20},{5,21},{6,22},{7,23},{8,24},{9,... | collective-permute-start | bytes 1572872 | tf_op jit(solution)/shard_map/ppermute | solution.py:51
  116.1 9.6 %collective-permute-start.30 = (bf16[2,512,256]{2,1,0:T(8,128)(2,1)}, bf16[2,512,256]{2,1,0:T(8,128)(2,1)S(1)}, u32[]{:S(2)}, u32[]{:S(2)}) collective-permute-start(bf16[2,512,256]{2,1,0:T(8,128)(2,1)} %collective-permute-done.23.refs_9_), channel_id=1, source_target_pairs={{0,96},{1,97},{2,98},{3,99},{4,100},{5,101},{6,102},{7,103},{8,104... | collective-permute-start | bytes 1572872 | tf_op jit(solution)/shard_map/ppermute | solution.py:51
  120.7 9.5 %collective-permute-start.32 = (bf16[128,8192]{1,0:T(8,128)(2,1)S(1)}, bf16[128,8192]{1,0:T(8,128)(2,1)S(1)}, u32[]{:S(2)}, u32[]{:S(2)}) collective-permute-start(bf16[128,8192]{1,0:T(8,128)(2,1)S(1)} %broadcast_select_fusion.refs_5_), channel_id=1, source_target_pairs={{0,16},{1,17},{2,18},{3,19},{4,20},{5,21},{6,22},{7,23},{8,24},{9,... | collective-permute-start | bytes 6291464 | tf_op jit(solution)/shard_map/ppermute | solution.py:51
  (29 other events, 238.8 us)

commit v6 on v5

--- a/solution.py
+++ b/solution.py
@@ -14,7 +14,7 @@
 NSLAB = 128
 RING = 4
 N_COL = 16
-WIDE = 2
+WIDE = 4
 BF16 = jnp.bfloat16
 F32 = jnp.float32
 AXES = ("row", "col")

time: 159 us -> 157 us (0.987)
  no operation moved by 1% of the time
where the time goes in v6:
time: 157 us
  waiting for transfers between devices  49.2 us (31%)
  starting transfers between devices  47.1 us (30%)
  blocking collectives  20.6 us (13%)
  Pallas kernels  15.8 us (10%)
  other arithmetic  14.2 us (9%)
  local copies, waits for them, and re-layouts  8.9 us (6%)
    ppermute x33, waiting for transfers between devices, send(): return lax.ppermute(value, AXES, route)  49.2 us
    ppermute x33, starting transfers between devices, send(): return lax.ppermute(value, AXES, route)  47.1 us
    all_to_all x1, blocking collectives, local(): terms = lax.all_to_all(density, AXES, 0, 0, tiled=True)  20.6 us
    pallas_call x2, Pallas kernels, local(): pl.pallas_call(functools.partial(response_kernel, part), name='response',...  6.06 us
    pallas_call x1, Pallas kernels, local(): pl.pallas_call(density_kernel, name='density', out_shape=(jax.ShapeDtypeS...  5.28 us
    pallas_call x1, Pallas kernels, local(): pl.pallas_call(early_kernel, name='early', out_shape=(jax.ShapeDtypeStruc...  4.51 us
    select_n x1, other arithmetic, local(): seed = jnp.where(core == z // 2, mine, send(theirs, OTHER_CORE))  3.89 us
    select_n x1, other arithmetic, local(): passed = jnp.where(x == y, seed, reached)  3.17 us
  transfers between devices with their start and end apart: 33, of which 12 were waited for; matrix products, arithmetic and copies ran while one was open for 12% of the time, Pallas kernels for 7%

profile of v6, /device:TPU:1, one launch (start us, length us, event | category | flops | bytes accessed | tf_op | source)
XLA Modules:
  0.0 156.9 jit_solution(4613968477149044498)
XLA Ops:
  7.0 1.9 %collective-permute-start.1 = (bf16[768,256]{1,0:T(8,128)(2,1)}, bf16[768,256]{1,0:T(8,128)(2,1)}, u32[]{:S(2)}, u32[]{:S(2)}) collective-permute-start(bf16[768,256]{1,0:T(8,128)(2,1)} %pad_maximum_fusion.6), channel_id=1, source_target_pairs={{0,4},{1,5},{2,6},{3,7},{4,0},{5,1},{6,2},{7,3},{8,12},{9,13},{10,... | collective-permute-start | bytes 1179656 | tf_op jit(solution)/shard_map/ppermute | solution.py:51
  11.3 2.3 %collective-permute-start = (bf16[768,256]{1,0:T(8,128)(2,1)}, bf16[768,256]{1,0:T(8,128)(2,1)}, u32[]{:S(2)}, u32[]{:S(2)}) collective-permute-start(bf16[768,256]{1,0:T(8,128)(2,1)} %pad_maximum_fusion.5), channel_id=1, source_target_pairs={{0,1},{1,0},{2,3},{3,2},{4,5},{5,4},{6,7},{7,6},{8,9},{9,8},{10,11... | collective-permute-start | bytes 1179656 | tf_op jit(solution)/shard_map/ppermute | solution.py:51
  15.6 3.9 %bitcast_select_fusion = bf16[128,8192]{1,0:T(8,128)(2,1)} fusion(bf16[128,8192]{1,0:T(8,128)(2,1)} %collective-permute-done.4, bf16[4,128,8192]{2,1,0:T(8,128)(2,1)} %refs_4_.1, s32[]{:T(128)S(6)} %select_n.64, pred[]{:T(512)S(6)} %eq.14), kind=kLoop, calls=%fused_computation | loop fusion | flops 1048576 | bytes 6291461 | tf_op jit(solution)/shard_map/jit(_where)/select_n | solution.py:246
  19.5 3.8 %collective-permute-done = bf16[768,256]{1,0:T(8,128)(2,1)} collective-permute-done((bf16[768,256]{1,0:T(8,128)(2,1)}, bf16[768,256]{1,0:T(8,128)(2,1)}, u32[]{:S(2)}, u32[]{:S(2)}) %collective-permute-start) | collective-permute-done | bytes 393248 | tf_op jit(solution)/shard_map/ppermute | solution.py:51
  30.5 3.1 %collective-permute-done.7 = bf16[512,256]{1,0:T(8,128)(2,1)S(1)} collective-permute-done((bf16[512,256]{1,0:T(8,128)(2,1)S(1)}, bf16[512,256]{1,0:T(8,128)(2,1)S(1)}, u32[]{:S(2)}, u32[]{:S(2)}) %collective-permute-start.7) | collective-permute-done | bytes 262176 | tf_op jit(solution)/shard_map/ppermute | solution.py:51
  35.8 2.5 %collective-permute-start.11 = (bf16[4,512,256]{2,1,0:T(8,128)(2,1)S(1)}, bf16[4,512,256]{2,1,0:T(8,128)(2,1)S(1)}, u32[]{:S(2)}, u32[]{:S(2)}) collective-permute-start(bf16[4,512,256]{2,1,0:T(8,128)(2,1)S(1)} %pad_maximum_fusion.1.refs_3_), channel_id=1, source_target_pairs={{0,1},{1,0},{2,3},{3,2},{4,5},{5,4},{6,7},{7,6},{8,9},{9,8},{10,11... | collective-permute-start | bytes 3145736 | tf_op jit(solution)/shard_map/ppermute | solution.py:51
  38.9 7.9 %collective-permute-done.13 = bf16[512,256]{1,0:T(8,128)(2,1)S(1)} collective-permute-done((bf16[512,256]{1,0:T(8,128)(2,1)S(1)}, bf16[512,256]{1,0:T(8,128)(2,1)S(1)}, u32[]{:S(2)}, u32[]{:S(2)}) %collective-permute-start.13) | collective-permute-done | bytes 262176 | tf_op jit(solution)/shard_map/ppermute | solution.py:51
  50.3 4.2 %collective-permute-done.12.refs_5_ = bf16[4,512,256]{2,1,0:T(8,128)(2,1)} collective-permute-done((bf16[4,512,256]{2,1,0:T(8,128)(2,1)S(1)}, bf16[4,512,256]{2,1,0:T(8,128)(2,1)}, u32[]{:S(2)}, u32[]{:S(2)}) %collective-permute-start.12) | collective-permute-done | bytes 1048608 | tf_op jit(solution)/shard_map/ppermute | solution.py:51
  54.5 5.1 %collective-permute-done.11.refs_4_ = bf16[4,512,256]{2,1,0:T(8,128)(2,1)S(1)} collective-permute-done((bf16[4,512,256]{2,1,0:T(8,128)(2,1)S(1)}, bf16[4,512,256]{2,1,0:T(8,128)(2,1)S(1)}, u32[]{:S(2)}, u32[]{:S(2)}) %collective-permute-start.11) | collective-permute-done | bytes 1048608 | tf_op jit(solution)/shard_map/ppermute | solution.py:51
  59.6 8.3 %collective-permute-done.9.refs_1_ = bf16[4,512,256]{2,1,0:T(8,128)(2,1)} collective-permute-done((bf16[4,512,256]{2,1,0:T(8,128)(2,1)S(1)}, bf16[4,512,256]{2,1,0:T(8,128)(2,1)}, u32[]{:S(2)}, u32[]{:S(2)}) %collective-permute-start.9) | collective-permute-done | bytes 1048608 | tf_op jit(solution)/shard_map/ppermute | solution.py:51
  71.2 3.2 %broadcast_select_fusion.1 = bf16[128,8192]{1,0:T(8,128)(2,1)} fusion(bf16[128,8192]{1,0:T(8,128)(2,1)} %bitcast_select_fusion, bf16[128,8192]{1,0:T(8,128)(2,1)} %collective-permute-done.25, pred[]{:T(512)S(6)} %eq.15), kind=kLoop, calls=%fused_computation.3 | loop fusion | flops 1048576 | bytes 6291457 | tf_op jit(solution)/shard_map/jit(_where)/select_n | solution.py:267
  74.9 3.8 %response.2.refs_4_ = f32[2,512,256]{2,1,0:T(8,128)S(1)} custom-call(s32[6]{0:T(128)S(1)} %stack.96.idx, s32[1024]{0:T(1024)S(1)} %reshape.17.mask, bf16[4,512,256]{2,1,0:T(8,128)(2,1)S(1)} %pad_maximum_fusion.refs_0_, bf16[4,512,256]{2,1,0:T(8,128)(2,1)} %collective-permute-done.9.refs_1_, bf16[4,512,256]{2,1,0:T(8,128)(2,1)} %collective-permute-done.10.refs_2_, ...), custom_call_target="tpu_custom_call" | custom-call | flops 4294967296 | bytes 9437184 | tf_op jit(solution)/shard_map/response/pallas_call | solution.py:279
  78.7 5.0 %collective-permute-done.14.refs_0_ = bf16[4,512,256]{2,1,0:T(8,128)(2,1)S(1)} collective-permute-done((bf16[4,512,256]{2,1,0:T(8,128)(2,1)}, bf16[4,512,256]{2,1,0:T(8,128)(2,1)S(1)}, u32[]{:S(2)}, u32[]{:S(2)}) %collective-permute-start.14) | collective-permute-done | bytes 1048608 | tf_op jit(solution)/shard_map/ppermute | solution.py:51
  85.5 2.9 %collective-permute-start.20 = (bf16[4,256,256]{2,1,0:T(8,128)(2,1)S(1)}, bf16[4,256,256]{2,1,0:T(8,128)(2,1)S(1)}, u32[]{:S(2)}, u32[]{:S(2)}) collective-permute-start(bf16[4,256,256]{2,1,0:T(8,128)(2,1)S(1)} %pad_maximum_fusion.4.refs_4_), channel_id=1, source_target_pairs={{0,1},{1,0},{2,3},{3,2},{4,5},{5,4},{6,7},{7,6},{8,9},{9,8},{10,11... | collective-permute-start | bytes 1572872 | tf_op jit(solution)/shard_map/ppermute | solution.py:51
  90.7 2.2 %response.3.refs_8_ = bf16[2,512,256]{2,1,0:T(8,128)(2,1)} custom-call(s32[6]{0:T(128)S(1)} %stack.96.idx, s32[1024]{0:T(1024)S(1)} %reshape.17.mask, bf16[4,512,256]{2,1,0:T(8,128)(2,1)S(1)} %collective-permute-done.14.refs_0_, bf16[4,512,256]{2,1,0:T(8,128)(2,1)S(1)} %collective-permute-done.15.refs_1_, ...), custom_call_target="tpu_custom_call" | custom-call | flops 68719476736 | bytes 9437184 | tf_op jit(solution)/shard_map/response/pallas_call | solution.py:279
  93.3 6.0 %collective-permute-done.20.refs_5_ = bf16[4,256,256]{2,1,0:T(8,128)(2,1)S(1)} collective-permute-done((bf16[4,256,256]{2,1,0:T(8,128)(2,1)S(1)}, bf16[4,256,256]{2,1,0:T(8,128)(2,1)S(1)}, u32[]{:S(2)}, u32[]{:S(2)}) %collective-permute-start.20) | collective-permute-done | bytes 524320 | tf_op jit(solution)/shard_map/ppermute | solution.py:51
  101.1 2.4 %collective-permute-done.17.refs_1_ = bf16[4,256,256]{2,1,0:T(8,128)(2,1)} collective-permute-done((bf16[4,256,256]{2,1,0:T(8,128)(2,1)S(1)}, bf16[4,256,256]{2,1,0:T(8,128)(2,1)}, u32[]{:S(2)}, u32[]{:S(2)}) %collective-permute-start.17) | collective-permute-done | bytes 524320 | tf_op jit(solution)/shard_map/ppermute | solution.py:51
  105.4 10.8 %collective-permute-start.27 = (bf16[2,512,256]{2,1,0:T(8,128)(2,1)}, bf16[2,512,256]{2,1,0:T(8,128)(2,1)S(1)}, u32[]{:S(2)}, u32[]{:S(2)}) collective-permute-start(bf16[2,512,256]{2,1,0:T(8,128)(2,1)} %response.3.refs_8_), channel_id=1, source_target_pairs={{0,16},{1,17},{2,18},{3,19},{4,20},{5,21},{6,22},{7,23},{8,24},{9,... | collective-permute-start | bytes 1572872 | tf_op jit(solution)/shard_map/ppermute | solution.py:51
  116.2 2.4 %collective-permute-start.28 = (bf16[2,512,256]{2,1,0:T(8,128)(2,1)}, bf16[2,512,256]{2,1,0:T(8,128)(2,1)S(1)}, u32[]{:S(2)}, u32[]{:S(2)}) collective-permute-start(bf16[2,512,256]{2,1,0:T(8,128)(2,1)} %collective-permute-done.23.refs_9_), channel_id=1, source_target_pairs={{0,16},{1,17},{2,18},{3,19},{4,20},{5,21},{6,22},{7,23},{8,24},{9,... | collective-permute-start | bytes 1572872 | tf_op jit(solution)/shard_map/ppermute | solution.py:51
  118.7 2.0 %broadcast_select_fusion.refs_5_ = bf16[128,8192]{1,0:T(8,128)(2,1)S(1)} fusion(bf16[128,8192]{1,0:T(8,128)(2,1)} %broadcast_select_fusion.1, bf16[128,8192]{1,0:T(8,128)(2,1)} %collective-permute-done.26, pred[]{:T(512)S(6)} %or.3), kind=kLoop, calls=%fused_computation.2 | loop fusion | flops 1048576 | bytes 6291457 | tf_op jit(solution)/shard_map/jit(_where)/select_n | solution.py:300
  121.3 4.5 %early.1 = (f32[2,512,256]{2,1,0:T(8,128)S(1)}, bf16[2,4,256,256]{3,2,1,0:T(8,128)(2,1)S(1)}) custom-call(s32[6]{0:T(128)S(1)} %stack.96.idx, s32[1024]{0:T(1024)S(1)} %reshape.18.mask_v, bf16[4,256,256]{2,1,0:T(8,128)(2,1)S(1)} %pad_maximum_fusion.3.refs_0_, bf16[4,256,256]{2,1,0:T(8,128)(2,1)} %collective-permute-done.17.refs_1_, ...), custom_call_target="tpu_custom_call" | custom-call | flops 68719476736 | bytes 8388608 | tf_op jit(solution)/shard_map/early/pallas_call | solution.py:304
  125.8 2.9 %collective-permute-start.31 = (bf16[2,512,256]{2,1,0:T(8,128)(2,1)S(1)}, bf16[2,512,256]{2,1,0:T(8,128)(2,1)S(1)}, u32[]{:S(2)}, u32[]{:S(2)}) collective-permute-start(bf16[2,512,256]{2,1,0:T(8,128)(2,1)S(1)} %collective-permute-done.30.refs_1_), channel_id=1, source_target_pairs={{0,16},{1,17},{2,18},{3,19},{4,20},{5,21},{6,22},{7,23},{8,24},{9,... | collective-permute-start | bytes 1572872 | tf_op jit(solution)/shard_map/ppermute | solution.py:51
  130.2 5.3 %density.1 = (bf16[2,512,256]{2,1,0:T(8,128)(2,1)}, f32[128,8,128]{2,1,0:T(8,128)S(1)}) custom-call(s32[6]{0:T(128)S(1)} %stack.96.idx, s32[1024]{0:T(1024)S(1)} %reshape.17.mask, s32[1024]{0:T(1024)S(1)} %reshape.18.mask_v, s32[32]{0:T(128)S(1)} %copy-done, bf16[2,4,256,256]{3,2,1,0:T(8,128)(2,1)S(1)} %get-tuple-element.81.refs_0_, ...), custom_call_target="tpu_custom_call" | custom-call | flops 8589934592 | bytes 23068672 | tf_op jit(solution)/shard_map/density/pallas_call | solution.py:325
  135.5 20.6 %all_to_all.5 = f32[128,8,128]{2,1,0:T(8,128)S(1)} all-to-all(f32[128,8,128]{2,1,0:T(8,128)S(1)} %get-tuple-element.87), channel_id=1, replica_groups=mesh['row'=8,'col'=16] {'row','col'}, dimensions={0} | all-to-all | bytes 1048576 | tf_op jit(solution)/shard_map/all_to_all | solution.py:344
  (115 shorter events, 39.0 us)
Async XLA Ops:
  2.5 13.1 %collective-permute-start.4 = (bf16[128,8192]{1,0:T(8,128)(2,1)S(1)}, bf16[128,8192]{1,0:T(8,128)(2,1)}, u32[]{:S(2)}, u32[]{:S(2)}) collective-permute-start(bf16[128,8192]{1,0:T(8,128)(2,1)S(1)} %dynamic-slice_bitcast_fusion), channel_id=1, source_target_pairs={{0,16},{1,17},{2,18},{3,19},{4,20},{5,21},{6,22},{7,23},{8,24},{9,... | collective-permute-start | bytes 6291464 | tf_op jit(solution)/shard_map/ppermute | solution.py:51
  5.6 13.8 %collective-permute-start.3 = (bf16[768,256]{1,0:T(8,128)(2,1)}, bf16[768,256]{1,0:T(8,128)(2,1)S(1)}, u32[]{:S(2)}, u32[]{:S(2)}) collective-permute-start(bf16[768,256]{1,0:T(8,128)(2,1)} %pad_maximum_fusion.6), channel_id=1, source_target_pairs={{0,12},{1,13},{2,14},{3,15},{4,8},{5,9},{6,10},{7,11},{8,4},{9,5},... | collective-permute-start | bytes 1179656 | tf_op jit(solution)/shard_map/ppermute | solution.py:51
  7.0 12.5 %collective-permute-start.1 = (bf16[768,256]{1,0:T(8,128)(2,1)}, bf16[768,256]{1,0:T(8,128)(2,1)}, u32[]{:S(2)}, u32[]{:S(2)}) collective-permute-start(bf16[768,256]{1,0:T(8,128)(2,1)} %pad_maximum_fusion.6), channel_id=1, source_target_pairs={{0,4},{1,5},{2,6},{3,7},{4,0},{5,1},{6,2},{7,3},{8,12},{9,13},{10,... | collective-permute-start | bytes 1179656 | tf_op jit(solution)/shard_map/ppermute | solution.py:51
  9.7 9.8 %collective-permute-start.2 = (bf16[768,256]{1,0:T(8,128)(2,1)}, bf16[768,256]{1,0:T(8,128)(2,1)S(1)}, u32[]{:S(2)}, u32[]{:S(2)}) collective-permute-start(bf16[768,256]{1,0:T(8,128)(2,1)} %pad_maximum_fusion.5), channel_id=1, source_target_pairs={{0,3},{1,2},{2,1},{3,0},{4,7},{5,6},{6,5},{7,4},{8,11},{9,10},{10,... | collective-permute-start | bytes 1179656 | tf_op jit(solution)/shard_map/ppermute | solution.py:51
  11.3 12.0 %collective-permute-start = (bf16[768,256]{1,0:T(8,128)(2,1)}, bf16[768,256]{1,0:T(8,128)(2,1)}, u32[]{:S(2)}, u32[]{:S(2)}) collective-permute-start(bf16[768,256]{1,0:T(8,128)(2,1)} %pad_maximum_fusion.5), channel_id=1, source_target_pairs={{0,1},{1,0},{2,3},{3,2},{4,5},{5,4},{6,7},{7,6},{8,9},{9,8},{10,11... | collective-permute-start | bytes 1179656 | tf_op jit(solution)/shard_map/ppermute | solution.py:51
  24.5 9.1 %collective-permute-start.7 = (bf16[512,256]{1,0:T(8,128)(2,1)S(1)}, bf16[512,256]{1,0:T(8,128)(2,1)S(1)}, u32[]{:S(2)}, u32[]{:S(2)}) collective-permute-start(bf16[512,256]{1,0:T(8,128)(2,1)S(1)} %bitcast_multiply_fusion), channel_id=1, source_target_pairs={{0,32},{1,33},{2,34},{3,35},{4,36},{5,37},{6,38},{7,39},{8,40},{9,... | collective-permute-start | bytes 786440 | tf_op jit(solution)/shard_map/ppermute | solution.py:51
  28.6 42.7 %collective-permute-start.25 = (bf16[128,8192]{1,0:T(8,128)(2,1)}, bf16[128,8192]{1,0:T(8,128)(2,1)}, u32[]{:S(2)}, u32[]{:S(2)}) collective-permute-start(bf16[128,8192]{1,0:T(8,128)(2,1)} %bitcast_select_fusion), channel_id=1, source_target_pairs={{0,32},{1,33},{2,34},{3,35},{4,36},{5,37},{6,38},{7,39},{8,40},{9,... | collective-permute-start | bytes 6291464 | tf_op jit(solution)/shard_map/ppermute | solution.py:51
  34.4 20.1 %collective-permute-start.12 = (bf16[4,512,256]{2,1,0:T(8,128)(2,1)S(1)}, bf16[4,512,256]{2,1,0:T(8,128)(2,1)}, u32[]{:S(2)}, u32[]{:S(2)}) collective-permute-start(bf16[4,512,256]{2,1,0:T(8,128)(2,1)S(1)} %pad_maximum_fusion.1.refs_3_), channel_id=1, source_target_pairs={{0,3},{1,2},{2,1},{3,0},{4,7},{5,6},{6,5},{7,4},{8,11},{9,10},{10,... | collective-permute-start | bytes 3145736 | tf_op jit(solution)/shard_map/ppermute | solution.py:51
  35.8 23.8 %collective-permute-start.11 = (bf16[4,512,256]{2,1,0:T(8,128)(2,1)S(1)}, bf16[4,512,256]{2,1,0:T(8,128)(2,1)S(1)}, u32[]{:S(2)}, u32[]{:S(2)}) collective-permute-start(bf16[4,512,256]{2,1,0:T(8,128)(2,1)S(1)} %pad_maximum_fusion.1.refs_3_), channel_id=1, source_target_pairs={{0,1},{1,0},{2,3},{3,2},{4,5},{5,4},{6,7},{7,6},{8,9},{9,8},{10,11... | collective-permute-start | bytes 3145736 | tf_op jit(solution)/shard_map/ppermute | solution.py:51
  38.8 20.7 %collective-permute-start.10 = (bf16[4,512,256]{2,1,0:T(8,128)(2,1)S(1)}, bf16[4,512,256]{2,1,0:T(8,128)(2,1)}, u32[]{:S(2)}, u32[]{:S(2)}) collective-permute-start(bf16[4,512,256]{2,1,0:T(8,128)(2,1)S(1)} %pad_maximum_fusion.refs_0_), channel_id=1, source_target_pairs={{0,12},{1,13},{2,14},{3,15},{4,8},{5,9},{6,10},{7,11},{8,4},{9,5},... | collective-permute-start | bytes 3145736 | tf_op jit(solution)/shard_map/ppermute | solution.py:51
  47.5 20.3 %collective-permute-start.9 = (bf16[4,512,256]{2,1,0:T(8,128)(2,1)S(1)}, bf16[4,512,256]{2,1,0:T(8,128)(2,1)}, u32[]{:S(2)}, u32[]{:S(2)}) collective-permute-start(bf16[4,512,256]{2,1,0:T(8,128)(2,1)S(1)} %pad_maximum_fusion.refs_0_), channel_id=1, source_target_pairs={{0,4},{1,5},{2,6},{3,7},{4,0},{5,1},{6,2},{7,3},{8,12},{9,13},{10,... | collective-permute-start | bytes 3145736 | tf_op jit(solution)/shard_map/ppermute | solution.py:51
  69.3 14.3 %collective-permute-start.14 = (bf16[4,512,256]{2,1,0:T(8,128)(2,1)}, bf16[4,512,256]{2,1,0:T(8,128)(2,1)S(1)}, u32[]{:S(2)}, u32[]{:S(2)}) collective-permute-start(bf16[4,512,256]{2,1,0:T(8,128)(2,1)} %collective-permute-done.9.refs_1_), channel_id=1, source_target_pairs={{0,12},{1,13},{2,14},{3,15},{4,8},{5,9},{6,10},{7,11},{8,4},{9,5},... | collective-permute-start | bytes 3145736 | tf_op jit(solution)/shard_map/ppermute | solution.py:51
  69.4 14.4 %collective-permute-start.15 = (bf16[4,512,256]{2,1,0:T(8,128)(2,1)S(1)}, bf16[4,512,256]{2,1,0:T(8,128)(2,1)S(1)}, u32[]{:S(2)}, u32[]{:S(2)}) collective-permute-start(bf16[4,512,256]{2,1,0:T(8,128)(2,1)S(1)} %collective-permute-done.11.refs_4_), channel_id=1, source_target_pairs={{0,3},{1,2},{2,1},{3,0},{4,7},{5,6},{6,5},{7,4},{8,11},{9,10},{10,... | collective-permute-start | bytes 3145736 | tf_op jit(solution)/shard_map/ppermute | solution.py:51
  74.4 41.7 %collective-permute-start.26 = (bf16[128,8192]{1,0:T(8,128)(2,1)}, bf16[128,8192]{1,0:T(8,128)(2,1)}, u32[]{:S(2)}, u32[]{:S(2)}) collective-permute-start(bf16[128,8192]{1,0:T(8,128)(2,1)} %broadcast_select_fusion.1), channel_id=1, source_target_pairs={{0,96},{1,97},{2,98},{3,99},{4,100},{5,101},{6,102},{7,103},{8,104... | collective-permute-start | bytes 6291464 | tf_op jit(solution)/shard_map/ppermute | solution.py:51
  85.5 13.8 %collective-permute-start.20 = (bf16[4,256,256]{2,1,0:T(8,128)(2,1)S(1)}, bf16[4,256,256]{2,1,0:T(8,128)(2,1)S(1)}, u32[]{:S(2)}, u32[]{:S(2)}) collective-permute-start(bf16[4,256,256]{2,1,0:T(8,128)(2,1)S(1)} %pad_maximum_fusion.4.refs_4_), channel_id=1, source_target_pairs={{0,1},{1,0},{2,3},{3,2},{4,5},{5,4},{6,7},{7,6},{8,9},{9,8},{10,11... | collective-permute-start | bytes 1572872 | tf_op jit(solution)/shard_map/ppermute | solution.py:51
  88.6 12.6 %collective-permute-start.18 = (bf16[4,256,256]{2,1,0:T(8,128)(2,1)S(1)}, bf16[4,256,256]{2,1,0:T(8,128)(2,1)S(1)}, u32[]{:S(2)}, u32[]{:S(2)}) collective-permute-start(bf16[4,256,256]{2,1,0:T(8,128)(2,1)S(1)} %pad_maximum_fusion.3.refs_0_), channel_id=1, source_target_pairs={{0,12},{1,13},{2,14},{3,15},{4,8},{5,9},{6,10},{7,11},{8,4},{9,5},... | collective-permute-start | bytes 1572872 | tf_op jit(solution)/shard_map/ppermute | solution.py:51
  89.9 13.6 %collective-permute-start.17 = (bf16[4,256,256]{2,1,0:T(8,128)(2,1)S(1)}, bf16[4,256,256]{2,1,0:T(8,128)(2,1)}, u32[]{:S(2)}, u32[]{:S(2)}) collective-permute-start(bf16[4,256,256]{2,1,0:T(8,128)(2,1)S(1)} %pad_maximum_fusion.3.refs_0_), channel_id=1, source_target_pairs={{0,4},{1,5},{2,6},{3,7},{4,0},{5,1},{6,2},{7,3},{8,12},{9,13},{10,... | collective-permute-start | bytes 1572872 | tf_op jit(solution)/shard_map/ppermute | solution.py:51
  92.9 12.4 %collective-permute-start.24 = (bf16[2,512,256]{2,1,0:T(8,128)(2,1)}, bf16[2,512,256]{2,1,0:T(8,128)(2,1)}, u32[]{:S(2)}, u32[]{:S(2)}) collective-permute-start(bf16[2,512,256]{2,1,0:T(8,128)(2,1)} %response.3.refs_8_), channel_id=1, source_target_pairs={{0,96},{1,97},{2,98},{3,99},{4,100},{5,101},{6,102},{7,103},{8,104... | collective-permute-start | bytes 1572872 | tf_op jit(solution)/shard_map/ppermute | solution.py:51
  99.3 16.8 %collective-permute-start.23 = (bf16[2,512,256]{2,1,0:T(8,128)(2,1)}, bf16[2,512,256]{2,1,0:T(8,128)(2,1)}, u32[]{:S(2)}, u32[]{:S(2)}) collective-permute-start(bf16[2,512,256]{2,1,0:T(8,128)(2,1)} %response.3.refs_8_), channel_id=1, source_target_pairs={{0,32},{1,33},{2,34},{3,35},{4,36},{5,37},{6,38},{7,39},{8,40},{9,... | collective-permute-start | bytes 1572872 | tf_op jit(solution)/shard_map/ppermute | solution.py:51
  101.1 15.0 %collective-permute-start.22 = (bf16[4,256,256]{2,1,0:T(8,128)(2,1)S(1)}, bf16[4,256,256]{2,1,0:T(8,128)(2,1)}, u32[]{:S(2)}, u32[]{:S(2)}) collective-permute-start(bf16[4,256,256]{2,1,0:T(8,128)(2,1)S(1)} %collective-permute-done.20.refs_5_), channel_id=1, source_target_pairs={{0,3},{1,2},{2,1},{3,0},{4,7},{5,6},{6,5},{7,4},{8,11},{9,10},{10,... | collective-permute-start | bytes 1572872 | tf_op jit(solution)/shard_map/ppermute | solution.py:51
  103.5 12.6 %collective-permute-start.19 = (bf16[4,256,256]{2,1,0:T(8,128)(2,1)}, bf16[4,256,256]{2,1,0:T(8,128)(2,1)}, u32[]{:S(2)}, u32[]{:S(2)}) collective-permute-start(bf16[4,256,256]{2,1,0:T(8,128)(2,1)} %collective-permute-done.17.refs_1_), channel_id=1, source_target_pairs={{0,12},{1,13},{2,14},{3,15},{4,8},{5,9},{6,10},{7,11},{8,4},{9,5},... | collective-permute-start | bytes 1572872 | tf_op jit(solution)/shard_map/ppermute | solution.py:51
  105.4 15.9 %collective-permute-start.27 = (bf16[2,512,256]{2,1,0:T(8,128)(2,1)}, bf16[2,512,256]{2,1,0:T(8,128)(2,1)S(1)}, u32[]{:S(2)}, u32[]{:S(2)}) collective-permute-start(bf16[2,512,256]{2,1,0:T(8,128)(2,1)} %response.3.refs_8_), channel_id=1, source_target_pairs={{0,16},{1,17},{2,18},{3,19},{4,20},{5,21},{6,22},{7,23},{8,24},{9,... | collective-permute-start | bytes 1572872 | tf_op jit(solution)/shard_map/ppermute | solution.py:51
  116.1 9.6 %collective-permute-start.30 = (bf16[2,512,256]{2,1,0:T(8,128)(2,1)}, bf16[2,512,256]{2,1,0:T(8,128)(2,1)S(1)}, u32[]{:S(2)}, u32[]{:S(2)}) collective-permute-start(bf16[2,512,256]{2,1,0:T(8,128)(2,1)} %collective-permute-done.23.refs_9_), channel_id=1, source_target_pairs={{0,96},{1,97},{2,98},{3,99},{4,100},{5,101},{6,102},{7,103},{8,104... | collective-permute-start | bytes 1572872 | tf_op jit(solution)/shard_map/ppermute | solution.py:51
  120.7 9.5 %collective-permute-start.32 = (bf16[128,8192]{1,0:T(8,128)(2,1)S(1)}, bf16[128,8192]{1,0:T(8,128)(2,1)S(1)}, u32[]{:S(2)}, u32[]{:S(2)}) collective-permute-start(bf16[128,8192]{1,0:T(8,128)(2,1)S(1)} %broadcast_select_fusion.refs_5_), channel_id=1, source_target_pairs={{0,16},{1,17},{2,18},{3,19},{4,20},{5,21},{6,22},{7,23},{8,24},{9,... | collective-permute-start | bytes 6291464 | tf_op jit(solution)/shard_map/ppermute | solution.py:51
  (29 other events, 238.8 us)
